TPU v7x, 256 devices: a whole 4x4x8 slice. The times are simulated.
256 devices in a mesh: section: 4 (over x_hi, core), dp: 64 (over z, x_lo, y).
Axes of the slice: x: 4 (x_hi: 2, x_lo: 2; x = x_hi * 2 + x_lo), y: 4, z: 8, core: 2. Of those that a mesh axis runs over, the one named last changes fastest.
Arguments:
- encoder_states: bfloat16 [2, 2048, 2048], P(None, 'dp', 'section'), may hold values from -860 to 860
- encoder_lengths: int32 [2, 64], P(None, 'dp'), may hold values from 8 to 32, as said below
- final_gain: bfloat16 [2048], P('section'), may hold values from 0.25 to 1.75
- decoder_states: bfloat16 [2, 4096, 2048], P(None, 'dp'), may hold values from -1800 to 1800
- query_gain: bfloat16 [4, 2048], P('section'), may hold values from 0.25 to 1.75
- cross_weight: bfloat16 [4, 2048, 4096], P('section', 'dp'), may hold values from -1 to 1.02
- upstream: bfloat16 [2, 4096, 2048], P(None, 'dp'), may hold values from -6 to 6
Outputs:
- encoder_gradient: float32 [2, 2048, 2048], P(None, 'dp', 'section')
- final_gradient: float32 [2048], P('section')
- layers_gradient: float32 [4, 2048], P('section')
Inputs may be any that keep to these rules, and one draw needn't show every extreme that they name: `encoder_lengths`: the valid positions of a sequence are its first ones; in each micro-batch some sequence has all 32.
All inputs are finite; a program needn't handle non-finite values.
Results may differ from a plain program's by a relative error of at most 0.013.
The roundings to bfloat16 on the way count: a program that leaves them out, or rounds other values in their place, can miss the bound.
Values may be sent and summed in bfloat16 or wider, within the bound.
No kernel may reach another device: no remote copies, remote signals or barrier semaphores. Data moves between devices by JAX's collectives and lax.ppermute only.
A program may use at most 128 MiB of HBM per device.

v0:
```python
import jax
import jax.numpy as jnp
import numpy as np
from jax import lax
from jax.experimental import pallas as pl
from jax.experimental.pallas import tpu as pltpu
from jax.sharding import Mesh
from jax.sharding import PartitionSpec as P

D = 2048
HEAD = 64
ENC = 32
ROWS = 32
LAYERS = 4
GROUPS = 8
EPSILON = 1e-06
AXES = ("xh", "core", "z", "xl", "y")
SIZES = (2, 2, 8, 2, 4)
NY = 4
BF, F32 = jnp.bfloat16, jnp.float32
MIB = 1 << 20


def shift(block, **moves):
    pairs = []
    for index in np.ndindex(*SIZES):
        to = list(index)
        for axis, by in moves.items():
            k = AXES.index(axis)
            to[k] = (index[k] + by) % SIZES[k] if axis == "y" else index[k] ^ by
        pairs.append((int(np.ravel_multi_index(index, SIZES)), int(np.ravel_multi_index(to, SIZES))))
    return lax.ppermute(block, AXES, pairs)


def kernel_call(body, ids, operands, outs, scratch=(), limit=24):
    return pl.pallas_call(
        body,
        out_shape=[jax.ShapeDtypeStruct(s, d) for s, d in outs],
        in_specs=[pl.BlockSpec(memory_space=pltpu.SMEM)] + [pl.BlockSpec(memory_space=pltpu.VMEM)] * len(operands),
        out_specs=[pl.BlockSpec(memory_space=pltpu.VMEM)] * len(outs),
        scratch_shapes=[pltpu.VMEM(s, d) for s, d in scratch],
        compiler_params=pltpu.CompilerParams(vmem_limit_bytes=limit * MIB),
    )(ids, *operands)


def lanes(start, size):
    return pl.ds(pl.multiple_of(start, size), size)


def pack_body(ids, states, final_gain, query_gain, pack):
    pack[:64, :] = states[...]
    gains = [final_gain[...].astype(F32)]
    gains += [query_gain[:, i * 512 : (i + 1) * 512].astype(F32) for i in range(4)]
    gains += [jnp.zeros((11, 512), F32)]
    pack[64:, :] = jnp.concatenate(gains, axis=0).astype(BF)


def norm_body(ids, p0, p1, p2, p3, half, factor, query_gains, wide, final_gains):
    section, c = ids[0] * 2 + ids[1], ids[1]
    for j, pack in enumerate((p0, p1, p2, p3)):
        peer = section ^ j
        wide[:, lanes(peer * 512, 512)] = pack[:64, :].astype(F32)
        gains = pack[64:, :].astype(F32)
        final_gains[:, lanes(peer * 512, 512)] = gains[0:1]
        for i in range(4):
            query_gains[peer, :, i * 512 : (i + 1) * 512] = gains[1 + i : 2 + i]
    states = wide[...]
    scale = lax.rsqrt(jnp.mean(states * states, axis=-1, keepdims=True) + EPSILON)
    factor[...] = jnp.broadcast_to(scale, (64, 128))
    wide[...] = states * scale * final_gains[...]
    half[...] = wide[lanes(c * 32, 32), :].astype(BF)


def project_body(ids, own, other, weight, out, result):
    c, xl, y = ids[1], ids[3], ids[4]
    for i, rows in enumerate((own, other)):
        m = (c + i) % 2
        result[...] = jnp.dot(rows[...].reshape(256, D), weight[...], preferred_element_type=F32).astype(BF)
        for dy in range(NY):
            for dxl in range(2):
                place = m * 8 + (xl + dxl) % 2 * 4 + (y + NY - dy) % NY
                k = dy * 2 + dxl
                out[place] = result[k * 32 : (k + 1) * 32, :]


def decoder_body(ids, own, other, stream_in, upstream, query_gains, keep, send, gain_parts,
                 pairs, streams, queries, softmax, incoming, query_gradient, gradients):
    xh, c = ids[0], ids[1]
    length = jnp.where(xh == 0, ids[5], ids[6])
    for i in range(2):
        for k in range(8):
            pairs[2 * i + c, :, k * 512 : (k + 1) * 512] = own[8 * i + k]
            pairs[2 * i + 1 - c, :, k * 512 : (k + 1) * 512] = other[8 * i + k]
    streams[0] = stream_in[...]
    incoming[...] = upstream[...].astype(F32)
    block = (lax.broadcasted_iota(jnp.int32, (128, 256), 0) // 32) == (
        lax.broadcasted_iota(jnp.int32, (128, 256), 1) // HEAD
    )
    block = jnp.where(block, 1.0, 0.0).astype(BF)
    lane = lax.broadcasted_iota(jnp.int32, (ROWS, 256), 1)
    visible = lax.broadcasted_iota(jnp.int32, (ENC, 128), 0) < length
    scale = HEAD**-0.5

    def spread(part):
        return jnp.concatenate([part] * 4, axis=0) * block

    def fold(part):
        low = jnp.where(lane < 64, part[0:32], part[32:64])
        high = jnp.where(lane < 192, part[64:96], part[96:128])
        return jnp.where(lane < 128, low, high)

    def dot(a, b, dims):
        return lax.dot_general(a, b, (dims, ((), ())), preferred_element_type=F32)

    def forward(layer, carry):
        wide = streams[layer].astype(F32)
        factor = lax.rsqrt(jnp.mean(wide * wide, axis=-1, keepdims=True) + EPSILON)
        queries[layer] = (wide * factor * query_gains[layer]).astype(BF)
        for g in range(GROUPS):
            span = slice(g * 256, (g + 1) * 256)
            keys = pairs[layer, :, span]
            values = pairs[layer, :, D + g * 256 : D + (g + 1) * 256]
            scores = dot(keys, spread(queries[layer, :, span]), ((1,), (1,))) * scale
            scores = jnp.where(visible, scores, -1e30)
            highest = jnp.max(scores, axis=0, keepdims=True)
            weights = jnp.where(visible, jnp.exp(scores - highest), 0.0)
            rows = weights / jnp.sum(weights, axis=0, keepdims=True)
            softmax[layer, g] = rows
            context = fold(dot(rows.astype(BF), values, ((0,), (0,))))
            streams[layer + 1, :, span] = (wide[:, span] + context).astype(BF)
        return carry

    lax.fori_loop(0, LAYERS, forward, 0)

    def backward(turn, carry):
        layer = LAYERS - 1 - turn
        wide = streams[layer].astype(F32)
        factor = lax.rsqrt(jnp.mean(wide * wide, axis=-1, keepdims=True) + EPSILON)
        for g in range(GROUPS):
            span = slice(g * 256, (g + 1) * 256)
            beyond = slice(D + g * 256, D + (g + 1) * 256)
            keys = pairs[layer, :, span]
            values = pairs[layer, :, beyond]
            rows = softmax[layer, g]
            heads = spread(incoming[:, span].astype(BF))
            softmax_gradient = dot(values, heads, ((1,), (1,)))
            gradients[layer, :, beyond] = dot(rows.astype(BF), heads, ((1,), (0,))).astype(BF)
            score_gradient = rows * (
                softmax_gradient - jnp.sum(rows * softmax_gradient, axis=0, keepdims=True)
            )
            score_gradient = score_gradient.astype(BF)
            query_gradient[:, span] = fold(dot(score_gradient, keys, ((0,), (0,)))) * scale
            key_gradient = dot(score_gradient, spread(queries[layer, :, span]), ((1,), (0,)))
            gradients[layer, :, span] = (key_gradient * scale).astype(BF)
        gradient = query_gradient[...]
        scaled = gradient * query_gains[layer]
        mean = jnp.mean(scaled * wide, axis=-1, keepdims=True)
        incoming[...] = incoming[...] + factor * scaled - wide * (factor * factor * factor) * mean
        gain_parts[layer] = jnp.sum(gradient * wide * factor, axis=0, keepdims=True)
        return carry

    lax.fori_loop(0, LAYERS, backward, 0)
    for i in range(2):
        keep[i] = gradients[2 * i + c]
        send[i] = gradients[2 * i + 1 - c]


def join_body(ids, keep, received, out):
    for xh in range(2):
        for y in range(NY):
            for half in range(2):
                span = slice(half * 2048 + y * 512, half * 2048 + (y + 1) * 512)
                total = keep[xh, :, span].astype(F32) + received[xh, :, span].astype(F32)
                out[xh * NY + y, :, half * 512 : (half + 1) * 512] = total.astype(BF)


def high_low(part):
    high = part.astype(BF)
    return high, (part - high.astype(F32)).astype(BF)


def back_body(ids, gradient, own, other, weight, partner, gain_parts, keep, extra, send, terms, parts, rows):
    c, xl, y = ids[1], ids[3], ids[4]
    mine = gradient[:, :, lanes(xl * 512, 512)].reshape(256, 512)
    theirs = gradient[:, :, lanes((1 - xl) * 512, 512)].reshape(256, 512)
    dims = (((1,), (1,)), ((), ()))
    for q in range(4):
        span = slice(q * 512, (q + 1) * 512)
        terms[:, span] = lax.dot_general(mine, weight[span, :], dims, preferred_element_type=F32) + lax.dot_general(
            theirs, partner[span, :], dims, preferred_element_type=F32
        )
    for m in range(2):
        for peer in range(NY):
            dy = (y + NY - peer) % NY
            place = (m * NY + peer) * 32
            encoder_rows = jnp.where(c == m, own[dy, 0].astype(F32), other[dy, 0].astype(F32))
            product = terms[place : place + 32, :] * encoder_rows
            if place == 0:
                parts[...] = jnp.sum(product, axis=0, keepdims=True)
            else:
                parts[...] += jnp.sum(product, axis=0, keepdims=True)
            rows[place : place + 32, :] = jnp.broadcast_to(jnp.sum(product, axis=1, keepdims=True), (32, 128))
    row_sums = jnp.transpose(rows[...])[0:1, :]
    for parity, is_send in ((c, False), (1 - c, True)):
        extras = []
        for i in range(2):
            layer_gain = gain_parts[2 * i + parity]
            extras += [layer_gain[:, :1024], layer_gain[:, 1024:]]
        extras.append(
            jnp.concatenate([parts[:, lanes((2 * i + parity) * 512, 512)] for i in range(2)], axis=1)
        )
        extras.append(jnp.concatenate([row_sums, jnp.zeros((1, 768), F32)], axis=1))
        extras.append(jnp.zeros((2, 1024), F32))
        block = jnp.concatenate(extras, axis=0)
        for i in range(2):
            part = terms[:, lanes((2 * i + parity) * 512, 512)]
            if is_send:
                send[:256, i * 512 : (i + 1) * 512] = part.astype(BF)
            else:
                keep[:, i * 512 : (i + 1) * 512] = part
        if is_send:
            send[256:, :] = jnp.concatenate(high_low(block), axis=0)
        else:
            extra[...] = block


def merge_body(ids, keep, extra, received, out):
    carried = received[256:, :].astype(F32)
    extras = extra[...] + carried[0:8] + carried[8:16]
    for xh in range(2):
        span = slice(xh * 512, (xh + 1) * 512)
        block = jnp.concatenate(
            [
                extras[2 * xh : 2 * xh + 1, :512],
                extras[2 * xh : 2 * xh + 1, 512:],
                extras[2 * xh + 1 : 2 * xh + 2, :512],
                extras[2 * xh + 1 : 2 * xh + 2, 512:],
                extras[4:5, span],
                extras[5:6, :512],
                jnp.zeros((2, 512), F32),
            ],
            axis=0,
        )
        block = jnp.concatenate(high_low(block), axis=0)
        for y in range(NY):
            for m in range(2):
                place = (m * NY + y) * 32
                part = keep[place : place + 32, span] + received[place : place + 32, span].astype(F32)
                out[xh * NY + y, m * 32 : (m + 1) * 32, :] = part.astype(BF)
            out[xh * NY + y, 64:, :] = block


def finish_body(ids, received, states, factor, final_gain, gradient, sums, rows):
    y = ids[4]
    total = received[0].astype(F32)
    for k in range(1, 8):
        total += received[k].astype(F32)
    extras = total[64:72] + total[72:80]
    sums[...] = extras
    rows[...] = jnp.transpose(jnp.broadcast_to(extras[5:6, :256], (128, 256)))
    for m in range(2):
        span = slice(m * 32, (m + 1) * 32)
        row_sum = rows[lanes(m * 128 + y * 32, 32), 0:1]
        scale = factor[span, 0:1]
        scaled = total[span] * final_gain[...].astype(F32)
        wide = states[span, :].astype(F32)
        gradient[span, :] = scale * scaled - wide * (scale * scale * (row_sum / D))


def touch_body(ids, after, block, out):
    pass


def touch(ids, block, after):
    return pl.pallas_call(
        touch_body,
        out_shape=jax.ShapeDtypeStruct(block.shape, block.dtype),
        in_specs=[pl.BlockSpec(memory_space=pltpu.SMEM)] + [pl.BlockSpec(memory_space=pl.ANY)] * 2,
        out_specs=pl.BlockSpec(memory_space=pl.ANY),
        input_output_aliases={2: 0},
    )(ids, after, block)


def per_device(
    encoder_states, encoder_lengths, final_gain, decoder_states, query_gain, cross_weight, upstream
):
    xh, c, z, xl, y = (lax.axis_index(axis) for axis in AXES)
    block = cross_weight[0].reshape(32, 8, 512).transpose(1, 0, 2)
    block = lax.all_to_all(block, ("xl", "y"), 0, 0, tiled=True).reshape(256, 512)
    weight = lax.all_gather(block, "z", axis=0, tiled=True)

    ids = jnp.stack([xh, c, z, xl, y, encoder_lengths[0, 0], encoder_lengths[1, 0], 0]).astype(jnp.int32)
    states = encoder_states.reshape(64, 512)
    stream = lax.dynamic_slice(decoder_states, (xh, c * ROWS, 0), (1, ROWS, D))[0]
    incoming = lax.dynamic_slice(upstream, (xh, c * ROWS, 0), (1, ROWS, D))[0]
    (pack,) = kernel_call(pack_body, ids, (states, final_gain[None], query_gain), [((80, 512), BF)])
    packs = [pack, shift(pack, core=1), shift(pack, xh=1), shift(pack, xh=1, core=1)]
    half, factor, query_gains = kernel_call(
        norm_body,
        ids,
        packs,
        [((32, D), BF), ((64, 128), F32), ((4, 1, D), F32)],
        [((64, D), F32), ((1, D), F32)],
    )
    both = jnp.stack([half, shift(half, xl=1)])
    own_rows = jnp.stack([both] + [shift(both, y=dy) for dy in range(1, NY)])
    other_rows = shift(own_rows, core=1)
    partner_block = shift(block, xl=1)

    (projected,) = kernel_call(
        project_body, ids, (own_rows, other_rows, weight), [((16, 32, 512), BF)], [((256, 512), BF)]
    )
    partner = lax.all_gather(touch(ids, partner_block, projected), "z", axis=0, tiled=True)
    own_pairs = lax.all_to_all(projected, ("xh", "xl", "y"), 0, 0, tiled=True)
    other_pairs = shift(own_pairs, core=1)
    keep, send, gain_parts = kernel_call(
        decoder_body,
        ids,
        (own_pairs, other_pairs, stream, incoming, query_gains),
        [((2, 32, 4096), BF), ((2, 32, 4096), BF), ((4, 1, D), F32)],
        [
            ((4, 32, 4096), BF),
            ((5, ROWS, D), BF),
            ((4, ROWS, D), BF),
            ((4, GROUPS, ENC, 128), F32),
            ((ROWS, D), F32),
            ((ROWS, D), F32),
            ((4, 32, 4096), BF),
        ],
    )
    (joined,) = kernel_call(join_body, ids, (keep, shift(send, core=1)), [((8, 32, 1024), BF)])
    joined = lax.all_to_all(joined, ("xh", "y"), 0, 0, tiled=True)
    term_keep, extra, term_send = kernel_call(
        back_body,
        ids,
        (joined, own_rows, other_rows, weight, partner, gain_parts),
        [((256, 1024), F32), ((8, 1024), F32), ((272, 1024), BF)],
        [((256, D), F32), ((1, D), F32), ((256, 128), F32)],
    )
    (merged,) = kernel_call(
        merge_body, ids, (term_keep, extra, shift(term_send, core=1)), [((8, 80, 512), BF)]
    )
    merged = lax.all_to_all(merged, ("xh", "y"), 0, 0, tiled=True)
    gradient, sums = kernel_call(
        finish_body,
        ids,
        (merged, states, factor, final_gain[None]),
        [((64, 512), F32), ((8, 512), F32)],
        [((256, 128), F32)],
    )
    for move in ({"xl": 1}, {"z": 1}, {"z": 2}, {"z": 4}):
        sums = sums + shift(sums, **move)
    final_gradient = sums[4] / final_gain.astype(F32)
    return (gradient.reshape(2, 32, 512), final_gradient, sums[:4].reshape(1, D))


def solution(mesh):
    dp, section = ("z", "xl", "y"), ("xh", "core")
    return jax.shard_map(
        per_device,
        mesh=Mesh(mesh.devices.reshape(SIZES), AXES),
        in_specs=(
            P(None, dp, section),
            P(None, dp),
            P(section),
            P(None, dp, None),
            P(section, None),
            P(section, dp, None),
            P(None, dp, None),
        ),
        out_specs=(P(None, dp, section), P(section), P(section, None)),
        check_vma=False,
    )
```

profile of v0, /device:TPU:8, one launch (start us, length us, event | category | flops | bytes accessed | tf_op | source)
XLA Modules:
  0.0 177.7 jit_solution(14256059758787041330)
XLA Ops:
  7.2 1.0 copy.12
  8.3 11.2 %all_to_all.20 = bf16[8,32,512]{2,1,0:T(8,128)(2,1)} all-to-all(bf16[8,32,512]{2,1,0:T(8,128)(2,1)S(1)} %bitcast.37), channel_id=1, replica_groups=mesh['xh'=2,'core'=2,'z'=8,'xl'=2,'y'=4] {'xl','y'}, dimensions={0} | all-to-all | bytes 524288 | tf_op jit(solution)/shard_map/all_to_all | solution.py:289
  19.6 0.7 broadcast_in_dim.4.final_gain
  20.3 1.4 fusion.1
  21.7 1.5 stack.47.ids
  23.1 0.8 copy-done.7
  24.0 0.7 copy-done.11
  25.3 2.8 %collective-permute-start.1 = (bf16[80,512]{1,0:T(8,128)(2,1)S(1)}, bf16[80,512]{1,0:T(8,128)(2,1)S(1)}, u32[]{:S(2)}, u32[]{:S(2)}) collective-permute-start(bf16[80,512]{1,0:T(8,128)(2,1)S(1)} %shard_map.94.p0), channel_id=1, source_target_pairs={{0,128},{1,129},{2,130},{3,131},{4,132},{5,133},{6,134},{7,135},{8... | collective-permute-start | bytes 245768 | tf_op jit(solution)/shard_map/ppermute | solution.py:32
  28.7 3.0 %collective-permute-done.1.p2 = bf16[80,512]{1,0:T(8,128)(2,1)S(1)} collective-permute-done((bf16[80,512]{1,0:T(8,128)(2,1)S(1)}, bf16[80,512]{1,0:T(8,128)(2,1)S(1)}, u32[]{:S(2)}, u32[]{:S(2)}) %collective-permute-start.1) | collective-permute-done | bytes 81952 | tf_op jit(solution)/shard_map/ppermute | solution.py:32
  31.7 2.4 %collective-permute-done.2.p3 = bf16[80,512]{1,0:T(8,128)(2,1)S(1)} collective-permute-done((bf16[80,512]{1,0:T(8,128)(2,1)S(1)}, bf16[80,512]{1,0:T(8,128)(2,1)S(1)}, u32[]{:S(2)}, u32[]{:S(2)}) %collective-permute-start.2) | collective-permute-done | bytes 81952 | tf_op jit(solution)/shard_map/ppermute | solution.py:32
  34.1 0.7 shard_map.95
  34.8 0.7 collective-permute-start.3
  35.6 4.9 %collective-permute-done.3 = bf16[32,2048]{1,0:T(8,128)(2,1)S(1)} collective-permute-done((bf16[32,2048]{1,0:T(8,128)(2,1)S(1)}, bf16[32,2048]{1,0:T(8,128)(2,1)S(1)}, u32[]{:S(2)}, u32[]{:S(2)}) %collective-permute-start.3) | collective-permute-done | bytes 131104 | tf_op jit(solution)/shard_map/ppermute | solution.py:32
  40.5 0.7 collective-permute-start.4
  41.2 3.2 %collective-permute-start.5 = (bf16[2,32,2048]{2,1,0:T(8,128)(2,1)S(1)}, bf16[2,32,2048]{2,1,0:T(8,128)(2,1)S(1)}, u32[]{:S(2)}, u32[]{:S(2)}) collective-permute-start(bf16[2,32,2048]{2,1,0:T(8,128)(2,1)S(1)} %get-tuple-element.26), channel_id=1, source_target_pairs={{0,2},{1,3},{2,0},{3,1},{4,6},{5,7},{6,4},{7,5},{8,10},{9,11},{10,... | collective-permute-start | bytes 786440 | tf_op jit(solution)/shard_map/ppermute | solution.py:32
  44.7 5.2 %collective-permute-done.4 = bf16[2,32,2048]{2,1,0:T(8,128)(2,1)S(1)} collective-permute-done((bf16[2,32,2048]{2,1,0:T(8,128)(2,1)S(1)}, bf16[2,32,2048]{2,1,0:T(8,128)(2,1)S(1)}, u32[]{:S(2)}, u32[]{:S(2)}) %collective-permute-start.4) | collective-permute-done | bytes 262176 | tf_op jit(solution)/shard_map/ppermute | solution.py:32
  49.8 2.2 %collective-permute-done.5 = bf16[2,32,2048]{2,1,0:T(8,128)(2,1)S(1)} collective-permute-done((bf16[2,32,2048]{2,1,0:T(8,128)(2,1)S(1)}, bf16[2,32,2048]{2,1,0:T(8,128)(2,1)S(1)}, u32[]{:S(2)}, u32[]{:S(2)}) %collective-permute-start.5) | collective-permute-done | bytes 262176 | tf_op jit(solution)/shard_map/ppermute | solution.py:32
  52.0 3.7 %collective-permute-done.6 = bf16[2,32,2048]{2,1,0:T(8,128)(2,1)S(1)} collective-permute-done((bf16[2,32,2048]{2,1,0:T(8,128)(2,1)S(1)}, bf16[2,32,2048]{2,1,0:T(8,128)(2,1)S(1)}, u32[]{:S(2)}, u32[]{:S(2)}) %collective-permute-start.6) | collective-permute-done | bytes 262176 | tf_op jit(solution)/shard_map/ppermute | solution.py:32
  56.6 1.9 %collective-permute-done.7.other = bf16[4,2,32,2048]{3,2,1,0:T(8,128)(2,1)S(1)} collective-permute-done((bf16[4,2,32,2048]{3,2,1,0:T(8,128)(2,1)S(1)}, bf16[4,2,32,2048]{3,2,1,0:T(8,128)(2,1)S(1)}, u32[]{:S(2)}, u32[]{:S(2)}) %collective-permute-start.7) | collective-permute-done | bytes 1048608 | tf_op jit(solution)/shard_map/ppermute | solution.py:32
  58.6 3.9 %all-gather.3.cloned.1.call-done.weight = bf16[2048,512]{1,0:T(8,128)(2,1)} async-done(((bf16[256,512]{1,0:T(8,128)(2,1)}), bf16[2048,512]{1,0:T(8,128)(2,1)}) %all-gather.3.cloned.1.call-update) | async-done | bytes 2097168 | tf_op jit(solution)/shard_map/all_gather | solution.py:290
  62.5 1.6 copy-done
  64.1 1.8 %shard_map.96.after = bf16[16,32,512]{2,1,0:T(8,128)(2,1)S(1)} custom-call(s32[8]{0:T(128)S(1)} %stack.47.ids, bf16[4,2,32,2048]{3,2,1,0:T(8,128)(2,1)S(1)} %pad_maximum_fusion.own, bf16[4,2,32,2048]{3,2,1,0:T(8,128)(2,1)S(1)} %collective-permute-done.7.other, bf16[2048,512]{1,0:T(8,128)(2,1)S(1)} %copy-done), custom_call_target="tpu_custom_call" | custom-call | tf_op jit(solution)/shard_map/pallas_call | solution.py:36
  65.9 0.8 copy-done.2
  66.7 0.7 copy-done.13
  67.4 0.8 shard_map.99
  68.2 16.1 %all_to_all.21.own = bf16[16,32,512]{2,1,0:T(8,128)(2,1)} all-to-all(bf16[16,32,512]{2,1,0:T(8,128)(2,1)} %copy-done.2), channel_id=1, replica_groups=mesh['xh'=2,'core'=2,'z'=8,'xl'=2,'y'=4] {'xh','xl','y'}, dimensions={0} | all-to-all | bytes 1048576 | tf_op jit(solution)/shard_map/all_to_all | solution.py:314
  84.3 1.0 dynamic-slice_bitcast_fusion
  85.3 1.2 collective-permute-done.8.other
  86.6 18.3 %shard_map.97 = (bf16[2,32,4096]{2,1,0:T(8,128)(2,1)S(1)}, bf16[2,32,4096]{2,1,0:T(8,128)(2,1)S(1)}, f32[4,1,2048]{2,1,0:T(1,128)S(1)}) custom-call(s32[8]{0:T(128)S(1)} %copy-done.10, bf16[16,32,512]{2,1,0:T(8,128)(2,1)} %all_to_all.21.own, bf16[16,32,512]{2,1,0:T(8,128)(2,1)} %collective-permute-done.8.other, ...), custom_call_target="tpu_custom_call" | custom-call | tf_op jit(solution)/shard_map/pallas_call | solution.py:36
  105.1 1.8 collective-permute-done.9.received
  106.9 0.7 shard_map.98
  107.5 14.9 %all_to_all.22.gradient = bf16[8,32,1024]{2,1,0:T(8,128)(2,1)} all-to-all(bf16[8,32,1024]{2,1,0:T(8,128)(2,1)S(1)} %shard_map.98), channel_id=1, replica_groups=mesh['xh'=2,'core'=2,'z'=8,'xl'=2,'y'=4] {'xh','y'}, dimensions={0} | all-to-all | bytes 1048576 | tf_op jit(solution)/shard_map/all_to_all | solution.py:332
  122.4 1.2 copy-done.4
  123.6 1.6 copy-done.5
  125.2 1.0 copy-done.6
  126.2 2.2 %shard_map.100 = (f32[256,1024]{1,0:T(8,128)S(1)}, f32[8,1024]{1,0:T(8,128)S(1)}, bf16[272,1024]{1,0:T(8,128)(2,1)S(1)}) custom-call(s32[8]{0:T(128)S(1)} %copy-done.10, bf16[8,32,1024]{2,1,0:T(8,128)(2,1)S(1)} %copy-done.6, bf16[4,2,32,2048]{3,2,1,0:T(8,128)(2,1)S(1)} %pad_maximum_fusion.own, bf16[4,2,32,2048]{3,2,1,0:T(8,128)(2,1)S(1)} %copy-done.4, ...), custom_call_target="tpu_custom_call" | custom-call | tf_op jit(solution)/shard_map/pallas_call | solution.py:36
  128.7 1.9 %collective-permute-done.11.received = bf16[272,1024]{1,0:T(8,128)(2,1)S(1)} collective-permute-done((bf16[272,1024]{1,0:T(8,128)(2,1)S(1)}, bf16[272,1024]{1,0:T(8,128)(2,1)S(1)}, u32[]{:S(2)}, u32[]{:S(2)}) %collective-permute-start.11) | collective-permute-done | bytes 557088 | tf_op jit(solution)/shard_map/ppermute | solution.py:32
  130.6 0.6 shard_map.101
  131.3 16.3 %all_to_all.23.received = bf16[8,80,512]{2,1,0:T(8,128)(2,1)S(1)} all-to-all(bf16[8,80,512]{2,1,0:T(8,128)(2,1)S(1)} %shard_map.101), channel_id=1, replica_groups=mesh['xh'=2,'core'=2,'z'=8,'xl'=2,'y'=4] {'xh','y'}, dimensions={0} | all-to-all | bytes 1310720 | tf_op jit(solution)/shard_map/all_to_all | solution.py:343
  147.6 1.4 shard_map.102
  149.2 3.5 %collective-permute-done.12 = f32[8,512]{1,0:T(8,128)S(1)} collective-permute-done((f32[8,512]{1,0:T(8,128)S(1)}, f32[8,512]{1,0:T(8,128)S(1)}, u32[]{:S(2)}, u32[]{:S(2)}) %collective-permute-start.12) | collective-permute-done | bytes 16416 | tf_op jit(solution)/shard_map/ppermute | solution.py:32
  152.7 1.2 collective-permute-start.13
  153.9 2.7 %collective-permute-done.13 = f32[8,512]{1,0:T(8,128)S(1)} collective-permute-done((f32[8,512]{1,0:T(8,128)S(1)}, f32[8,512]{1,0:T(8,128)S(1)}, u32[]{:S(2)}, u32[]{:S(2)}) %collective-permute-start.13) | collective-permute-done | bytes 16416 | tf_op jit(solution)/shard_map/ppermute | solution.py:32
  156.6 1.8 collective-permute-start.14
  158.4 2.9 %collective-permute-done.14 = f32[8,512]{1,0:T(8,128)S(1)} collective-permute-done((f32[8,512]{1,0:T(8,128)S(1)}, f32[8,512]{1,0:T(8,128)S(1)}, u32[]{:S(2)}, u32[]{:S(2)}) %collective-permute-start.14) | collective-permute-done | bytes 16416 | tf_op jit(solution)/shard_map/ppermute | solution.py:32
  161.3 6.6 %collective-permute-start.15 = (f32[8,512]{1,0:T(8,128)S(1)}, f32[8,512]{1,0:T(8,128)S(1)}, u32[]{:S(2)}, u32[]{:S(2)}) collective-permute-start(f32[8,512]{1,0:T(8,128)S(1)} %add.24), channel_id=1, source_target_pairs={{0,32},{1,33},{2,34},{3,35},{4,36},{5,37},{6,38},{7,39},{8,40},{9,... | collective-permute-start | bytes 49160 | tf_op jit(solution)/shard_map/ppermute | solution.py:32
  167.9 1.7 collective-permute-done.15
  169.6 0.6 copy.13
  (49 shorter events, 4.0 us)
Async XLA Ops:
  7.2 55.3 %all-gather.3.cloned.1.call-start = ((), (), s32[]{:S(2)}) async-start(), calls=%async_computation.4 | async-start | bytes 2359296 | tf_op jit(solution)/shard_map/all_gather | solution.py:290
  19.5 36.6 %copy-start.12 = (bf16[8,32,512]{2,1,0:T(8,128)(2,1)S(1)}, bf16[8,32,512]{2,1,0:T(8,128)(2,1)}, u32[]{:S(2)}) copy-start(bf16[8,32,512]{2,1,0:T(8,128)(2,1)} %all_to_all.20) | copy-start | bytes 786436
  19.5 102.9 %all-gather.5.cloned.1.call-start = ((), (), s32[]{:S(2)}) async-start(), calls=%async_computation.5 | async-start | bytes 2359296 | tf_op jit(solution)/shard_map/all_gather | solution.py:313
  23.1 42.8 %copy-start.9 = (s32[8]{0:T(128)}, s32[8]{0:T(128)S(1)}, u32[]{:S(2)}) copy-start(s32[8]{0:T(128)S(1)} %stack.47.ids) | copy-start | bytes 100
  23.1 0.8 copy-start.7
  24.0 0.7 copy-start.11
  25.2 3.5 %collective-permute-start = (bf16[80,512]{1,0:T(8,128)(2,1)S(1)}, bf16[80,512]{1,0:T(8,128)(2,1)S(1)}, u32[]{:S(2)}, u32[]{:S(2)}) collective-permute-start(bf16[80,512]{1,0:T(8,128)(2,1)S(1)} %shard_map.94.p0), channel_id=1, source_target_pairs={{0,64},{1,65},{2,66},{3,67},{4,68},{5,69},{6,70},{7,71},{8,72},{9,... | collective-permute-start | bytes 245768 | tf_op jit(solution)/shard_map/ppermute | solution.py:32
  25.3 6.4 %collective-permute-start.1 = (bf16[80,512]{1,0:T(8,128)(2,1)S(1)}, bf16[80,512]{1,0:T(8,128)(2,1)S(1)}, u32[]{:S(2)}, u32[]{:S(2)}) collective-permute-start(bf16[80,512]{1,0:T(8,128)(2,1)S(1)} %shard_map.94.p0), channel_id=1, source_target_pairs={{0,128},{1,129},{2,130},{3,131},{4,132},{5,133},{6,134},{7,135},{8... | collective-permute-start | bytes 245768 | tf_op jit(solution)/shard_map/ppermute | solution.py:32
  28.1 5.9 %collective-permute-start.2 = (bf16[80,512]{1,0:T(8,128)(2,1)S(1)}, bf16[80,512]{1,0:T(8,128)(2,1)S(1)}, u32[]{:S(2)}, u32[]{:S(2)}) collective-permute-start(bf16[80,512]{1,0:T(8,128)(2,1)S(1)} %shard_map.94.p0), channel_id=1, source_target_pairs={{0,192},{1,193},{2,194},{3,195},{4,196},{5,197},{6,198},{7,199},{8... | collective-permute-start | bytes 245768 | tf_op jit(solution)/shard_map/ppermute | solution.py:32
  34.8 5.6 %collective-permute-start.3 = (bf16[32,2048]{1,0:T(8,128)(2,1)S(1)}, bf16[32,2048]{1,0:T(8,128)(2,1)S(1)}, u32[]{:S(2)}, u32[]{:S(2)}) collective-permute-start(bf16[32,2048]{1,0:T(8,128)(2,1)S(1)} %get-tuple-element.14), channel_id=1, source_target_pairs={{0,4},{1,5},{2,6},{3,7},{4,0},{5,1},{6,2},{7,3},{8,12},{9,13},{10,... | collective-permute-start | bytes 393224 | tf_op jit(solution)/shard_map/ppermute | solution.py:32
  40.5 9.3 %collective-permute-start.4 = (bf16[2,32,2048]{2,1,0:T(8,128)(2,1)S(1)}, bf16[2,32,2048]{2,1,0:T(8,128)(2,1)S(1)}, u32[]{:S(2)}, u32[]{:S(2)}) collective-permute-start(bf16[2,32,2048]{2,1,0:T(8,128)(2,1)S(1)} %get-tuple-element.26), channel_id=1, source_target_pairs={{0,1},{1,2},{2,3},{3,0},{4,5},{5,6},{6,7},{7,4},{8,9},{9,10},{10,1... | collective-permute-start | bytes 786440 | tf_op jit(solution)/shard_map/ppermute | solution.py:32
  41.2 10.8 %collective-permute-start.5 = (bf16[2,32,2048]{2,1,0:T(8,128)(2,1)S(1)}, bf16[2,32,2048]{2,1,0:T(8,128)(2,1)S(1)}, u32[]{:S(2)}, u32[]{:S(2)}) collective-permute-start(bf16[2,32,2048]{2,1,0:T(8,128)(2,1)S(1)} %get-tuple-element.26), channel_id=1, source_target_pairs={{0,2},{1,3},{2,0},{3,1},{4,6},{5,7},{6,4},{7,5},{8,10},{9,11},{10,... | collective-permute-start | bytes 786440 | tf_op jit(solution)/shard_map/ppermute | solution.py:32
  44.4 11.3 %collective-permute-start.6 = (bf16[2,32,2048]{2,1,0:T(8,128)(2,1)S(1)}, bf16[2,32,2048]{2,1,0:T(8,128)(2,1)S(1)}, u32[]{:S(2)}, u32[]{:S(2)}) collective-permute-start(bf16[2,32,2048]{2,1,0:T(8,128)(2,1)S(1)} %get-tuple-element.26), channel_id=1, source_target_pairs={{0,3},{1,0},{2,1},{3,2},{4,7},{5,4},{6,5},{7,6},{8,11},{9,8},{10,9... | collective-permute-start | bytes 786440 | tf_op jit(solution)/shard_map/ppermute | solution.py:32
  55.8 2.7 %collective-permute-start.7 = (bf16[4,2,32,2048]{3,2,1,0:T(8,128)(2,1)S(1)}, bf16[4,2,32,2048]{3,2,1,0:T(8,128)(2,1)S(1)}, u32[]{:S(2)}, u32[]{:S(2)}) collective-permute-start(bf16[4,2,32,2048]{3,2,1,0:T(8,128)(2,1)S(1)} %pad_maximum_fusion.own), channel_id=1, source_target_pairs={{0,64},{1,65},{2,66},{3,67},{4,68},{5,69},{6,70},{7,71},{8,72},{9,... | collective-permute-start | bytes 3145736 | tf_op jit(solution)/shard_map/ppermute | solution.py:32
  56.0 10.7 %collective-permute-start.10 = (bf16[256,512]{1,0:T(8,128)(2,1)S(1)}, bf16[256,512]{1,0:T(8,128)(2,1)S(1)}, u32[]{:S(2)}, u32[]{:S(2)}) collective-permute-start(bf16[256,512]{1,0:T(8,128)(2,1)S(1)} %bitcast.36), channel_id=1, source_target_pairs={{0,4},{1,5},{2,6},{3,7},{4,0},{5,1},{6,2},{7,3},{8,12},{9,13},{10,... | collective-permute-start | bytes 786440 | tf_op jit(solution)/shard_map/ppermute | solution.py:32
  58.6 7.3 %copy-start.3 = (bf16[4,2,32,2048]{3,2,1,0:T(8,128)(2,1)}, bf16[4,2,32,2048]{3,2,1,0:T(8,128)(2,1)S(1)}, u32[]{:S(2)}) copy-start(bf16[4,2,32,2048]{3,2,1,0:T(8,128)(2,1)S(1)} %collective-permute-done.7.other) | copy-start | bytes 3145732
  62.5 1.6 copy-start
  65.9 0.8 copy-start.2
  66.7 0.7 copy-start.13
  67.4 19.2 %copy-start.10 = (s32[8]{0:T(128)S(1)}, s32[8]{0:T(128)}, u32[]{:S(2)}) copy-start(s32[8]{0:T(128)} %copy-done.9) | copy-start | bytes 100
  84.3 2.3 %collective-permute-start.8 = (bf16[16,32,512]{2,1,0:T(8,128)(2,1)}, bf16[16,32,512]{2,1,0:T(8,128)(2,1)}, u32[]{:S(2)}, u32[]{:S(2)}) collective-permute-start(bf16[16,32,512]{2,1,0:T(8,128)(2,1)} %all_to_all.21.own), channel_id=1, source_target_pairs={{0,64},{1,65},{2,66},{3,67},{4,68},{5,69},{6,70},{7,71},{8,72},{9,... | collective-permute-start | bytes 1572872 | tf_op jit(solution)/shard_map/ppermute | solution.py:32
  85.3 37.1 %copy-start.1 = (bf16[2048,512]{1,0:T(8,128)(2,1)S(1)}, bf16[2048,512]{1,0:T(8,128)(2,1)}, u32[]{:S(2)}) copy-start(bf16[2048,512]{1,0:T(8,128)(2,1)} %all-gather.3.cloned.1.call-done.weight) | copy-start | bytes 6291460
  104.9 2.0 %collective-permute-start.9 = (bf16[2,32,4096]{2,1,0:T(8,128)(2,1)S(1)}, bf16[2,32,4096]{2,1,0:T(8,128)(2,1)S(1)}, u32[]{:S(2)}, u32[]{:S(2)}) collective-permute-start(bf16[2,32,4096]{2,1,0:T(8,128)(2,1)S(1)} %get-tuple-element.17), channel_id=1, source_target_pairs={{0,64},{1,65},{2,66},{3,67},{4,68},{5,69},{6,70},{7,71},{8,72},{9,... | collective-permute-start | bytes 1572872 | tf_op jit(solution)/shard_map/ppermute | solution.py:32
  122.4 1.2 copy-start.4
  123.6 1.6 copy-start.5
  125.2 1.0 copy-start.6
  128.4 19.1 %copy-start.8 = (bf16[2,32,512]{2,1,0:T(8,128)(2,1)S(1)}, bf16[2,32,512]{2,1,0:T(8,128)(2,1)}, u32[]{:S(2)}) copy-start(bf16[2,32,512]{2,1,0:T(8,128)(2,1)} %param.7) | copy-start | bytes 196612
  128.4 2.2 %collective-permute-start.11 = (bf16[272,1024]{1,0:T(8,128)(2,1)S(1)}, bf16[272,1024]{1,0:T(8,128)(2,1)S(1)}, u32[]{:S(2)}, u32[]{:S(2)}) collective-permute-start(bf16[272,1024]{1,0:T(8,128)(2,1)S(1)} %get-tuple-element.21), channel_id=1, source_target_pairs={{0,64},{1,65},{2,66},{3,67},{4,68},{5,69},{6,70},{7,71},{8,72},{9,... | collective-permute-start | bytes 1671176 | tf_op jit(solution)/shard_map/ppermute | solution.py:32
  130.6 39.6 %copy-start.14 = (bf16[512]{0:T(512)(128)(2,1)S(1)}, bf16[512]{0:T(512)(128)(2,1)}, u32[]{:S(2)}) copy-start(bf16[512]{0:T(512)(128)(2,1)} %param.9) | copy-start | bytes 3076
  148.9 3.7 %collective-permute-start.12 = (f32[8,512]{1,0:T(8,128)S(1)}, f32[8,512]{1,0:T(8,128)S(1)}, u32[]{:S(2)}, u32[]{:S(2)}) collective-permute-start(f32[8,512]{1,0:T(8,128)S(1)} %get-tuple-element.24), channel_id=1, source_target_pairs={{0,4},{1,5},{2,6},{3,7},{4,0},{5,1},{6,2},{7,3},{8,12},{9,13},{10,... | collective-permute-start | bytes 49160 | tf_op jit(solution)/shard_map/ppermute | solution.py:32
  152.7 3.9 %collective-permute-start.13 = (f32[8,512]{1,0:T(8,128)S(1)}, f32[8,512]{1,0:T(8,128)S(1)}, u32[]{:S(2)}, u32[]{:S(2)}) collective-permute-start(f32[8,512]{1,0:T(8,128)S(1)} %add.22), channel_id=1, source_target_pairs={{0,8},{1,9},{2,10},{3,11},{4,12},{5,13},{6,14},{7,15},{8,0},{9,1},... | collective-permute-start | bytes 49160 | tf_op jit(solution)/shard_map/ppermute | solution.py:32
  156.6 4.6 %collective-permute-start.14 = (f32[8,512]{1,0:T(8,128)S(1)}, f32[8,512]{1,0:T(8,128)S(1)}, u32[]{:S(2)}, u32[]{:S(2)}) collective-permute-start(f32[8,512]{1,0:T(8,128)S(1)} %add.23), channel_id=1, source_target_pairs={{0,16},{1,17},{2,18},{3,19},{4,20},{5,21},{6,22},{7,23},{8,24},{9,... | collective-permute-start | bytes 49160 | tf_op jit(solution)/shard_map/ppermute | solution.py:32
  161.3 8.4 %collective-permute-start.15 = (f32[8,512]{1,0:T(8,128)S(1)}, f32[8,512]{1,0:T(8,128)S(1)}, u32[]{:S(2)}, u32[]{:S(2)}) collective-permute-start(f32[8,512]{1,0:T(8,128)S(1)} %add.24), channel_id=1, source_target_pairs={{0,32},{1,33},{2,34},{3,35},{4,36},{5,37},{6,38},{7,39},{8,40},{9,... | collective-permute-start | bytes 49160 | tf_op jit(solution)/shard_map/ppermute | solution.py:32
Sparse Core Ops, SparseCore 0:
  19.6 42.7 all-gather.2
  68.4 42.2 all-gather.4
where the time goes:
time: 178 us
  blocking collectives  58.4 us (33%)
  waiting for transfers between devices  42.9 us (24%)
  Pallas kernels  27 us (15%)
  starting transfers between devices  19.7 us (11%)
  local copies, waits for them, and re-layouts  14.7 us (8%)
  between operations  14.2 us (8%)
    ppermute x16, waiting for transfers between devices, shift(): return lax.ppermute(block, AXES, pairs)  39 us
    pallas_call x8, Pallas kernels, kernel_call(): pl.pallas_call(body, out_shape=[jax.ShapeDtypeStruct(s, d) for s, d in ou...  26.3 us
    ppermute x16, starting transfers between devices, shift(): return lax.ppermute(block, AXES, pairs)  19.6 us
    all_to_all x1, blocking collectives, per_device(): merged = lax.all_to_all(merged, ('xh', 'y'), 0, 0, tiled=True)  16.3 us
    all_to_all x1, blocking collectives, per_device(): own_pairs = lax.all_to_all(projected, ('xh', 'xl', 'y'), 0, 0, tiled=True)  16.1 us
    all_to_all x1, blocking collectives, per_device(): joined = lax.all_to_all(joined, ('xh', 'y'), 0, 0, tiled=True)  14.9 us
    all_to_all x1, blocking collectives, per_device(): lax.all_to_all(block, ('xl', 'y'), 0, 0, tiled=True).reshape(256, 512)  11.2 us
    unnamed x33, local copies, waits for them, and re-layouts  10.1 us
  transfers between devices with their start and end apart: 18, of which 15 were waited for; matrix products, arithmetic and copies ran while one was open for 3% of the time, Pallas kernels for 12%

commit v1 on v0

v1 whole, which is shorter than its diff:
```python
import jax
import jax.numpy as jnp
import numpy as np
from jax import lax
from jax.experimental import pallas as pl
from jax.experimental.pallas import tpu as pltpu
from jax.sharding import Mesh
from jax.sharding import PartitionSpec as P

D = 2048
HEAD = 64
ENC = 32
ROWS = 32
LAYERS = 4
GROUPS = 8
EPSILON = 1e-06
AXES = ("xh", "core", "z", "xl", "y")
SIZES = (2, 2, 8, 2, 4)
NY = 4
BF, F32 = jnp.bfloat16, jnp.float32
MIB = 1 << 20


def shift(block, **moves):
    pairs = []
    for index in np.ndindex(*SIZES):
        to = list(index)
        for axis, by in moves.items():
            k = AXES.index(axis)
            to[k] = (index[k] + by) % SIZES[k] if axis in "yz" else index[k] ^ by
        pairs.append((int(np.ravel_multi_index(index, SIZES)), int(np.ravel_multi_index(to, SIZES))))
    return lax.ppermute(block, AXES, pairs)


def kernel_call(body, operands, outs, scratch=(), scalars=0, far=(), limit=16):
    spaces = [pltpu.SMEM if i < scalars else pl.ANY if i in far else pltpu.VMEM for i in range(len(operands))]
    return pl.pallas_call(
        body,
        out_shape=[jax.ShapeDtypeStruct(s, d) for s, d in outs],
        in_specs=[pl.BlockSpec(memory_space=space) for space in spaces],
        out_specs=[pl.BlockSpec(memory_space=pltpu.VMEM)] * len(outs),
        scratch_shapes=[x if hasattr(x, "dtype") and not isinstance(x, tuple) else pltpu.VMEM(*x) for x in scratch],
        compiler_params=pltpu.CompilerParams(vmem_limit_bytes=limit * MIB),
    )(*operands)


def coordinates(*axes):
    return tuple(lax.axis_index(axis) for axis in axes)


def lanes(start, size):
    return pl.ds(pl.multiple_of(start, size), size)


def pack_body(states, final_gain, query_gain, pack):
    pack[:64, :] = states[...]
    gains = [final_gain[...].astype(F32)]
    gains += [query_gain[:, i * 512 : (i + 1) * 512].astype(F32) for i in range(4)]
    gains += [jnp.zeros((11, 512), F32)]
    pack[64:, :] = jnp.concatenate(gains, axis=0).astype(BF)


def norm_body(p0, p1, p2, p3, half, factor, query_gains, wide, final_gains):
    xh, c = coordinates("xh", "core")
    section = xh * 2 + c
    for j, pack in enumerate((p0, p1, p2, p3)):
        peer = section ^ j
        wide[:, lanes(peer * 512, 512)] = pack[:64, :].astype(F32)
        gains = pack[64:, :].astype(F32)
        final_gains[:, lanes(peer * 512, 512)] = gains[0:1]
        for i in range(4):
            query_gains[peer, :, i * 512 : (i + 1) * 512] = gains[1 + i : 2 + i]
    states = wide[...]
    scale = lax.rsqrt(jnp.mean(states * states, axis=-1, keepdims=True) + EPSILON)
    factor[...] = jnp.broadcast_to(scale, (64, 128))
    wide[...] = states * scale * final_gains[...]
    half[...] = wide[lanes(c * 32, 32), :].astype(BF)


def project_body(own, other, weight, out, held, result):
    c, xl, y = coordinates("core", "xl", "y")
    for i, rows in enumerate((own, other)):
        m = (c + i) % 2
        result[...] = jnp.dot(rows[...].reshape(256, D), weight[...], preferred_element_type=F32).astype(BF)
        for dy in range(NY):
            for dxl in range(2):
                place = m * 8 + (xl + dxl) % 2 * 4 + (y + NY - dy) % NY
                k = dy * 2 + dxl
                if dxl == 0:
                    held[m, place % 4] = rows[dy, 0]
                out[place] = result[k * 32 : (k + 1) * 32, :]


def decoder_body(lengths, own, other, stream_in, upstream, query_gains, keep, send, gain_parts,
                 pairs, streams, queries, softmax, incoming, gradients):
    xh, c = coordinates("xh", "core")
    length = lengths[xh, 0]
    for i in range(2):
        for k in range(8):
            pairs[2 * i + c, :, k * 512 : (k + 1) * 512] = own[8 * i + k]
            pairs[2 * i + 1 - c, :, k * 512 : (k + 1) * 512] = other[8 * i + k]
    streams[0] = stream_in[...]
    incoming[...] = upstream[...].astype(F32)
    block = (lax.broadcasted_iota(jnp.int32, (128, 256), 0) // 32) == (
        lax.broadcasted_iota(jnp.int32, (128, 256), 1) // HEAD)
    block = jnp.where(block, 1.0, 0.0).astype(BF)
    lane = lax.broadcasted_iota(jnp.int32, (ROWS, 256), 1)
    visible = lax.broadcasted_iota(jnp.int32, (ENC, 1024), 0) < length
    scale = HEAD**-0.5
    def spread(part): return jnp.concatenate([part] * 4, axis=0) * block
    def fold(part):
        low = jnp.where(lane < 64, part[0:32], part[32:64])
        high = jnp.where(lane < 192, part[64:96], part[96:128])
        return jnp.where(lane < 128, low, high)
    def dot(a, b, dims): return lax.dot_general(a, b, (dims, ((), ())), preferred_element_type=F32)
    def col(g, base=0): return slice(base + g * 256, base + (g + 1) * 256)
    def lan(g): return slice(g * 128, (g + 1) * 128)
    G8 = range(GROUPS)
    def forward(layer, carry):
        wide = streams[layer].astype(F32)
        factor = lax.rsqrt(jnp.mean(wide * wide, axis=-1, keepdims=True) + EPSILON)
        q = (wide * factor * query_gains[layer]).astype(BF)
        queries[layer] = q
        scores = jnp.concatenate([dot(pairs[layer, :, col(g)], spread(q[:, col(g)]), ((1,), (1,))) for g in G8], axis=1) * scale
        scores = jnp.where(visible, scores, -1e30)
        highest = jnp.max(scores, axis=0, keepdims=True)
        weights = jnp.where(visible, jnp.exp(scores - highest), 0.0)
        rows = weights / jnp.sum(weights, axis=0, keepdims=True)
        softmax[layer] = rows
        narrow = rows.astype(BF)
        ctx = [fold(dot(narrow[:, lan(g)], pairs[layer, :, col(g, D)], ((0,), (0,)))) for g in G8]
        streams[layer + 1] = (wide + jnp.concatenate(ctx, axis=1)).astype(BF)
        return carry
    lax.fori_loop(0, LAYERS, forward, 0)
    def backward(turn, carry):
        layer = LAYERS - 1 - turn
        wide = streams[layer].astype(F32)
        factor = lax.rsqrt(jnp.mean(wide * wide, axis=-1, keepdims=True) + EPSILON)
        grad = incoming[...]
        narrow_grad = grad.astype(BF)
        rows = softmax[layer]
        narrow = rows.astype(BF)
        parts = []
        for g in G8:
            heads = spread(narrow_grad[:, col(g)])
            parts.append(dot(pairs[layer, :, col(g, D)], heads, ((1,), (1,))))
            gradients[layer, :, col(g, D)] = dot(narrow[:, lan(g)], heads, ((1,), (0,))).astype(BF)
        softmax_gradient = jnp.concatenate(parts, axis=1)
        ds = rows * (softmax_gradient - jnp.sum(rows * softmax_gradient, axis=0, keepdims=True))
        ds = ds.astype(BF)
        q = queries[layer]
        dq = []
        for g in G8:
            dq.append(fold(dot(ds[:, lan(g)], pairs[layer, :, col(g)], ((0,), (0,)))))
            gradients[layer, :, col(g)] = (dot(ds[:, lan(g)], spread(q[:, col(g)]), ((1,), (0,))) * scale).astype(BF)
        gradient = jnp.concatenate(dq, axis=1) * scale
        scaled = gradient * query_gains[layer]
        mean = jnp.mean(scaled * wide, axis=-1, keepdims=True)
        incoming[...] = grad + factor * scaled - wide * (factor * factor * factor) * mean
        gain_parts[layer] = jnp.sum(gradient * wide * factor, axis=0, keepdims=True)
        return carry
    lax.fori_loop(0, LAYERS, backward, 0)
    for i in range(2):
        keep[i] = gradients[2 * i + c]
        send[i] = gradients[2 * i + 1 - c]


def join_body(keep, received, out):
    for xh in range(2):
        for y in range(NY):
            for half in range(2):
                span = slice(half * 2048 + y * 512, half * 2048 + (y + 1) * 512)
                total = keep[xh, :, span].astype(F32) + received[xh, :, span].astype(F32)
                out[xh * NY + y, :, half * 512 : (half + 1) * 512] = total.astype(BF)


def high_low(part):
    high = part.astype(BF)
    return high, (part - high.astype(F32)).astype(BF)


def back_body(gradient, held, weight, partner, gain_parts, keep, extra, send, terms, parts, rows):
    c, xl = coordinates("core", "xl")
    mine = gradient[:, :, lanes(xl * 512, 512)].reshape(256, 512)
    theirs = gradient[:, :, lanes((1 - xl) * 512, 512)].reshape(256, 512)
    dims = (((1,), (1,)), ((), ()))
    for q in range(4):
        span = slice(q * 512, (q + 1) * 512)
        terms[:, span] = lax.dot_general(mine, weight[span, :], dims, preferred_element_type=F32) + lax.dot_general(
            theirs, partner[span, :], dims, preferred_element_type=F32
        )
    for m in range(2):
        for peer in range(NY):
            place = (m * NY + peer) * 32
            product = terms[place : place + 32, :] * held[m, peer].astype(F32)
            if place == 0:
                parts[...] = jnp.sum(product, axis=0, keepdims=True)
            else:
                parts[...] += jnp.sum(product, axis=0, keepdims=True)
            rows[place : place + 32, :] = jnp.broadcast_to(jnp.sum(product, axis=1, keepdims=True), (32, 128))
    row_sums = jnp.transpose(rows[...])[0:1, :]
    for parity, is_send in ((c, False), (1 - c, True)):
        extras = []
        for i in range(2):
            layer_gain = gain_parts[2 * i + parity]
            extras += [layer_gain[:, :1024], layer_gain[:, 1024:]]
        extras.append(
            jnp.concatenate([parts[:, lanes((2 * i + parity) * 512, 512)] for i in range(2)], axis=1)
        )
        extras.append(jnp.concatenate([row_sums, jnp.zeros((1, 768), F32)], axis=1))
        extras.append(jnp.zeros((2, 1024), F32))
        block = jnp.concatenate(extras, axis=0)
        for i in range(2):
            part = terms[:, lanes((2 * i + parity) * 512, 512)]
            if is_send:
                send[:256, i * 512 : (i + 1) * 512] = part.astype(BF)
            else:
                keep[:, i * 512 : (i + 1) * 512] = part
        if is_send:
            send[256:, :] = jnp.concatenate(high_low(block), axis=0)
        else:
            extra[...] = block


def merge_body(keep, extra, received, out):
    carried = received[256:, :].astype(F32)
    extras = extra[...] + carried[0:8] + carried[8:16]
    for xh in range(2):
        span = slice(xh * 512, (xh + 1) * 512)
        block = jnp.concatenate(
            [
                extras[2 * xh : 2 * xh + 1, :512],
                extras[2 * xh : 2 * xh + 1, 512:],
                extras[2 * xh + 1 : 2 * xh + 2, :512],
                extras[2 * xh + 1 : 2 * xh + 2, 512:],
                extras[4:5, span],
                extras[5:6, :512],
                jnp.zeros((2, 512), F32),
            ],
            axis=0,
        )
        block = jnp.concatenate(high_low(block), axis=0)
        for y in range(NY):
            for m in range(2):
                place = (m * NY + y) * 32
                part = keep[place : place + 32, span] + received[place : place + 32, span].astype(F32)
                out[xh * NY + y, m * 32 : (m + 1) * 32, :] = part.astype(BF)
            out[xh * NY + y, 64:, :] = block


def finish_body(received, states, factor, final_gain, gradient, sums, rows):
    (y,) = coordinates("y")
    total = received[0].astype(F32)
    for k in range(1, 8):
        total += received[k].astype(F32)
    extras = total[64:72] + total[72:80]
    sums[...] = extras
    rows[...] = jnp.transpose(jnp.broadcast_to(extras[5:6, :256], (128, 256)))
    for m in range(2):
        span = slice(m * 32, (m + 1) * 32)
        row_sum = rows[lanes(m * 128 + y * 32, 32), 0:1]
        scale = factor[span, 0:1]
        scaled = total[span] * final_gain[...].astype(F32)
        wide = states[span, :].astype(F32)
        gradient[span, :] = scale * scaled - wide * (scale * scale * (row_sum / D))


def per_device(
    encoder_states, encoder_lengths, final_gain, decoder_states, query_gain, cross_weight, upstream
):
    xh, c = coordinates("xh", "core")
    block = cross_weight[0].reshape(32, 8, 512).transpose(1, 0, 2)
    block = lax.all_to_all(block, ("xl", "y"), 0, 0, tiled=True).reshape(256, 512)
    weight = lax.all_gather(block, "z", axis=0, tiled=True)

    states = encoder_states.reshape(64, 512)
    stream = lax.dynamic_slice(decoder_states, (xh, c * ROWS, 0), (1, ROWS, D))[0]
    incoming = lax.dynamic_slice(upstream, (xh, c * ROWS, 0), (1, ROWS, D))[0]
    (pack,) = kernel_call(pack_body, (states, final_gain[None], query_gain), [((80, 512), BF)])
    packs = [pack, shift(pack, core=1), shift(pack, xh=1), shift(pack, xh=1, core=1)]
    half, factor, query_gains = kernel_call(
        norm_body,
        packs,
        [((32, D), BF), ((64, 128), F32), ((4, 1, D), F32)],
        [((64, D), F32), ((1, D), F32)],
    )
    both = jnp.stack([half, shift(half, xl=1)])
    own_rows = jnp.stack([both] + [shift(both, y=dy) for dy in range(1, NY)])
    other_rows = shift(own_rows, core=1)
    partner_block = shift(block, xl=1)

    projected, held = kernel_call(
        project_body,
        (own_rows, other_rows, weight),
        [((16, 32, 512), BF), ((2, NY, 32, D), BF)],
        [((256, 512), BF)],
    )
    partner = lax.all_gather(partner_block, "z", axis=0, tiled=True)
    own_pairs = lax.all_to_all(projected, ("xh", "xl", "y"), 0, 0, tiled=True)
    other_pairs = shift(own_pairs, core=1)
    keep, send, gain_parts = kernel_call(
        decoder_body,
        (encoder_lengths, own_pairs, other_pairs, stream, incoming, query_gains),
        [((2, 32, 4096), BF), ((2, 32, 4096), BF), ((4, 1, D), F32)],
        [
            ((4, 32, 4096), BF),
            ((5, ROWS, D), BF),
            ((4, ROWS, D), BF),
            ((4, ENC, 1024), F32),
            ((ROWS, D), F32),
            ((4, 32, 4096), BF),
        ],
        scalars=1,
    )
    (joined,) = kernel_call(join_body, (keep, shift(send, core=1)), [((8, 32, 1024), BF)])
    joined = lax.all_to_all(joined, ("xh", "y"), 0, 0, tiled=True)
    term_keep, extra, term_send = kernel_call(
        back_body,
        (joined, held, weight, partner, gain_parts),
        [((256, 1024), F32), ((8, 1024), F32), ((272, 1024), BF)],
        [((256, D), F32), ((1, D), F32), ((256, 128), F32)],
    )
    (merged,) = kernel_call(
        merge_body, (term_keep, extra, shift(term_send, core=1)), [((8, 80, 512), BF)]
    )
    merged = lax.all_to_all(merged, ("xh", "y"), 0, 0, tiled=True)
    gradient, sums = kernel_call(
        finish_body,
        (merged, states, factor, final_gain[None]),
        [((64, 512), F32), ((8, 512), F32)],
        [((256, 128), F32)],
    )
    sums = sums + shift(sums, xl=1)
    ahead = shift(sums, z=1)
    pair = sums + ahead
    triple = pair + shift(sums, z=-1)
    sums = triple + shift(triple, z=-3) + shift(pair, z=2)
    final_gradient = sums[4] / final_gain.astype(F32)
    return (gradient.reshape(2, 32, 512), final_gradient, sums[:4].reshape(1, D))


def solution(mesh):
    dp, section = ("z", "xl", "y"), ("xh", "core")
    return jax.shard_map(
        per_device,
        mesh=Mesh(mesh.devices.reshape(SIZES), AXES),
        in_specs=(
            P(None, dp, section),
            P(None, dp),
            P(section),
            P(None, dp, None),
            P(section, None),
            P(section, dp, None),
            P(None, dp, None),
        ),
        out_specs=(P(None, dp, section), P(section), P(section, None)),
        check_vma=False,
    )
```

time: 178 us -> 158 us (0.89)
  Pallas kernels: 27 us -> 11.1 us
  blocking collectives: 58.4 us -> 44.2 us
  waiting for transfers between devices: 42.9 us -> 51.9 us
  starting transfers between devices: 19.7 us -> 23.8 us
  local copies, waits for them, and re-layouts: 14.7 us -> 11.1 us
    pallas_call x8, Pallas kernels: 26.3 us -> 11.1 us  [kernel_call(): pl.pallas_call(body, out_shape=[jax.ShapeDtypeStruct(s, d) for s, d in ou...]
    all_to_all x1 -> x0, blocking collectives: 14.9 us -> none  [per_device(): joined = lax.all_to_all(joined, ('xh', 'y'), 0, 0, tiled=True)]
    all_gather x1, waiting for transfers between devices: 0.01 us -> 6.31 us  [per_device(): partner = lax.all_gather(partner_block, 'z', axis=0, tiled=True)]
    all_to_all x0 -> x1, starting transfers between devices: none -> 4.86 us  [per_device(): joined = lax.all_to_all(joined, ('xh', 'y'), 0, 0, tiled=True)]
    ppermute x16 -> x17, waiting for transfers between devices: 39 us -> 35.6 us  [shift(): return lax.ppermute(block, AXES, pairs)]
    all_to_all x0 -> x1, waiting for transfers between devices: none -> 3.22 us  [per_device(): joined = lax.all_to_all(joined, ('xh', 'y'), 0, 0, tiled=True)]
    all_gather x1, waiting for transfers between devices: 3.88 us -> 6.75 us  [per_device(): weight = lax.all_gather(block, 'z', axis=0, tiled=True)]
    unnamed x33 -> x26, local copies, waits for them, and re-layouts: 10.1 us -> 9.38 us
  transfers between devices with their start and end apart: 18 -> 20, of which waited for: 15 -> 16; matrix products, arithmetic and copies ran while one was open for 3% -> 1% of each run, Pallas kernels for 12% -> 5%
where the time goes in v1:
time: 158 us; the launch traced here: 157 us
  waiting for transfers between devices  51.9 us (33%)
  blocking collectives  44.2 us (28%)
  starting transfers between devices  23.8 us (15%)
  between operations  14.2 us (9%)
  local copies, waits for them, and re-layouts  11.1 us (7%)
  Pallas kernels  11.1 us (7%)
    ppermute x17, waiting for transfers between devices, shift(): return lax.ppermute(block, AXES, pairs)  35.6 us
    ppermute x17, starting transfers between devices, shift(): return lax.ppermute(block, AXES, pairs)  18.8 us
    all_to_all x1, blocking collectives, per_device(): merged = lax.all_to_all(merged, ('xh', 'y'), 0, 0, tiled=True)  16.9 us
    all_to_all x1, blocking collectives, per_device(): own_pairs = lax.all_to_all(projected, ('xh', 'xl', 'y'), 0, 0, tiled=True)  16.1 us
    all_to_all x1, blocking collectives, per_device(): lax.all_to_all(block, ('xl', 'y'), 0, 0, tiled=True).reshape(256, 512)  11.2 us
    pallas_call x8, Pallas kernels, kernel_call(): pl.pallas_call(body, out_shape=[jax.ShapeDtypeStruct(s, d) for s, d in ou...  11.1 us
    unnamed x26, local copies, waits for them, and re-layouts  9.38 us
    all_gather x1, waiting for transfers between devices, per_device(): weight = lax.all_gather(block, 'z', axis=0, tiled=True)  6.75 us
  transfers between devices with their start and end apart: 20, of which 16 were waited for; matrix products, arithmetic and copies ran while one was open for 1% of the time, Pallas kernels for 5%

profile of v1, /device:TPU:8, one launch (start us, length us, event | category | flops | bytes accessed | tf_op | source)
XLA Modules:
  0.0 157.1 jit_solution(7491484180539666234)
XLA Ops:
  7.2 1.0 copy.12
  8.3 11.2 %all_to_all.20 = bf16[8,32,512]{2,1,0:T(8,128)(2,1)} all-to-all(bf16[8,32,512]{2,1,0:T(8,128)(2,1)S(1)} %bitcast.30), channel_id=1, replica_groups=mesh['xh'=2,'core'=2,'z'=8,'xl'=2,'y'=4] {'xl','y'}, dimensions={0} | all-to-all | bytes 524288 | tf_op jit(solution)/shard_map/all_to_all | solution.py:273
  19.6 1.4 collective-permute-start.10
  20.9 0.7 broadcast_in_dim.4.final_gain
  21.6 0.8 copy-done.5
  22.4 0.7 copy-done.7
  23.3 2.8 %collective-permute-start.1 = (bf16[80,512]{1,0:T(8,128)(2,1)S(1)}, bf16[80,512]{1,0:T(8,128)(2,1)S(1)}, u32[]{:S(2)}, u32[]{:S(2)}) collective-permute-start(bf16[80,512]{1,0:T(8,128)(2,1)S(1)} %shard_map.94.p0), channel_id=1, source_target_pairs={{0,128},{1,129},{2,130},{3,131},{4,132},{5,133},{6,134},{7,135},{8... | collective-permute-start | bytes 245768 | tf_op jit(solution)/shard_map/ppermute | solution.py:32
  26.1 0.6 collective-permute-start.2
  26.6 3.8 %collective-permute-done.1.p2 = bf16[80,512]{1,0:T(8,128)(2,1)S(1)} collective-permute-done((bf16[80,512]{1,0:T(8,128)(2,1)S(1)}, bf16[80,512]{1,0:T(8,128)(2,1)S(1)}, u32[]{:S(2)}, u32[]{:S(2)}) %collective-permute-start.1) | collective-permute-done | bytes 81952 | tf_op jit(solution)/shard_map/ppermute | solution.py:32
  30.4 1.6 %collective-permute-done.2.p3 = bf16[80,512]{1,0:T(8,128)(2,1)S(1)} collective-permute-done((bf16[80,512]{1,0:T(8,128)(2,1)S(1)}, bf16[80,512]{1,0:T(8,128)(2,1)S(1)}, u32[]{:S(2)}, u32[]{:S(2)}) %collective-permute-start.2) | collective-permute-done | bytes 81952 | tf_op jit(solution)/shard_map/ppermute | solution.py:32
  32.5 0.7 copy-done.8
  33.2 4.7 %collective-permute-done.3 = bf16[32,2048]{1,0:T(8,128)(2,1)S(1)} collective-permute-done((bf16[32,2048]{1,0:T(8,128)(2,1)S(1)}, bf16[32,2048]{1,0:T(8,128)(2,1)S(1)}, u32[]{:S(2)}, u32[]{:S(2)}) %collective-permute-start.3) | collective-permute-done | bytes 131104 | tf_op jit(solution)/shard_map/ppermute | solution.py:32
  37.9 0.3 collective-permute-start.4
  38.2 3.0 %collective-permute-start.5 = (bf16[2,32,2048]{2,1,0:T(8,128)(2,1)S(1)}, bf16[2,32,2048]{2,1,0:T(8,128)(2,1)S(1)}, u32[]{:S(2)}, u32[]{:S(2)}) collective-permute-start(bf16[2,32,2048]{2,1,0:T(8,128)(2,1)S(1)} %get-tuple-element.32), channel_id=1, source_target_pairs={{0,2},{1,3},{2,0},{3,1},{4,6},{5,7},{6,4},{7,5},{8,10},{9,11},{10,... | collective-permute-start | bytes 786440 | tf_op jit(solution)/shard_map/ppermute | solution.py:32
  41.2 0.9 collective-permute-start.6
  42.1 5.2 %collective-permute-done.4 = bf16[2,32,2048]{2,1,0:T(8,128)(2,1)S(1)} collective-permute-done((bf16[2,32,2048]{2,1,0:T(8,128)(2,1)S(1)}, bf16[2,32,2048]{2,1,0:T(8,128)(2,1)S(1)}, u32[]{:S(2)}, u32[]{:S(2)}) %collective-permute-start.4) | collective-permute-done | bytes 262176 | tf_op jit(solution)/shard_map/ppermute | solution.py:32
  47.2 1.8 %collective-permute-done.5 = bf16[2,32,2048]{2,1,0:T(8,128)(2,1)S(1)} collective-permute-done((bf16[2,32,2048]{2,1,0:T(8,128)(2,1)S(1)}, bf16[2,32,2048]{2,1,0:T(8,128)(2,1)S(1)}, u32[]{:S(2)}, u32[]{:S(2)}) %collective-permute-start.5) | collective-permute-done | bytes 262176 | tf_op jit(solution)/shard_map/ppermute | solution.py:32
  49.0 3.9 %collective-permute-done.6 = bf16[2,32,2048]{2,1,0:T(8,128)(2,1)S(1)} collective-permute-done((bf16[2,32,2048]{2,1,0:T(8,128)(2,1)S(1)}, bf16[2,32,2048]{2,1,0:T(8,128)(2,1)S(1)}, u32[]{:S(2)}, u32[]{:S(2)}) %collective-permute-start.6) | collective-permute-done | bytes 262176 | tf_op jit(solution)/shard_map/ppermute | solution.py:32
  53.2 2.5 %collective-permute-done.7.other = bf16[4,2,32,2048]{3,2,1,0:T(8,128)(2,1)S(1)} collective-permute-done((bf16[4,2,32,2048]{3,2,1,0:T(8,128)(2,1)S(1)}, bf16[4,2,32,2048]{3,2,1,0:T(8,128)(2,1)S(1)}, u32[]{:S(2)}, u32[]{:S(2)}) %collective-permute-start.7) | collective-permute-done | bytes 1048608 | tf_op jit(solution)/shard_map/ppermute | solution.py:32
  55.7 6.8 %all-gather.3.cloned.1.call-done.weight = bf16[2048,512]{1,0:T(8,128)(2,1)} async-done(((bf16[256,512]{1,0:T(8,128)(2,1)}), bf16[2048,512]{1,0:T(8,128)(2,1)}) %all-gather.3.cloned.1.call-update) | async-done | bytes 2097168 | tf_op jit(solution)/shard_map/all_gather | solution.py:274
  62.5 1.6 %copy-done = bf16[2048,512]{1,0:T(8,128)(2,1)S(1)} copy-done((bf16[2048,512]{1,0:T(8,128)(2,1)S(1)}, bf16[2048,512]{1,0:T(8,128)(2,1)}, u32[]{:S(2)}) %copy-start) | copy-done | bytes 2097176
  64.1 1.2 shard_map.96
  65.3 1.0 copy-done.3
  66.3 16.1 %all_to_all.21.own = bf16[16,32,512]{2,1,0:T(8,128)(2,1)S(1)} all-to-all(bf16[16,32,512]{2,1,0:T(8,128)(2,1)S(1)} %get-tuple-element.17), channel_id=1, replica_groups=mesh['xh'=2,'core'=2,'z'=8,'xl'=2,'y'=4] {'xh','xl','y'}, dimensions={0} | all-to-all | bytes 1048576 | tf_op jit(solution)/shard_map/all_to_all | solution.py:299
  82.5 1.0 dynamic-slice_bitcast_fusion
  83.5 0.8 collective-permute-done.8.other
  84.3 6.0 %shard_map.97 = (bf16[2,32,4096]{2,1,0:T(8,128)(2,1)S(1)}, bf16[2,32,4096]{2,1,0:T(8,128)(2,1)S(1)}, f32[4,1,2048]{2,1,0:T(1,128)S(1)}) custom-call(s32[2,1]{1,0:T(2,128)S(1)} %copy.11.lengths, bf16[16,32,512]{2,1,0:T(8,128)(2,1)S(1)} %all_to_all.21.own, bf16[16,32,512]{2,1,0:T(8,128)(2,1)S(1)} %collective-permute-done.8.other, ...), custom_call_target="tpu_custom_call" | custom-call | tf_op jit(solution)/shard_map/pallas_call | solution.py:37
  90.6 1.8 %collective-permute-done.9.received = bf16[2,32,4096]{2,1,0:T(8,128)(2,1)S(1)} collective-permute-done((bf16[2,32,4096]{2,1,0:T(8,128)(2,1)S(1)}, bf16[2,32,4096]{2,1,0:T(8,128)(2,1)S(1)}, u32[]{:S(2)}, u32[]{:S(2)}) %collective-permute-start.9) | collective-permute-done | bytes 524320 | tf_op jit(solution)/shard_map/ppermute | solution.py:32
  92.4 0.9 shard_map.98
  93.3 4.9 %all-to-all-start.2 = ((bf16[8,32,1024]{2,1,0:T(8,128)(2,1)}), bf16[8,32,1024]{2,1,0:T(8,128)(2,1)S(1)}, u32[]{:S(2)}, u32[]{:S(2)}) async-start(bf16[8,32,1024]{2,1,0:T(8,128)(2,1)} %shard_map.98), calls=%async_computation.2 | async-start | bytes 1048576 | tf_op jit(solution)/shard_map/all_to_all | solution.py:316
  98.1 6.3 %all-gather.5.cloned.1.call-done.partner = bf16[2048,512]{1,0:T(8,128)(2,1)} async-done(((bf16[256,512]{1,0:T(8,128)(2,1)}), bf16[2048,512]{1,0:T(8,128)(2,1)}) %all-gather.5.cloned.1.call-update) | async-done | bytes 2097168 | tf_op jit(solution)/shard_map/all_gather | solution.py:298
  104.4 3.2 %all-to-all-done.2.gradient = bf16[8,32,1024]{2,1,0:T(8,128)(2,1)S(1)} async-done(((bf16[8,32,1024]{2,1,0:T(8,128)(2,1)}), bf16[8,32,1024]{2,1,0:T(8,128)(2,1)S(1)}, u32[]{:S(2)}, u32[]{:S(2)}) %all-to-all-start.2) | async-done | bytes 524320 | tf_op jit(solution)/shard_map/all_to_all | solution.py:316
  107.6 1.6 %copy-done.2 = bf16[2048,512]{1,0:T(8,128)(2,1)S(1)} copy-done((bf16[2048,512]{1,0:T(8,128)(2,1)S(1)}, bf16[2048,512]{1,0:T(8,128)(2,1)}, u32[]{:S(2)}) %copy-start.2) | copy-done | bytes 2097176
  109.2 1.2 copy-done.4
  110.5 1.7 %shard_map.99 = (f32[256,1024]{1,0:T(8,128)S(1)}, f32[8,1024]{1,0:T(8,128)S(1)}, bf16[272,1024]{1,0:T(8,128)(2,1)S(1)}) custom-call(bf16[8,32,1024]{2,1,0:T(8,128)(2,1)S(1)} %all-to-all-done.2.gradient, bf16[2,4,32,2048]{3,2,1,0:T(8,128)(2,1)S(1)} %copy-done.4, bf16[2048,512]{1,0:T(8,128)(2,1)S(1)} %copy-done.1, bf16[2048,512]{1,0:T(8,128)(2,1)S(1)} %copy-done.2, ...), custom_call_target="tpu_custom_call" | custom-call | tf_op jit(solution)/shard_map/pallas_call | solution.py:37
  112.2 0.3 collective-permute-start.11
  112.5 1.9 %collective-permute-done.11.received = bf16[272,1024]{1,0:T(8,128)(2,1)S(1)} collective-permute-done((bf16[272,1024]{1,0:T(8,128)(2,1)S(1)}, bf16[272,1024]{1,0:T(8,128)(2,1)S(1)}, u32[]{:S(2)}, u32[]{:S(2)}) %collective-permute-start.11) | collective-permute-done | bytes 557088 | tf_op jit(solution)/shard_map/ppermute | solution.py:32
  114.5 16.9 %all_to_all.22.received = bf16[8,80,512]{2,1,0:T(8,128)(2,1)S(1)} all-to-all(bf16[8,80,512]{2,1,0:T(8,128)(2,1)S(1)} %shard_map.100), channel_id=1, replica_groups=mesh['xh'=2,'core'=2,'z'=8,'xl'=2,'y'=4] {'xh','y'}, dimensions={0} | all-to-all | bytes 1310720 | tf_op jit(solution)/shard_map/all_to_all | solution.py:326
  131.5 0.9 shard_map.101
  132.4 3.7 %collective-permute-done.12 = f32[8,512]{1,0:T(8,128)S(1)} collective-permute-done((f32[8,512]{1,0:T(8,128)S(1)}, f32[8,512]{1,0:T(8,128)S(1)}, u32[]{:S(2)}, u32[]{:S(2)}) %collective-permute-start.12) | collective-permute-done | bytes 16416 | tf_op jit(solution)/shard_map/ppermute | solution.py:32
  136.1 0.9 collective-permute-start.13
  137.0 2.3 %collective-permute-start.14 = (f32[8,512]{1,0:T(8,128)S(1)}, f32[8,512]{1,0:T(8,128)S(1)}, u32[]{:S(2)}, u32[]{:S(2)}) collective-permute-start(f32[8,512]{1,0:T(8,128)S(1)} %add.25), channel_id=1, source_target_pairs={{0,56},{1,57},{2,58},{3,59},{4,60},{5,61},{6,62},{7,63},{8,0},{9,1... | collective-permute-start | bytes 49160 | tf_op jit(solution)/shard_map/ppermute | solution.py:32
  139.3 1.7 %collective-permute-done.13 = f32[8,512]{1,0:T(8,128)S(1)} collective-permute-done((f32[8,512]{1,0:T(8,128)S(1)}, f32[8,512]{1,0:T(8,128)S(1)}, u32[]{:S(2)}, u32[]{:S(2)}) %collective-permute-start.13) | collective-permute-done | bytes 16416 | tf_op jit(solution)/shard_map/ppermute | solution.py:32
  141.1 2.0 %collective-permute-start.15 = (f32[8,512]{1,0:T(8,128)S(1)}, f32[8,512]{1,0:T(8,128)S(1)}, u32[]{:S(2)}, u32[]{:S(2)}) collective-permute-start(f32[8,512]{1,0:T(8,128)S(1)} %get-tuple-element.29), channel_id=1, source_target_pairs={{0,40},{1,41},{2,42},{3,43},{4,44},{5,45},{6,46},{7,47},{8,48},{9,... | collective-permute-start | bytes 49160 | tf_op jit(solution)/shard_map/ppermute | solution.py:32
  143.0 3.6 %collective-permute-start.16 = (f32[8,512]{1,0:T(8,128)S(1)}, f32[8,512]{1,0:T(8,128)S(1)}, u32[]{:S(2)}, u32[]{:S(2)}) collective-permute-start(f32[8,512]{1,0:T(8,128)S(1)} %get-tuple-element.30), channel_id=1, source_target_pairs={{0,16},{1,17},{2,18},{3,19},{4,20},{5,21},{6,22},{7,23},{8,24},{9,... | collective-permute-start | bytes 49160 | tf_op jit(solution)/shard_map/ppermute | solution.py:32
  146.7 2.3 %collective-permute-done.16 = f32[8,512]{1,0:T(8,128)S(1)} collective-permute-done((f32[8,512]{1,0:T(8,128)S(1)}, f32[8,512]{1,0:T(8,128)S(1)}, u32[]{:S(2)}, u32[]{:S(2)}) %collective-permute-start.16) | collective-permute-done | bytes 16416 | tf_op jit(solution)/shard_map/ppermute | solution.py:32
  149.0 0.6 copy.13
  149.6 0.6 convert_divide_fusion
  (41 shorter events, 1.7 us)
Async XLA Ops:
  7.2 55.3 %all-gather.3.cloned.1.call-start = ((), (), s32[]{:S(2)}) async-start(), calls=%async_computation.4 | async-start | bytes 2359296 | tf_op jit(solution)/shard_map/all_gather | solution.py:274
  19.5 84.9 %all-gather.5.cloned.1.call-start = ((), (), s32[]{:S(2)}) async-start(), calls=%async_computation.5 | async-start | bytes 2359296 | tf_op jit(solution)/shard_map/all_gather | solution.py:298
  19.6 12.9 %collective-permute-start.10 = (bf16[256,512]{1,0:T(8,128)(2,1)}, bf16[256,512]{1,0:T(8,128)(2,1)S(1)}, u32[]{:S(2)}, u32[]{:S(2)}) collective-permute-start(bf16[256,512]{1,0:T(8,128)(2,1)} %bitcast.29), channel_id=1, source_target_pairs={{0,4},{1,5},{2,6},{3,7},{4,0},{5,1},{6,2},{7,3},{8,12},{9,13},{10,... | collective-permute-start | bytes 786440 | tf_op jit(solution)/shard_map/ppermute | solution.py:32
  21.6 0.8 copy-start.5
  22.4 0.7 copy-start.7
  23.2 3.5 %collective-permute-start = (bf16[80,512]{1,0:T(8,128)(2,1)S(1)}, bf16[80,512]{1,0:T(8,128)(2,1)S(1)}, u32[]{:S(2)}, u32[]{:S(2)}) collective-permute-start(bf16[80,512]{1,0:T(8,128)(2,1)S(1)} %shard_map.94.p0), channel_id=1, source_target_pairs={{0,64},{1,65},{2,66},{3,67},{4,68},{5,69},{6,70},{7,71},{8,72},{9,... | collective-permute-start | bytes 245768 | tf_op jit(solution)/shard_map/ppermute | solution.py:32
  23.3 7.1 %collective-permute-start.1 = (bf16[80,512]{1,0:T(8,128)(2,1)S(1)}, bf16[80,512]{1,0:T(8,128)(2,1)S(1)}, u32[]{:S(2)}, u32[]{:S(2)}) collective-permute-start(bf16[80,512]{1,0:T(8,128)(2,1)S(1)} %shard_map.94.p0), channel_id=1, source_target_pairs={{0,128},{1,129},{2,130},{3,131},{4,132},{5,133},{6,134},{7,135},{8... | collective-permute-start | bytes 245768 | tf_op jit(solution)/shard_map/ppermute | solution.py:32
  26.1 5.9 %collective-permute-start.2 = (bf16[80,512]{1,0:T(8,128)(2,1)S(1)}, bf16[80,512]{1,0:T(8,128)(2,1)S(1)}, u32[]{:S(2)}, u32[]{:S(2)}) collective-permute-start(bf16[80,512]{1,0:T(8,128)(2,1)S(1)} %shard_map.94.p0), channel_id=1, source_target_pairs={{0,192},{1,193},{2,194},{3,195},{4,196},{5,197},{6,198},{7,199},{8... | collective-permute-start | bytes 245768 | tf_op jit(solution)/shard_map/ppermute | solution.py:32
  32.2 5.6 %collective-permute-start.3 = (bf16[32,2048]{1,0:T(8,128)(2,1)S(1)}, bf16[32,2048]{1,0:T(8,128)(2,1)S(1)}, u32[]{:S(2)}, u32[]{:S(2)}) collective-permute-start(bf16[32,2048]{1,0:T(8,128)(2,1)S(1)} %get-tuple-element.16), channel_id=1, source_target_pairs={{0,4},{1,5},{2,6},{3,7},{4,0},{5,1},{6,2},{7,3},{8,12},{9,13},{10,... | collective-permute-start | bytes 393224 | tf_op jit(solution)/shard_map/ppermute | solution.py:32
  32.5 0.7 copy-start.8
  37.9 9.3 %collective-permute-start.4 = (bf16[2,32,2048]{2,1,0:T(8,128)(2,1)S(1)}, bf16[2,32,2048]{2,1,0:T(8,128)(2,1)S(1)}, u32[]{:S(2)}, u32[]{:S(2)}) collective-permute-start(bf16[2,32,2048]{2,1,0:T(8,128)(2,1)S(1)} %get-tuple-element.32), channel_id=1, source_target_pairs={{0,1},{1,2},{2,3},{3,0},{4,5},{5,6},{6,7},{7,4},{8,9},{9,10},{10,1... | collective-permute-start | bytes 786440 | tf_op jit(solution)/shard_map/ppermute | solution.py:32
  38.2 10.8 %collective-permute-start.5 = (bf16[2,32,2048]{2,1,0:T(8,128)(2,1)S(1)}, bf16[2,32,2048]{2,1,0:T(8,128)(2,1)S(1)}, u32[]{:S(2)}, u32[]{:S(2)}) collective-permute-start(bf16[2,32,2048]{2,1,0:T(8,128)(2,1)S(1)} %get-tuple-element.32), channel_id=1, source_target_pairs={{0,2},{1,3},{2,0},{3,1},{4,6},{5,7},{6,4},{7,5},{8,10},{9,11},{10,... | collective-permute-start | bytes 786440 | tf_op jit(solution)/shard_map/ppermute | solution.py:32
  41.2 11.6 %collective-permute-start.6 = (bf16[2,32,2048]{2,1,0:T(8,128)(2,1)S(1)}, bf16[2,32,2048]{2,1,0:T(8,128)(2,1)S(1)}, u32[]{:S(2)}, u32[]{:S(2)}) collective-permute-start(bf16[2,32,2048]{2,1,0:T(8,128)(2,1)S(1)} %get-tuple-element.32), channel_id=1, source_target_pairs={{0,3},{1,0},{2,1},{3,2},{4,7},{5,4},{6,5},{7,6},{8,11},{9,8},{10,9... | collective-permute-start | bytes 786440 | tf_op jit(solution)/shard_map/ppermute | solution.py:32
  52.8 29.6 %copy-start.10 = (s32[2,1]{0,1:T(1,128)S(1)}, s32[2,1]{0,1:T(1,128)}, u32[]{:S(2)}) copy-start(s32[2,1]{0,1:T(1,128)} %param.8) | copy-start | bytes 28
  53.0 2.7 %collective-permute-start.7 = (bf16[4,2,32,2048]{3,2,1,0:T(8,128)(2,1)S(1)}, bf16[4,2,32,2048]{3,2,1,0:T(8,128)(2,1)S(1)}, u32[]{:S(2)}, u32[]{:S(2)}) collective-permute-start(bf16[4,2,32,2048]{3,2,1,0:T(8,128)(2,1)S(1)} %pad_maximum_fusion.own), channel_id=1, source_target_pairs={{0,64},{1,65},{2,66},{3,67},{4,68},{5,69},{6,70},{7,71},{8,72},{9,... | collective-permute-start | bytes 3145736 | tf_op jit(solution)/shard_map/ppermute | solution.py:32
  62.5 1.6 %copy-start = (bf16[2048,512]{1,0:T(8,128)(2,1)S(1)}, bf16[2048,512]{1,0:T(8,128)(2,1)}, u32[]{:S(2)}) copy-start(bf16[2048,512]{1,0:T(8,128)(2,1)} %all-gather.3.cloned.1.call-done.weight) | copy-start | bytes 6291460
  65.3 1.0 copy-start.3
  82.4 1.9 %collective-permute-start.8 = (bf16[16,32,512]{2,1,0:T(8,128)(2,1)S(1)}, bf16[16,32,512]{2,1,0:T(8,128)(2,1)S(1)}, u32[]{:S(2)}, u32[]{:S(2)}) collective-permute-start(bf16[16,32,512]{2,1,0:T(8,128)(2,1)S(1)} %all_to_all.21.own), channel_id=1, source_target_pairs={{0,64},{1,65},{2,66},{3,67},{4,68},{5,69},{6,70},{7,71},{8,72},{9,... | collective-permute-start | bytes 1572872 | tf_op jit(solution)/shard_map/ppermute | solution.py:32
  83.5 24.2 %copy-start.1 = (bf16[2048,512]{1,0:T(8,128)(2,1)S(1)}, bf16[2048,512]{1,0:T(8,128)(2,1)}, u32[]{:S(2)}) copy-start(bf16[2048,512]{1,0:T(8,128)(2,1)} %all-gather.3.cloned.1.call-done.weight) | copy-start | bytes 6291460
  90.4 2.0 %collective-permute-start.9 = (bf16[2,32,4096]{2,1,0:T(8,128)(2,1)S(1)}, bf16[2,32,4096]{2,1,0:T(8,128)(2,1)S(1)}, u32[]{:S(2)}, u32[]{:S(2)}) collective-permute-start(bf16[2,32,4096]{2,1,0:T(8,128)(2,1)S(1)} %get-tuple-element.20), channel_id=1, source_target_pairs={{0,64},{1,65},{2,66},{3,67},{4,68},{5,69},{6,70},{7,71},{8,72},{9,... | collective-permute-start | bytes 1572872 | tf_op jit(solution)/shard_map/ppermute | solution.py:32
  93.3 14.4 %all-to-all-start.2 = ((bf16[8,32,1024]{2,1,0:T(8,128)(2,1)}), bf16[8,32,1024]{2,1,0:T(8,128)(2,1)S(1)}, u32[]{:S(2)}, u32[]{:S(2)}) async-start(bf16[8,32,1024]{2,1,0:T(8,128)(2,1)} %shard_map.98), calls=%async_computation.2 | async-start | bytes 1048576 | tf_op jit(solution)/shard_map/all_to_all | solution.py:316
  107.6 1.6 %copy-start.2 = (bf16[2048,512]{1,0:T(8,128)(2,1)S(1)}, bf16[2048,512]{1,0:T(8,128)(2,1)}, u32[]{:S(2)}) copy-start(bf16[2048,512]{1,0:T(8,128)(2,1)} %all-gather.5.cloned.1.call-done.partner) | copy-start | bytes 6291460
  109.2 1.2 copy-start.4
  112.2 19.3 %copy-start.6 = (bf16[2,32,512]{2,1,0:T(8,128)(2,1)S(1)}, bf16[2,32,512]{2,1,0:T(8,128)(2,1)}, u32[]{:S(2)}) copy-start(bf16[2,32,512]{2,1,0:T(8,128)(2,1)} %param.7) | copy-start | bytes 196612
  112.2 2.2 %collective-permute-start.11 = (bf16[272,1024]{1,0:T(8,128)(2,1)S(1)}, bf16[272,1024]{1,0:T(8,128)(2,1)S(1)}, u32[]{:S(2)}, u32[]{:S(2)}) collective-permute-start(bf16[272,1024]{1,0:T(8,128)(2,1)S(1)} %get-tuple-element.25), channel_id=1, source_target_pairs={{0,64},{1,65},{2,66},{3,67},{4,68},{5,69},{6,70},{7,71},{8,72},{9,... | collective-permute-start | bytes 1671176 | tf_op jit(solution)/shard_map/ppermute | solution.py:32
  114.4 35.2 %copy-start.9 = (bf16[512]{0:T(512)(128)(2,1)S(1)}, bf16[512]{0:T(512)(128)(2,1)}, u32[]{:S(2)}) copy-start(bf16[512]{0:T(512)(128)(2,1)} %param.9) | copy-start | bytes 3076
  132.4 3.7 %collective-permute-start.12 = (f32[8,512]{1,0:T(8,128)S(1)}, f32[8,512]{1,0:T(8,128)S(1)}, u32[]{:S(2)}, u32[]{:S(2)}) collective-permute-start(f32[8,512]{1,0:T(8,128)S(1)} %get-tuple-element.28), channel_id=1, source_target_pairs={{0,4},{1,5},{2,6},{3,7},{4,0},{5,1},{6,2},{7,3},{8,12},{9,13},{10,... | collective-permute-start | bytes 49160 | tf_op jit(solution)/shard_map/ppermute | solution.py:32
  136.1 4.9 %collective-permute-start.13 = (f32[8,512]{1,0:T(8,128)S(1)}, f32[8,512]{1,0:T(8,128)S(1)}, u32[]{:S(2)}, u32[]{:S(2)}) collective-permute-start(f32[8,512]{1,0:T(8,128)S(1)} %add.25), channel_id=1, source_target_pairs={{0,8},{1,9},{2,10},{3,11},{4,12},{5,13},{6,14},{7,15},{8,16},{9,17... | collective-permute-start | bytes 49160 | tf_op jit(solution)/shard_map/ppermute | solution.py:32
  137.0 4.1 %collective-permute-start.14 = (f32[8,512]{1,0:T(8,128)S(1)}, f32[8,512]{1,0:T(8,128)S(1)}, u32[]{:S(2)}, u32[]{:S(2)}) collective-permute-start(f32[8,512]{1,0:T(8,128)S(1)} %add.25), channel_id=1, source_target_pairs={{0,56},{1,57},{2,58},{3,59},{4,60},{5,61},{6,62},{7,63},{8,0},{9,1... | collective-permute-start | bytes 49160 | tf_op jit(solution)/shard_map/ppermute | solution.py:32
  141.1 5.6 %collective-permute-start.15 = (f32[8,512]{1,0:T(8,128)S(1)}, f32[8,512]{1,0:T(8,128)S(1)}, u32[]{:S(2)}, u32[]{:S(2)}) collective-permute-start(f32[8,512]{1,0:T(8,128)S(1)} %get-tuple-element.29), channel_id=1, source_target_pairs={{0,40},{1,41},{2,42},{3,43},{4,44},{5,45},{6,46},{7,47},{8,48},{9,... | collective-permute-start | bytes 49160 | tf_op jit(solution)/shard_map/ppermute | solution.py:32
  143.0 6.0 %collective-permute-start.16 = (f32[8,512]{1,0:T(8,128)S(1)}, f32[8,512]{1,0:T(8,128)S(1)}, u32[]{:S(2)}, u32[]{:S(2)}) collective-permute-start(f32[8,512]{1,0:T(8,128)S(1)} %get-tuple-element.30), channel_id=1, source_target_pairs={{0,16},{1,17},{2,18},{3,19},{4,20},{5,21},{6,22},{7,23},{8,24},{9,... | collective-permute-start | bytes 49160 | tf_op jit(solution)/shard_map/ppermute | solution.py:32
Sparse Core Ops, SparseCore 0:
  19.6 42.7 all-gather.2
  64.3 40.1 all-gather.4

commit v2 on v1

v2 whole, which is shorter than its diff:
```python
import jax
import jax.numpy as jnp
import numpy as np
from jax import lax
from jax.experimental import pallas as pl
from jax.experimental.pallas import tpu as pltpu
from jax.sharding import Mesh
from jax.sharding import PartitionSpec as P

D = 2048
HEAD = 64
ENC = 32
ROWS = 32
LAYERS = 4
GROUPS = 8
EPSILON = 1e-06
AXES = ("xh", "core", "z", "xl", "y")
SIZES = (2, 2, 8, 2, 4)
NY = 4
BF, F32 = jnp.bfloat16, jnp.float32
MIB = 1 << 20


def shift(block, **moves):
    pairs = []
    for index in np.ndindex(*SIZES):
        to = list(index)
        for axis, by in moves.items():
            k = AXES.index(axis)
            to[k] = (index[k] + by) % SIZES[k] if axis in "yz" else index[k] ^ by
        pairs.append((int(np.ravel_multi_index(index, SIZES)), int(np.ravel_multi_index(to, SIZES))))
    return lax.ppermute(block, AXES, pairs)


def kernel_call(body, operands, outs, scratch=(), scalars=0, far=(), far_outs=(), aliases=None, limit=16):
    operands = [
        pltpu.with_memory_space_constraint(x, pltpu.HBM) if i in far else x for i, x in enumerate(operands)
    ]
    spaces = [pltpu.SMEM if i < scalars else pltpu.HBM if i in far else pltpu.VMEM for i in range(len(operands))]
    return pl.pallas_call(
        body,
        out_shape=[
            pltpu.HBM(s, d) if i in far_outs else jax.ShapeDtypeStruct(s, d) for i, (s, d) in enumerate(outs)
        ],
        in_specs=[pl.BlockSpec(memory_space=space) for space in spaces],
        out_specs=[pl.BlockSpec(memory_space=pltpu.HBM if i in far_outs else pltpu.VMEM) for i in range(len(outs))],
        scratch_shapes=[pltpu.VMEM(*x) if isinstance(x, tuple) else x for x in scratch],
        input_output_aliases=aliases or {},
        compiler_params=pltpu.CompilerParams(vmem_limit_bytes=limit * MIB),
    )(*operands)


def coordinates(*axes):
    return tuple(lax.axis_index(axis) for axis in axes)


def lanes(start, size):
    return pl.ds(pl.multiple_of(start, size), size)


RING = (0, -1, 1, -2, 2, -3, 3, -4, -4)


def pack_body(states, final_gain, query_gain, pack):
    pack[:64, :] = states[...]
    gains = [final_gain[...].astype(F32)]
    gains += [query_gain[:, i * 512 : (i + 1) * 512].astype(F32) for i in range(4)]
    gains += [jnp.zeros((11, 512), F32)]
    pack[64:, :] = jnp.concatenate(gains, axis=0).astype(BF)


def norm_body(p0, p1, p2, p3, ahead_in, behind_in, streams, upstreams,
              half, factor, query_gains, stream, upstream, ahead, behind, wide, final_gains, sems):
    xh, c = coordinates("xh", "core")
    mine = pl.ds(pl.multiple_of(c * ROWS, ROWS), ROWS)
    copies = [
        pltpu.make_async_copy(streams.at[xh, mine], stream, sems.at[0]),
        pltpu.make_async_copy(upstreams.at[xh, mine], upstream, sems.at[1]),
    ]
    for copy in copies:
        copy.start()
    section = xh * 2 + c
    for j, pack in enumerate((p0, p1, p2, p3)):
        peer = section ^ j
        wide[:, lanes(peer * 512, 512)] = pack[:64, :].astype(F32)
        gains = pack[64:, :].astype(F32)
        final_gains[:, lanes(peer * 512, 512)] = gains[0:1]
        for i in range(4):
            query_gains[peer, :, i * 512 : (i + 1) * 512] = gains[1 + i : 2 + i]
    states = wide[...]
    scale = lax.rsqrt(jnp.mean(states * states, axis=-1, keepdims=True) + EPSILON)
    factor[...] = jnp.broadcast_to(scale, (64, 128))
    wide[...] = states * scale * final_gains[...]
    half[...] = wide[lanes(c * 32, 32), :].astype(BF)
    for copy in copies:
        copy.wait()


def near_body(half, p1, p2, p3, across_in, ahead_in, behind_in, near, others, across, ahead, behind):
    near[0] = half[...]
    for k, part in enumerate((p1, p2, p3)):
        near[k + 1] = part[...]
        others[k] = part[...]


def group_body(near, across, beyond, ahead_in, behind_in, rows, upper, lower, ahead, behind):
    rows[0, 1] = across[...]
    for k in range(NY):
        rows[k, 0] = near[k]
        if k:
            rows[k, 1] = beyond[k - 1]
    upper[...] = ahead_in[:128]
    lower[...] = behind_in[128:]


def project_body(own, other, *refs):
    blocks, (out, held, weight_out, weight, result, sems) = refs[:9], refs[9:]
    c, z, xl, y = coordinates("core", "z", "xl", "y")
    copies = []
    for i, rows in enumerate((own, other)):
        for dy in range(NY):
            for dxl in range(2):
                place = held.at[(c + i) % 2, (xl + dxl) % 2 * 4 + (y + NY - dy) % NY]
                copies.append(pltpu.make_async_copy(rows.at[dy, dxl], place, sems.at[i * 8 + dy * 2 + dxl]))
                copies[-1].start()
    for k, block in enumerate(blocks):
        place = (z + 8 + RING[k]) % 8 * 256 + 128 * (k == 8)
        weight[pl.ds(pl.multiple_of(place, 128), block.shape[0]), :] = block[...]
    copies.append(pltpu.make_async_copy(weight, weight_out, sems.at[16]))
    copies[-1].start()
    for i, rows in enumerate((own, other)):
        result[...] = jnp.dot(rows[...].reshape(256, D), weight[...], preferred_element_type=F32).astype(BF)
        for dy in range(NY):
            for dxl in range(2):
                place = (c + i) % 2 * 8 + (xl + dxl) % 2 * 4 + (y + NY - dy) % NY
                row = (dy * 2 + dxl) * 32
                out[place] = result[row : row + 32, :]
    for copy in copies:
        copy.wait()


def decoder_body(lengths, own, other, stream_in, upstream, query_gains, keep, send, gain_parts,
                 pairs, streams, queries, softmax, incoming, gradients):
    xh, c = coordinates("xh", "core")
    for i in range(2):
        pairs[2 * i + c] = own[8 * i : 8 * i + 8]
        pairs[2 * i + 1 - c] = other[8 * i : 8 * i + 8]
    streams[0] = stream_in[...]
    incoming[...] = upstream[...].astype(F32)
    length = lengths[xh, 0]
    block = (lax.broadcasted_iota(jnp.int32, (128, 256), 0) // 32) == (
        lax.broadcasted_iota(jnp.int32, (128, 256), 1) // HEAD)
    block = jnp.where(block, 1.0, 0.0).astype(BF)
    lane = lax.broadcasted_iota(jnp.int32, (ROWS, 256), 1)
    visible = lax.broadcasted_iota(jnp.int32, (ENC, 1024), 0) < length
    scale = HEAD**-0.5
    def spread(part):
        return jnp.concatenate([part] * 4, axis=0) * block
    def fold(part):
        low = jnp.where(lane < 64, part[0:32], part[32:64])
        high = jnp.where(lane < 192, part[64:96], part[96:128])
        return jnp.where(lane < 128, low, high)
    def dot(a, b, dims):
        return lax.dot_general(a, b, (dims, ((), ())), preferred_element_type=F32)
    def col(g, base=0):
        return slice(base + g * 256, base + (g + 1) * 256)

    def lan(g):
        return slice(g * 128, (g + 1) * 128)

    def keys(layer, g):
        return pairs[layer, g // 2, :, col(g % 2)]

    def values(layer, g):
        return pairs[layer, 4 + g // 2, :, col(g % 2)]

    for layer in range(LAYERS):
        wide = streams[layer].astype(F32)
        factor = lax.rsqrt(jnp.mean(wide * wide, axis=-1, keepdims=True) + EPSILON)
        q = (wide * factor * query_gains[layer]).astype(BF)
        queries[layer] = q
        scores = jnp.concatenate([dot(keys(layer, g), spread(q[:, col(g)]), ((1,), (1,))) for g in range(GROUPS)], axis=1) * scale
        scores = jnp.where(visible, scores, -1e30)
        highest = jnp.max(scores, axis=0, keepdims=True)
        weights = jnp.where(visible, jnp.exp(scores - highest), 0.0)
        rows = weights / jnp.sum(weights, axis=0, keepdims=True)
        softmax[layer] = rows
        narrow = rows.astype(BF)
        ctx = [fold(dot(narrow[:, lan(g)], values(layer, g), ((0,), (0,)))) for g in range(GROUPS)]
        streams[layer + 1] = (wide + jnp.concatenate(ctx, axis=1)).astype(BF)
    for layer in reversed(range(LAYERS)):
        wide = streams[layer].astype(F32)
        factor = lax.rsqrt(jnp.mean(wide * wide, axis=-1, keepdims=True) + EPSILON)
        grad = incoming[...]
        narrow_grad = grad.astype(BF)
        rows = softmax[layer]
        narrow = rows.astype(BF)
        parts = []
        for g in range(GROUPS):
            heads = spread(narrow_grad[:, col(g)])
            parts.append(dot(values(layer, g), heads, ((1,), (1,))))
            gradients[layer, :, col(g, D)] = dot(narrow[:, lan(g)], heads, ((1,), (0,))).astype(BF)
        softmax_gradient = jnp.concatenate(parts, axis=1)
        ds = rows * (softmax_gradient - jnp.sum(rows * softmax_gradient, axis=0, keepdims=True))
        ds = ds.astype(BF)
        q = queries[layer]
        dq = []
        for g in range(GROUPS):
            dq.append(fold(dot(ds[:, lan(g)], keys(layer, g), ((0,), (0,)))))
            gradients[layer, :, col(g)] = (dot(ds[:, lan(g)], spread(q[:, col(g)]), ((1,), (0,))) * scale).astype(BF)
        gradient = jnp.concatenate(dq, axis=1) * scale
        scaled = gradient * query_gains[layer]
        mean = jnp.mean(scaled * wide, axis=-1, keepdims=True)
        incoming[...] = grad + factor * scaled - wide * (factor * factor * factor) * mean
        gain_parts[layer] = jnp.sum(gradient * wide * factor, axis=0, keepdims=True)
    for i in range(2):
        keep[i] = gradients[2 * i + c]
        send[i] = gradients[2 * i + 1 - c]


def join_body(keep, received, out):
    for xh in range(2):
        for k in range(8):
            span = slice(k * 512, (k + 1) * 512)
            total = keep[xh, :, span].astype(F32) + received[xh, :, span].astype(F32)
            out[xh * 8 + k] = total.astype(BF)


def high_low(part):
    high = part.astype(BF)
    return high, (part - high.astype(F32)).astype(BF)


def back_body(gradient, held_far, weight, gain_parts, keep, extra, send, terms, parts, rows, held, sem):
    (c,) = coordinates("core")
    copy = pltpu.make_async_copy(held_far, held, sem)
    copy.start()
    flat = gradient[...].reshape(512, 512)
    for q in range(4):
        span = slice(q * 512, (q + 1) * 512)
        terms[:, span] = lax.dot_general(flat, weight[span, :], (((1,), (1,)), ((), ())), preferred_element_type=F32)
    copy.wait()
    for m in range(2):
        for peer in range(8):
            place = (m * 8 + peer) * 32
            product = terms[place : place + 32, :] * held[m, peer].astype(F32)
            if place == 0:
                parts[...] = jnp.sum(product, axis=0, keepdims=True)
            else:
                parts[...] += jnp.sum(product, axis=0, keepdims=True)
            rows[place : place + 32, :] = jnp.broadcast_to(jnp.sum(product, axis=1, keepdims=True), (32, 128))
    row_sums = jnp.transpose(rows[...])[0:1, :]
    for parity, is_send in ((c, False), (1 - c, True)):
        extras = []
        for i in range(2):
            layer_gain = gain_parts[2 * i + parity]
            extras += [layer_gain[:, :1024], layer_gain[:, 1024:]]
        extras.append(
            jnp.concatenate([parts[:, lanes((2 * i + parity) * 512, 512)] for i in range(2)], axis=1)
        )
        extras.append(jnp.concatenate([row_sums, jnp.zeros((1, 512), F32)], axis=1))
        extras.append(jnp.zeros((2, 1024), F32))
        block = jnp.concatenate(extras, axis=0)
        for i in range(2):
            part = terms[:, lanes((2 * i + parity) * 512, 512)]
            if is_send:
                send[:512, i * 512 : (i + 1) * 512] = part.astype(BF)
            else:
                keep[:, i * 512 : (i + 1) * 512] = part
        if is_send:
            send[512:, :] = jnp.concatenate(high_low(block), axis=0)
        else:
            extra[...] = block


def merge_body(keep, extra, received, out):
    carried = received[512:, :].astype(F32)
    extras = extra[...] + carried[0:8] + carried[8:16]
    for xh in range(2):
        span = slice(xh * 512, (xh + 1) * 512)
        block = jnp.concatenate(
            [
                extras[2 * xh : 2 * xh + 1, :512],
                extras[2 * xh : 2 * xh + 1, 512:],
                extras[2 * xh + 1 : 2 * xh + 2, :512],
                extras[2 * xh + 1 : 2 * xh + 2, 512:],
                extras[4:5, span],
                extras[5:6, :512],
                jnp.zeros((2, 512), F32),
            ],
            axis=0,
        )
        block = jnp.concatenate(high_low(block), axis=0)
        for k in range(8):
            for m in range(2):
                place = (m * 8 + k) * 32
                part = keep[place : place + 32, span] + received[place : place + 32, span].astype(F32)
                out[xh * 8 + k, m * 32 : (m + 1) * 32, :] = part.astype(BF)
            out[xh * 8 + k, 64:, :] = block


def finish_body(received, states, factor, final_gain, gradient, sums, rows):
    xl, y = coordinates("xl", "y")
    total = received[0].astype(F32)
    for k in range(1, 16):
        total += received[k].astype(F32)
    extras = total[64:72] + total[72:80]
    sums[...] = extras
    rows[...] = jnp.transpose(jnp.broadcast_to(extras[5:6], (128, 512)))
    for m in range(2):
        span = slice(m * 32, (m + 1) * 32)
        row_sum = rows[lanes(m * 256 + (xl * 4 + y) * 32, 32), 0:1]
        scale = factor[span, 0:1]
        scaled = total[span] * final_gain[...].astype(F32)
        wide = states[span, :].astype(F32)
        gradient[span, :] = scale * scaled - wide * (scale * scale * (row_sum / D))


def close_body(first, second, third, final_gain, final_gradient, layers_gradient):
    total = first[...] + second[...] + third[...]
    for i in range(4):
        layers_gradient[:, i * 512 : (i + 1) * 512] = total[i : i + 1]
    final_gradient[...] = total[4:5] / final_gain[...].astype(F32)


def per_device(
    encoder_states, encoder_lengths, final_gain, decoder_states, query_gain, cross_weight, upstream
):
    block = lax.all_to_all(cross_weight[0], ("xl", "y"), 1, 0, tiled=True)
    states = encoder_states.reshape(64, 512)
    (pack,) = kernel_call(pack_body, (states, final_gain[None], query_gain), [((80, 512), BF)])
    packs = [pack, shift(pack, core=1), shift(pack, xh=1), shift(pack, xh=1, core=1)]
    tile = ((256, 512), BF)
    half, factor, query_gains, stream, incoming, ahead1, behind1 = kernel_call(
        norm_body,
        packs + [shift(block, z=1), shift(block, z=-1), decoder_states, upstream],
        [((32, D), BF), ((64, 128), F32), ((4, 1, D), F32), ((ROWS, D), BF), ((ROWS, D), BF), tile, tile],
        [((64, D), F32), ((1, D), F32), pltpu.SemaphoreType.DMA((2,))],
        far=(6, 7),
        aliases={4: 5, 5: 6},
    )
    near, others, across, ahead2, behind2 = kernel_call(
        near_body,
        [half] + [shift(half, y=dy) for dy in range(1, NY)]
        + [shift(half, xl=1), shift(ahead1, z=1), shift(behind1, z=-1)],
        [((NY, 32, D), BF), ((NY - 1, 32, D), BF), ((32, D), BF), tile, tile],
        aliases={4: 2, 5: 3, 6: 4},
    )
    own_rows, upper, lower, ahead3, behind3 = kernel_call(
        group_body,
        [near, across, shift(others, xl=1), shift(ahead2, z=1), shift(behind2, z=-1)],
        [((NY, 2, 32, D), BF), ((128, 512), BF), ((128, 512), BF), tile, tile],
        aliases={3: 3, 4: 4},
    )
    ring = [block, ahead1, behind1, ahead2, behind2, ahead3, behind3, shift(upper, z=1), shift(lower, z=-1)]
    projected, held, weight = kernel_call(
        project_body,
        [own_rows, shift(own_rows, core=1)] + ring,
        [((16, 32, 512), BF), ((2, 8, 32, D), BF), ((D, 512), BF)],
        [((D, 512), BF), ((256, 512), BF), pltpu.SemaphoreType.DMA((17,))],
        far_outs=(1, 2),
    )
    own_pairs = lax.all_to_all(projected, ("xh", "xl", "y"), 0, 0, tiled=True)
    other_pairs = shift(own_pairs, core=1)
    keep, send, gain_parts = kernel_call(
        decoder_body,
        (encoder_lengths, own_pairs, other_pairs, stream, incoming, query_gains),
        [((2, 32, 4096), BF), ((2, 32, 4096), BF), ((4, 1, D), F32)],
        [
            ((4, 8, 32, 512), BF),
            ((5, ROWS, D), BF),
            ((4, ROWS, D), BF),
            ((4, ENC, 1024), F32),
            ((ROWS, D), F32),
            ((4, 32, 4096), BF),
        ],
        scalars=1,
    )
    (joined,) = kernel_call(join_body, (keep, shift(send, core=1)), [((16, 32, 512), BF)])
    joined = lax.all_to_all(joined, ("xh", "xl", "y"), 0, 0, tiled=True)
    term_keep, extra, term_send = kernel_call(
        back_body,
        (joined, held, weight, gain_parts),
        [((512, 1024), F32), ((8, 1024), F32), ((528, 1024), BF)],
        [
            ((512, D), F32),
            ((1, D), F32),
            ((512, 128), F32),
            ((2, 8, 32, D), BF),
            pltpu.SemaphoreType.DMA,
        ],
        far=(1,),
    )
    (merged,) = kernel_call(
        merge_body, (term_keep, extra, shift(term_send, core=1)), [((16, 80, 512), BF)]
    )
    merged = lax.all_to_all(merged, ("xh", "xl", "y"), 0, 0, tiled=True)
    gradient, sums = kernel_call(
        finish_body,
        (merged, states, factor, final_gain[None]),
        [((64, 512), F32), ((8, 512), F32)],
        [((512, 128), F32)],
    )
    ahead = shift(sums, z=1)
    pair = sums + ahead
    triple = pair + shift(sums, z=-1)
    final_gradient, layers_gradient = kernel_call(
        close_body,
        (triple, shift(triple, z=-3), shift(pair, z=2), final_gain[None]),
        [((1, 512), F32), ((1, D), F32)],
    )
    return (gradient.reshape(2, 32, 512), final_gradient[0], layers_gradient)


def solution(mesh):
    dp, section = ("z", "xl", "y"), ("xh", "core")
    return jax.shard_map(
        per_device,
        mesh=Mesh(mesh.devices.reshape(SIZES), AXES),
        in_specs=(
            P(None, dp, section),
            P(None, dp),
            P(section),
            P(None, dp, None),
            P(section, None),
            P(section, dp, None),
            P(None, dp, None),
        ),
        out_specs=(P(None, dp, section), P(section), P(section, None)),
        check_vma=False,
    )
```

time: 158 us -> 148 us (0.937)
  blocking collectives: 44.2 us -> 66.3 us
  waiting for transfers between devices: 51.9 us -> 33 us
  between operations: 14.2 us -> 0.8 us
  local copies, waits for them, and re-layouts: 11.1 us -> 1.26 us
  starting transfers between devices: 23.8 us -> 32.1 us
  Pallas kernels: 11.1 us -> 14.4 us
    all_to_all x2 -> x3, blocking collectives: 28.1 us -> 49.4 us  [the longest x1 23.1 us: per_device(): merged = lax.all_to_all(merged, ('xh', 'xl', 'y'), 0, 0, tiled=True)]
    ppermute x17 -> x24, starting transfers between devices: 18.8 us -> 32.1 us  [shift(): return lax.ppermute(block, AXES, pairs)]
    all_gather x2 -> x0, waiting for transfers between devices: 13.1 us -> none  [the longest x1 6.75 us: per_device(): weight = lax.all_gather(block, 'z', axis=0, tiled=True)]
    unnamed x26 -> x12, local copies, waits for them, and re-layouts: 9.38 us -> 1.18 us
    all_to_all x1 -> x0, starting transfers between devices: 4.86 us -> none  [per_device(): joined = lax.all_to_all(joined, ('xh', 'y'), 0, 0, tiled=True)]
    pallas_call x8 -> x11, Pallas kernels: 11.1 us -> 14.4 us  [kernel_call(): pl.pallas_call(body, out_shape=[pltpu.HBM(s, d) if i in far_outs else jax...]
    all_to_all x1 -> x0, waiting for transfers between devices: 3.22 us -> none  [per_device(): joined = lax.all_to_all(joined, ('xh', 'y'), 0, 0, tiled=True)]
    ppermute x17 -> x24, waiting for transfers between devices: 35.6 us -> 33 us  [shift(): return lax.ppermute(block, AXES, pairs)]
  transfers between devices with their start and end apart: 20 -> 24, of which waited for: 16 -> 14; matrix products, arithmetic and copies ran while one was open for 1% -> 0% of each run, Pallas kernels for 5% -> 0%
where the time goes in v2:
time: 148 us
  blocking collectives  66.3 us (45%)
  waiting for transfers between devices  33 us (22%)
  starting transfers between devices  32.1 us (22%)
  Pallas kernels  14.4 us (10%)
    ppermute x24, waiting for transfers between devices, shift(): return lax.ppermute(block, AXES, pairs)  33 us
    ppermute x24, starting transfers between devices, shift(): return lax.ppermute(block, AXES, pairs)  32.1 us
    all_to_all x1, blocking collectives, per_device(): merged = lax.all_to_all(merged, ('xh', 'xl', 'y'), 0, 0, tiled=True)  23.1 us
    all_to_all x1, blocking collectives, per_device(): own_pairs = lax.all_to_all(projected, ('xh', 'xl', 'y'), 0, 0, tiled=True)  16.8 us
    all_to_all x1, blocking collectives, per_device(): joined = lax.all_to_all(joined, ('xh', 'xl', 'y'), 0, 0, tiled=True)  15.3 us
    pallas_call x11, Pallas kernels, kernel_call(): pl.pallas_call(body, out_shape=[pltpu.HBM(s, d) if i in far_outs else jax...  14.4 us
    all_to_all x1, blocking collectives, per_device(): block = lax.all_to_all(cross_weight[0], ('xl', 'y'), 1, 0, tiled=True)  11.1 us
  transfers between devices with their start and end apart: 24, of which 14 were waited for; matrix products, arithmetic and copies ran while one was open for 0% of the time, Pallas kernels for 0%

profile of v2, /device:TPU:8, one launch (start us, length us, event | category | flops | bytes accessed | tf_op | source)
XLA Modules:
  0.0 147.8 jit_solution(3169306982422529629)
XLA Ops:
  0.7 1.1 copy.19
  1.8 11.1 %all_to_all.34 = bf16[32,8,512]{2,0,1:T(8,128)(2,1)S(1)} all-to-all(bf16[32,8,512]{2,0,1:T(8,128)(2,1)S(1)} %copy.17), channel_id=1, replica_groups=mesh['xh'=2,'core'=2,'z'=8,'xl'=2,'y'=4] {'xl','y'}, dimensions={1} | all-to-all | bytes 524288 | tf_op jit(solution)/shard_map/all_to_all | solution.py:329
  12.9 1.9 %collective-permute-start.3 = (bf16[256,512]{1,0:T(8,128)(2,1)S(1)}, bf16[256,512]{1,0:T(8,128)(2,1)S(1)}, u32[]{:S(2)}, u32[]{:S(2)}) collective-permute-start(bf16[256,512]{1,0:T(8,128)(2,1)S(1)} %bitcast.9), channel_id=1, source_target_pairs={{0,8},{1,9},{2,10},{3,11},{4,12},{5,13},{6,14},{7,15},{8,16},{9,17... | collective-permute-start | bytes 786440 | tf_op jit(solution)/shard_map/ppermute | solution.py:32
  14.8 3.9 %collective-permute-start.4 = (bf16[256,512]{1,0:T(8,128)(2,1)S(1)}, bf16[256,512]{1,0:T(8,128)(2,1)S(1)}, u32[]{:S(2)}, u32[]{:S(2)}) collective-permute-start(bf16[256,512]{1,0:T(8,128)(2,1)S(1)} %bitcast.10), channel_id=1, source_target_pairs={{0,56},{1,57},{2,58},{3,59},{4,60},{5,61},{6,62},{7,63},{8,0},{9,1... | collective-permute-start | bytes 786440 | tf_op jit(solution)/shard_map/ppermute | solution.py:32
  18.8 0.1 collective-permute-start
  18.9 2.8 %collective-permute-start.1 = (bf16[80,512]{1,0:T(8,128)(2,1)S(1)}, bf16[80,512]{1,0:T(8,128)(2,1)S(1)}, u32[]{:S(2)}, u32[]{:S(2)}) collective-permute-start(bf16[80,512]{1,0:T(8,128)(2,1)S(1)} %shard_map.94.p0), channel_id=1, source_target_pairs={{0,128},{1,129},{2,130},{3,131},{4,132},{5,133},{6,134},{7,135},{8... | collective-permute-start | bytes 245768 | tf_op jit(solution)/shard_map/ppermute | solution.py:32
  21.7 0.6 collective-permute-start.2
  22.3 3.0 %collective-permute-done.1.p2 = bf16[80,512]{1,0:T(8,128)(2,1)S(1)} collective-permute-done((bf16[80,512]{1,0:T(8,128)(2,1)S(1)}, bf16[80,512]{1,0:T(8,128)(2,1)S(1)}, u32[]{:S(2)}, u32[]{:S(2)}) %collective-permute-start.1) | collective-permute-done | bytes 81952 | tf_op jit(solution)/shard_map/ppermute | solution.py:32
  25.3 2.4 %collective-permute-done.2.p3 = bf16[80,512]{1,0:T(8,128)(2,1)S(1)} collective-permute-done((bf16[80,512]{1,0:T(8,128)(2,1)S(1)}, bf16[80,512]{1,0:T(8,128)(2,1)S(1)}, u32[]{:S(2)}, u32[]{:S(2)}) %collective-permute-start.2) | collective-permute-done | bytes 81952 | tf_op jit(solution)/shard_map/ppermute | solution.py:32
  27.6 1.1 shard_map.95
  28.7 0.7 collective-permute-start.5
  29.4 2.0 %collective-permute-start.10 = (bf16[256,512]{1,0:T(8,128)(2,1)S(1)}, bf16[256,512]{1,0:T(8,128)(2,1)S(1)}, u32[]{:S(2)}, u32[]{:S(2)}) collective-permute-start(bf16[256,512]{1,0:T(8,128)(2,1)S(1)} %get-tuple-element.35.refs_2_), channel_id=1, source_target_pairs={{0,56},{1,57},{2,58},{3,59},{4,60},{5,61},{6,62},{7,63},{8,0},{9,1... | collective-permute-start | bytes 786440 | tf_op jit(solution)/shard_map/ppermute | solution.py:32
  31.5 3.2 %collective-permute-start.6 = (bf16[32,2048]{1,0:T(8,128)(2,1)S(1)}, bf16[32,2048]{1,0:T(8,128)(2,1)S(1)}, u32[]{:S(2)}, u32[]{:S(2)}) collective-permute-start(bf16[32,2048]{1,0:T(8,128)(2,1)S(1)} %get-tuple-element.33.half), channel_id=1, source_target_pairs={{0,2},{1,3},{2,0},{3,1},{4,6},{5,7},{6,4},{7,5},{8,10},{9,11},{10,... | collective-permute-start | bytes 393224 | tf_op jit(solution)/shard_map/ppermute | solution.py:32
  34.7 0.2 collective-permute-start.7
  34.9 0.7 collective-permute-start.8
  35.6 3.9 %collective-permute-done.6.p2 = bf16[32,2048]{1,0:T(8,128)(2,1)S(1)} collective-permute-done((bf16[32,2048]{1,0:T(8,128)(2,1)S(1)}, bf16[32,2048]{1,0:T(8,128)(2,1)S(1)}, u32[]{:S(2)}, u32[]{:S(2)}) %collective-permute-start.6) | collective-permute-done | bytes 131104 | tf_op jit(solution)/shard_map/ppermute | solution.py:32
  39.5 1.3 collective-permute-done.7.p3
  40.9 0.4 collective-permute-start.11
  41.3 3.2 %collective-permute-start.13 = (bf16[256,512]{1,0:T(8,128)(2,1)S(1)}, bf16[256,512]{1,0:T(8,128)(2,1)S(1)}, u32[]{:S(2)}, u32[]{:S(2)}) collective-permute-start(bf16[256,512]{1,0:T(8,128)(2,1)S(1)} %get-tuple-element.40.refs_4_), channel_id=1, source_target_pairs={{0,56},{1,57},{2,58},{3,59},{4,60},{5,61},{6,62},{7,63},{8,0},{9,1... | collective-permute-start | bytes 786440 | tf_op jit(solution)/shard_map/ppermute | solution.py:32
  44.6 5.4 %collective-permute-done.12.ahead_in = bf16[256,512]{1,0:T(8,128)(2,1)S(1)} collective-permute-done((bf16[256,512]{1,0:T(8,128)(2,1)S(1)}, bf16[256,512]{1,0:T(8,128)(2,1)S(1)}, u32[]{:S(2)}, u32[]{:S(2)}) %collective-permute-start.12) | collective-permute-done | bytes 262176 | tf_op jit(solution)/shard_map/ppermute | solution.py:32
  49.9 1.3 collective-permute-done.11.beyond
  51.3 0.1 collective-permute-start.14
  51.5 3.2 %collective-permute-start.16 = (bf16[128,512]{1,0:T(8,128)(2,1)S(1)}, bf16[128,512]{1,0:T(8,128)(2,1)S(1)}, u32[]{:S(2)}, u32[]{:S(2)}) collective-permute-start(bf16[128,512]{1,0:T(8,128)(2,1)S(1)} %get-tuple-element.45), channel_id=1, source_target_pairs={{0,56},{1,57},{2,58},{3,59},{4,60},{5,61},{6,62},{7,63},{8,0},{9,1... | collective-permute-start | bytes 393224 | tf_op jit(solution)/shard_map/ppermute | solution.py:32
  54.7 3.8 %collective-permute-done.15.refs_7_ = bf16[128,512]{1,0:T(8,128)(2,1)S(1)} collective-permute-done((bf16[128,512]{1,0:T(8,128)(2,1)S(1)}, bf16[128,512]{1,0:T(8,128)(2,1)S(1)}, u32[]{:S(2)}, u32[]{:S(2)}) %collective-permute-start.15) | collective-permute-done | bytes 131104 | tf_op jit(solution)/shard_map/ppermute | solution.py:32
  58.5 3.1 %shard_map.98 = (bf16[16,32,512]{2,1,0:T(8,128)(2,1)S(1)}, bf16[2,8,32,2048]{3,2,1,0:T(8,128)(2,1)}, bf16[2048,512]{1,0:T(8,128)(2,1)}) custom-call(bf16[4,2,32,2048]{3,2,1,0:T(8,128)(2,1)S(1)} %get-tuple-element.41.own, bf16[4,2,32,2048]{3,2,1,0:T(8,128)(2,1)S(1)} %collective-permute-done.14.other, bf16[256,512]{1,0:T(8,128)(2,1)S(1)} %bitcast.11, ...), custom_call_target="tpu_custom_call" | custom-call | tf_op jit(solution)/shard_map/pallas_call | solution.py:40
  61.6 16.8 %all_to_all.35.own = bf16[16,32,512]{2,1,0:T(8,128)(2,1)S(1)} all-to-all(bf16[16,32,512]{2,1,0:T(8,128)(2,1)S(1)} %get-tuple-element.46), channel_id=1, replica_groups=mesh['xh'=2,'core'=2,'z'=8,'xl'=2,'y'=4] {'xh','xl','y'}, dimensions={0} | all-to-all | bytes 1048576 | tf_op jit(solution)/shard_map/all_to_all | solution.py:363
  78.4 0.1 copy.18.lengths
  78.5 1.8 %collective-permute-done.17.other = bf16[16,32,512]{2,1,0:T(8,128)(2,1)S(1)} collective-permute-done((bf16[16,32,512]{2,1,0:T(8,128)(2,1)S(1)}, bf16[16,32,512]{2,1,0:T(8,128)(2,1)S(1)}, u32[]{:S(2)}, u32[]{:S(2)}) %collective-permute-start.17) | collective-permute-done | bytes 524320 | tf_op jit(solution)/shard_map/ppermute | solution.py:32
  80.3 5.6 %shard_map.99 = (bf16[2,32,4096]{2,1,0:T(8,128)(2,1)S(1)}, bf16[2,32,4096]{2,1,0:T(8,128)(2,1)S(1)}, f32[4,1,2048]{2,1,0:T(1,128)S(1)}) custom-call(s32[2,1]{1,0:T(2,128)S(1)} %copy.18.lengths, bf16[16,32,512]{2,1,0:T(8,128)(2,1)S(1)} %all_to_all.35.own, bf16[16,32,512]{2,1,0:T(8,128)(2,1)S(1)} %collective-permute-done.17.other, ...), custom_call_target="tpu_custom_call" | custom-call | tf_op jit(solution)/shard_map/pallas_call | solution.py:40
  85.9 0.3 collective-permute-start.18
  86.2 1.7 %collective-permute-done.18.received = bf16[2,32,4096]{2,1,0:T(8,128)(2,1)S(1)} collective-permute-done((bf16[2,32,4096]{2,1,0:T(8,128)(2,1)S(1)}, bf16[2,32,4096]{2,1,0:T(8,128)(2,1)S(1)}, u32[]{:S(2)}, u32[]{:S(2)}) %collective-permute-start.18) | collective-permute-done | bytes 524320 | tf_op jit(solution)/shard_map/ppermute | solution.py:32
  87.9 0.1 shard_map.100
  88.0 15.3 %all_to_all.36.gradient = bf16[16,32,512]{2,1,0:T(8,128)(2,1)S(1)} all-to-all(bf16[16,32,512]{2,1,0:T(8,128)(2,1)S(1)} %shard_map.100), channel_id=1, replica_groups=mesh['xh'=2,'core'=2,'z'=8,'xl'=2,'y'=4] {'xh','xl','y'}, dimensions={0} | all-to-all | bytes 1048576 | tf_op jit(solution)/shard_map/all_to_all | solution.py:380
  103.3 2.7 %shard_map.101 = (f32[512,1024]{1,0:T(8,128)S(1)}, f32[8,1024]{1,0:T(8,128)S(1)}, bf16[528,1024]{1,0:T(8,128)(2,1)S(1)}) custom-call(bf16[16,32,512]{2,1,0:T(8,128)(2,1)S(1)} %all_to_all.36.gradient, bf16[2,8,32,2048]{3,2,1,0:T(8,128)(2,1)} %get-tuple-element.52.held_far, bf16[2048,512]{1,0:T(8,128)(2,1)S(1)} %copy-done, ...), custom_call_target="tpu_custom_call" | custom-call | tf_op jit(solution)/shard_map/pallas_call | solution.py:40
  106.0 0.1 collective-permute-start.19
  106.1 2.7 %collective-permute-done.19.received = bf16[528,1024]{1,0:T(8,128)(2,1)S(1)} collective-permute-done((bf16[528,1024]{1,0:T(8,128)(2,1)S(1)}, bf16[528,1024]{1,0:T(8,128)(2,1)S(1)}, u32[]{:S(2)}, u32[]{:S(2)}) %collective-permute-start.19) | collective-permute-done | bytes 1081376 | tf_op jit(solution)/shard_map/ppermute | solution.py:32
  108.8 0.2 shard_map.102
  109.0 23.1 %all_to_all.37.received = bf16[16,80,512]{2,1,0:T(8,128)(2,1)S(1)} all-to-all(bf16[16,80,512]{2,1,0:T(8,128)(2,1)S(1)} %shard_map.102), channel_id=1, replica_groups=mesh['xh'=2,'core'=2,'z'=8,'xl'=2,'y'=4] {'xh','xl','y'}, dimensions={0} | all-to-all | bytes 2621440 | tf_op jit(solution)/shard_map/all_to_all | solution.py:397
  132.1 0.9 shard_map.103
  133.0 1.6 %collective-permute-start.20 = (f32[8,512]{1,0:T(8,128)S(1)}, f32[8,512]{1,0:T(8,128)S(1)}, u32[]{:S(2)}, u32[]{:S(2)}) collective-permute-start(f32[8,512]{1,0:T(8,128)S(1)} %get-tuple-element.60), channel_id=1, source_target_pairs={{0,8},{1,9},{2,10},{3,11},{4,12},{5,13},{6,14},{7,15},{8,16},{9,17... | collective-permute-start | bytes 49160 | tf_op jit(solution)/shard_map/ppermute | solution.py:32
  134.6 1.7 %collective-permute-start.21 = (f32[8,512]{1,0:T(8,128)S(1)}, f32[8,512]{1,0:T(8,128)S(1)}, u32[]{:S(2)}, u32[]{:S(2)}) collective-permute-start(f32[8,512]{1,0:T(8,128)S(1)} %get-tuple-element.60), channel_id=1, source_target_pairs={{0,56},{1,57},{2,58},{3,59},{4,60},{5,61},{6,62},{7,63},{8,0},{9,1... | collective-permute-start | bytes 49160 | tf_op jit(solution)/shard_map/ppermute | solution.py:32
  136.3 1.7 %collective-permute-done.20 = f32[8,512]{1,0:T(8,128)S(1)} collective-permute-done((f32[8,512]{1,0:T(8,128)S(1)}, f32[8,512]{1,0:T(8,128)S(1)}, u32[]{:S(2)}, u32[]{:S(2)}) %collective-permute-start.20) | collective-permute-done | bytes 16416 | tf_op jit(solution)/shard_map/ppermute | solution.py:32
  138.0 0.4 collective-permute-done.21
  138.3 2.4 %collective-permute-start.22 = (f32[8,512]{1,0:T(8,128)S(1)}, f32[8,512]{1,0:T(8,128)S(1)}, u32[]{:S(2)}, u32[]{:S(2)}) collective-permute-start(f32[8,512]{1,0:T(8,128)S(1)} %get-tuple-element.63.first), channel_id=1, source_target_pairs={{0,40},{1,41},{2,42},{3,43},{4,44},{5,45},{6,46},{7,47},{8,48},{9,... | collective-permute-start | bytes 49160 | tf_op jit(solution)/shard_map/ppermute | solution.py:32
  140.7 2.8 %collective-permute-start.23 = (f32[8,512]{1,0:T(8,128)S(1)}, f32[8,512]{1,0:T(8,128)S(1)}, u32[]{:S(2)}, u32[]{:S(2)}) collective-permute-start(f32[8,512]{1,0:T(8,128)S(1)} %get-tuple-element.64), channel_id=1, source_target_pairs={{0,16},{1,17},{2,18},{3,19},{4,20},{5,21},{6,22},{7,23},{8,24},{9,... | collective-permute-start | bytes 49160 | tf_op jit(solution)/shard_map/ppermute | solution.py:32
  143.6 1.1 collective-permute-done.22.second
  144.7 2.5 %collective-permute-done.23.third = f32[8,512]{1,0:T(8,128)S(1)} collective-permute-done((f32[8,512]{1,0:T(8,128)S(1)}, f32[8,512]{1,0:T(8,128)S(1)}, u32[]{:S(2)}, u32[]{:S(2)}) %collective-permute-start.23) | collective-permute-done | bytes 16416 | tf_op jit(solution)/shard_map/ppermute | solution.py:32
  147.2 0.6 shard_map.104
  (30 shorter events, 0.4 us)
Async XLA Ops:
  0.6 18.1 %copy-start.3 = (bf16[512]{0:T(512)(128)(2,1)S(1)}, bf16[512]{0:T(512)(128)(2,1)}, u32[]{:S(2)}) copy-start(bf16[512]{0:T(512)(128)(2,1)} %param.9) | copy-start | bytes 3076
  0.6 18.1 %copy-start.1 = (bf16[2,32,512]{2,1,0:T(8,128)(2,1)S(1)}, bf16[2,32,512]{2,1,0:T(8,128)(2,1)}, u32[]{:S(2)}) copy-start(bf16[2,32,512]{2,1,0:T(8,128)(2,1)} %param.7) | copy-start | bytes 196612
  0.7 18.1 %copy-start.2 = (bf16[1,2048]{1,0:T(2,128)(2,1)S(1)}, bf16[1,2048]{1,0:T(2,128)(2,1)}, u32[]{:S(2)}) copy-start(bf16[1,2048]{1,0:T(2,128)(2,1)} %query_gain.1) | copy-start | bytes 12292
  12.9 14.7 %collective-permute-start.3 = (bf16[256,512]{1,0:T(8,128)(2,1)S(1)}, bf16[256,512]{1,0:T(8,128)(2,1)S(1)}, u32[]{:S(2)}, u32[]{:S(2)}) collective-permute-start(bf16[256,512]{1,0:T(8,128)(2,1)S(1)} %bitcast.9), channel_id=1, source_target_pairs={{0,8},{1,9},{2,10},{3,11},{4,12},{5,13},{6,14},{7,15},{8,16},{9,17... | collective-permute-start | bytes 786440 | tf_op jit(solution)/shard_map/ppermute | solution.py:32
  14.8 12.8 %collective-permute-start.4 = (bf16[256,512]{1,0:T(8,128)(2,1)S(1)}, bf16[256,512]{1,0:T(8,128)(2,1)S(1)}, u32[]{:S(2)}, u32[]{:S(2)}) collective-permute-start(bf16[256,512]{1,0:T(8,128)(2,1)S(1)} %bitcast.10), channel_id=1, source_target_pairs={{0,56},{1,57},{2,58},{3,59},{4,60},{5,61},{6,62},{7,63},{8,0},{9,1... | collective-permute-start | bytes 786440 | tf_op jit(solution)/shard_map/ppermute | solution.py:32
  18.8 3.5 %collective-permute-start = (bf16[80,512]{1,0:T(8,128)(2,1)S(1)}, bf16[80,512]{1,0:T(8,128)(2,1)S(1)}, u32[]{:S(2)}, u32[]{:S(2)}) collective-permute-start(bf16[80,512]{1,0:T(8,128)(2,1)S(1)} %shard_map.94.p0), channel_id=1, source_target_pairs={{0,64},{1,65},{2,66},{3,67},{4,68},{5,69},{6,70},{7,71},{8,72},{9,... | collective-permute-start | bytes 245768 | tf_op jit(solution)/shard_map/ppermute | solution.py:32
  18.9 6.4 %collective-permute-start.1 = (bf16[80,512]{1,0:T(8,128)(2,1)S(1)}, bf16[80,512]{1,0:T(8,128)(2,1)S(1)}, u32[]{:S(2)}, u32[]{:S(2)}) collective-permute-start(bf16[80,512]{1,0:T(8,128)(2,1)S(1)} %shard_map.94.p0), channel_id=1, source_target_pairs={{0,128},{1,129},{2,130},{3,131},{4,132},{5,133},{6,134},{7,135},{8... | collective-permute-start | bytes 245768 | tf_op jit(solution)/shard_map/ppermute | solution.py:32
  21.7 5.9 %collective-permute-start.2 = (bf16[80,512]{1,0:T(8,128)(2,1)S(1)}, bf16[80,512]{1,0:T(8,128)(2,1)S(1)}, u32[]{:S(2)}, u32[]{:S(2)}) collective-permute-start(bf16[80,512]{1,0:T(8,128)(2,1)S(1)} %shard_map.94.p0), channel_id=1, source_target_pairs={{0,192},{1,193},{2,194},{3,195},{4,196},{5,197},{6,198},{7,199},{8... | collective-permute-start | bytes 245768 | tf_op jit(solution)/shard_map/ppermute | solution.py:32
  28.7 6.2 %collective-permute-start.5 = (bf16[32,2048]{1,0:T(8,128)(2,1)S(1)}, bf16[32,2048]{1,0:T(8,128)(2,1)S(1)}, u32[]{:S(2)}, u32[]{:S(2)}) collective-permute-start(bf16[32,2048]{1,0:T(8,128)(2,1)S(1)} %get-tuple-element.33.half), channel_id=1, source_target_pairs={{0,1},{1,2},{2,3},{3,0},{4,5},{5,6},{6,7},{7,4},{8,9},{9,10},{10,1... | collective-permute-start | bytes 393224 | tf_op jit(solution)/shard_map/ppermute | solution.py:32
  29.4 11.4 %collective-permute-start.10 = (bf16[256,512]{1,0:T(8,128)(2,1)S(1)}, bf16[256,512]{1,0:T(8,128)(2,1)S(1)}, u32[]{:S(2)}, u32[]{:S(2)}) collective-permute-start(bf16[256,512]{1,0:T(8,128)(2,1)S(1)} %get-tuple-element.35.refs_2_), channel_id=1, source_target_pairs={{0,56},{1,57},{2,58},{3,59},{4,60},{5,61},{6,62},{7,63},{8,0},{9,1... | collective-permute-start | bytes 786440 | tf_op jit(solution)/shard_map/ppermute | solution.py:32
  31.5 9.4 %collective-permute-start.9 = (bf16[256,512]{1,0:T(8,128)(2,1)S(1)}, bf16[256,512]{1,0:T(8,128)(2,1)S(1)}, u32[]{:S(2)}, u32[]{:S(2)}) collective-permute-start(bf16[256,512]{1,0:T(8,128)(2,1)S(1)} %get-tuple-element.34.refs_1_), channel_id=1, source_target_pairs={{0,8},{1,9},{2,10},{3,11},{4,12},{5,13},{6,14},{7,15},{8,16},{9,17... | collective-permute-start | bytes 786440 | tf_op jit(solution)/shard_map/ppermute | solution.py:32
  31.5 8.0 %collective-permute-start.6 = (bf16[32,2048]{1,0:T(8,128)(2,1)S(1)}, bf16[32,2048]{1,0:T(8,128)(2,1)S(1)}, u32[]{:S(2)}, u32[]{:S(2)}) collective-permute-start(bf16[32,2048]{1,0:T(8,128)(2,1)S(1)} %get-tuple-element.33.half), channel_id=1, source_target_pairs={{0,2},{1,3},{2,0},{3,1},{4,6},{5,7},{6,4},{7,5},{8,10},{9,11},{10,... | collective-permute-start | bytes 393224 | tf_op jit(solution)/shard_map/ppermute | solution.py:32
  34.7 6.1 %collective-permute-start.7 = (bf16[32,2048]{1,0:T(8,128)(2,1)S(1)}, bf16[32,2048]{1,0:T(8,128)(2,1)S(1)}, u32[]{:S(2)}, u32[]{:S(2)}) collective-permute-start(bf16[32,2048]{1,0:T(8,128)(2,1)S(1)} %get-tuple-element.33.half), channel_id=1, source_target_pairs={{0,3},{1,0},{2,1},{3,2},{4,7},{5,4},{6,5},{7,6},{8,11},{9,8},{10,9... | collective-permute-start | bytes 393224 | tf_op jit(solution)/shard_map/ppermute | solution.py:32
  34.9 5.9 %collective-permute-start.8 = (bf16[32,2048]{1,0:T(8,128)(2,1)S(1)}, bf16[32,2048]{1,0:T(8,128)(2,1)S(1)}, u32[]{:S(2)}, u32[]{:S(2)}) collective-permute-start(bf16[32,2048]{1,0:T(8,128)(2,1)S(1)} %get-tuple-element.33.half), channel_id=1, source_target_pairs={{0,4},{1,5},{2,6},{3,7},{4,0},{5,1},{6,2},{7,3},{8,12},{9,13},{10,... | collective-permute-start | bytes 393224 | tf_op jit(solution)/shard_map/ppermute | solution.py:32
  40.9 10.3 %collective-permute-start.11 = (bf16[3,32,2048]{2,1,0:T(8,128)(2,1)S(1)}, bf16[3,32,2048]{2,1,0:T(8,128)(2,1)S(1)}, u32[]{:S(2)}, u32[]{:S(2)}) collective-permute-start(bf16[3,32,2048]{2,1,0:T(8,128)(2,1)S(1)} %get-tuple-element.38), channel_id=1, source_target_pairs={{0,4},{1,5},{2,6},{3,7},{4,0},{5,1},{6,2},{7,3},{8,12},{9,13},{10,... | collective-permute-start | bytes 1179656 | tf_op jit(solution)/shard_map/ppermute | solution.py:32
  41.3 8.6 %collective-permute-start.12 = (bf16[256,512]{1,0:T(8,128)(2,1)S(1)}, bf16[256,512]{1,0:T(8,128)(2,1)S(1)}, u32[]{:S(2)}, u32[]{:S(2)}) collective-permute-start(bf16[256,512]{1,0:T(8,128)(2,1)S(1)} %get-tuple-element.39.refs_3_), channel_id=1, source_target_pairs={{0,8},{1,9},{2,10},{3,11},{4,12},{5,13},{6,14},{7,15},{8,16},{9,17... | collective-permute-start | bytes 786440 | tf_op jit(solution)/shard_map/ppermute | solution.py:32
  41.3 8.6 %collective-permute-start.13 = (bf16[256,512]{1,0:T(8,128)(2,1)S(1)}, bf16[256,512]{1,0:T(8,128)(2,1)S(1)}, u32[]{:S(2)}, u32[]{:S(2)}) collective-permute-start(bf16[256,512]{1,0:T(8,128)(2,1)S(1)} %get-tuple-element.40.refs_4_), channel_id=1, source_target_pairs={{0,56},{1,57},{2,58},{3,59},{4,60},{5,61},{6,62},{7,63},{8,0},{9,1... | collective-permute-start | bytes 786440 | tf_op jit(solution)/shard_map/ppermute | solution.py:32
  51.3 7.2 %collective-permute-start.14 = (bf16[4,2,32,2048]{3,2,1,0:T(8,128)(2,1)S(1)}, bf16[4,2,32,2048]{3,2,1,0:T(8,128)(2,1)S(1)}, u32[]{:S(2)}, u32[]{:S(2)}) collective-permute-start(bf16[4,2,32,2048]{3,2,1,0:T(8,128)(2,1)S(1)} %get-tuple-element.41.own), channel_id=1, source_target_pairs={{0,64},{1,65},{2,66},{3,67},{4,68},{5,69},{6,70},{7,71},{8,72},{9,... | collective-permute-start | bytes 3145736 | tf_op jit(solution)/shard_map/ppermute | solution.py:32
  51.4 7.1 %collective-permute-start.15 = (bf16[128,512]{1,0:T(8,128)(2,1)S(1)}, bf16[128,512]{1,0:T(8,128)(2,1)S(1)}, u32[]{:S(2)}, u32[]{:S(2)}) collective-permute-start(bf16[128,512]{1,0:T(8,128)(2,1)S(1)} %get-tuple-element.44), channel_id=1, source_target_pairs={{0,8},{1,9},{2,10},{3,11},{4,12},{5,13},{6,14},{7,15},{8,16},{9,17... | collective-permute-start | bytes 393224 | tf_op jit(solution)/shard_map/ppermute | solution.py:32
  51.5 7.0 %collective-permute-start.16 = (bf16[128,512]{1,0:T(8,128)(2,1)S(1)}, bf16[128,512]{1,0:T(8,128)(2,1)S(1)}, u32[]{:S(2)}, u32[]{:S(2)}) collective-permute-start(bf16[128,512]{1,0:T(8,128)(2,1)S(1)} %get-tuple-element.45), channel_id=1, source_target_pairs={{0,56},{1,57},{2,58},{3,59},{4,60},{5,61},{6,62},{7,63},{8,0},{9,1... | collective-permute-start | bytes 393224 | tf_op jit(solution)/shard_map/ppermute | solution.py:32
  58.5 19.9 %copy-start.4 = (s32[2,1]{0,1:T(1,128)S(1)}, s32[2,1]{0,1:T(1,128)}, u32[]{:S(2)}) copy-start(s32[2,1]{0,1:T(1,128)} %param.8) | copy-start | bytes 28
  78.4 1.9 %collective-permute-start.17 = (bf16[16,32,512]{2,1,0:T(8,128)(2,1)S(1)}, bf16[16,32,512]{2,1,0:T(8,128)(2,1)S(1)}, u32[]{:S(2)}, u32[]{:S(2)}) collective-permute-start(bf16[16,32,512]{2,1,0:T(8,128)(2,1)S(1)} %all_to_all.35.own), channel_id=1, source_target_pairs={{0,64},{1,65},{2,66},{3,67},{4,68},{5,69},{6,70},{7,71},{8,72},{9,... | collective-permute-start | bytes 1572872 | tf_op jit(solution)/shard_map/ppermute | solution.py:32
  85.9 2.0 %collective-permute-start.18 = (bf16[2,32,4096]{2,1,0:T(8,128)(2,1)S(1)}, bf16[2,32,4096]{2,1,0:T(8,128)(2,1)S(1)}, u32[]{:S(2)}, u32[]{:S(2)}) collective-permute-start(bf16[2,32,4096]{2,1,0:T(8,128)(2,1)S(1)} %get-tuple-element.51), channel_id=1, source_target_pairs={{0,64},{1,65},{2,66},{3,67},{4,68},{5,69},{6,70},{7,71},{8,72},{9,... | collective-permute-start | bytes 1572872 | tf_op jit(solution)/shard_map/ppermute | solution.py:32
  87.9 15.4 %copy-start = (bf16[2048,512]{1,0:T(8,128)(2,1)S(1)}, bf16[2048,512]{1,0:T(8,128)(2,1)}, u32[]{:S(2)}) copy-start(bf16[2048,512]{1,0:T(8,128)(2,1)} %get-tuple-element.53.weight) | copy-start | bytes 6291460
  106.0 2.8 %collective-permute-start.19 = (bf16[528,1024]{1,0:T(8,128)(2,1)S(1)}, bf16[528,1024]{1,0:T(8,128)(2,1)S(1)}, u32[]{:S(2)}, u32[]{:S(2)}) collective-permute-start(bf16[528,1024]{1,0:T(8,128)(2,1)S(1)} %get-tuple-element.57), channel_id=1, source_target_pairs={{0,64},{1,65},{2,66},{3,67},{4,68},{5,69},{6,70},{7,71},{8,72},{9,... | collective-permute-start | bytes 3244040 | tf_op jit(solution)/shard_map/ppermute | solution.py:32
  133.0 4.9 %collective-permute-start.20 = (f32[8,512]{1,0:T(8,128)S(1)}, f32[8,512]{1,0:T(8,128)S(1)}, u32[]{:S(2)}, u32[]{:S(2)}) collective-permute-start(f32[8,512]{1,0:T(8,128)S(1)} %get-tuple-element.60), channel_id=1, source_target_pairs={{0,8},{1,9},{2,10},{3,11},{4,12},{5,13},{6,14},{7,15},{8,16},{9,17... | collective-permute-start | bytes 49160 | tf_op jit(solution)/shard_map/ppermute | solution.py:32
  134.6 3.7 %collective-permute-start.21 = (f32[8,512]{1,0:T(8,128)S(1)}, f32[8,512]{1,0:T(8,128)S(1)}, u32[]{:S(2)}, u32[]{:S(2)}) collective-permute-start(f32[8,512]{1,0:T(8,128)S(1)} %get-tuple-element.60), channel_id=1, source_target_pairs={{0,56},{1,57},{2,58},{3,59},{4,60},{5,61},{6,62},{7,63},{8,0},{9,1... | collective-permute-start | bytes 49160 | tf_op jit(solution)/shard_map/ppermute | solution.py:32
  138.3 6.3 %collective-permute-start.22 = (f32[8,512]{1,0:T(8,128)S(1)}, f32[8,512]{1,0:T(8,128)S(1)}, u32[]{:S(2)}, u32[]{:S(2)}) collective-permute-start(f32[8,512]{1,0:T(8,128)S(1)} %get-tuple-element.63.first), channel_id=1, source_target_pairs={{0,40},{1,41},{2,42},{3,43},{4,44},{5,45},{6,46},{7,47},{8,48},{9,... | collective-permute-start | bytes 49160 | tf_op jit(solution)/shard_map/ppermute | solution.py:32
  140.7 6.4 %collective-permute-start.23 = (f32[8,512]{1,0:T(8,128)S(1)}, f32[8,512]{1,0:T(8,128)S(1)}, u32[]{:S(2)}, u32[]{:S(2)}) collective-permute-start(f32[8,512]{1,0:T(8,128)S(1)} %get-tuple-element.64), channel_id=1, source_target_pairs={{0,16},{1,17},{2,18},{3,19},{4,20},{5,21},{6,22},{7,23},{8,24},{9,... | collective-permute-start | bytes 49160 | tf_op jit(solution)/shard_map/ppermute | solution.py:32

commit v3 on v2

--- a/solution.py
+++ b/solution.py
@@ -32,7 +32,7 @@
     return lax.ppermute(block, AXES, pairs)
 
 
-def kernel_call(body, operands, outs, scratch=(), scalars=0, far=(), far_outs=(), aliases=None, limit=16):
+def kernel_call(body, operands, outs, scratch=(), scalars=0, far=(), far_outs=(), near_outs=(), aliases=None, limit=16):
     operands = [
         pltpu.with_memory_space_constraint(x, pltpu.HBM) if i in far else x for i, x in enumerate(operands)
     ]
@@ -40,7 +40,8 @@
     return pl.pallas_call(
         body,
         out_shape=[
-            pltpu.HBM(s, d) if i in far_outs else jax.ShapeDtypeStruct(s, d) for i, (s, d) in enumerate(outs)
+            pltpu.HBM(s, d) if i in far_outs else pltpu.VMEM(s, d) if i in near_outs else jax.ShapeDtypeStruct(s, d)
+            for i, (s, d) in enumerate(outs)
         ],
         in_specs=[pl.BlockSpec(memory_space=space) for space in spaces],
         out_specs=[pl.BlockSpec(memory_space=pltpu.HBM if i in far_outs else pltpu.VMEM) for i in range(len(outs))],
@@ -61,12 +62,27 @@
 RING = (0, -1, 1, -2, 2, -3, 3, -4, -4)
 
 
-def pack_body(states, final_gain, query_gain, pack):
-    pack[:64, :] = states[...]
-    gains = [final_gain[...].astype(F32)]
-    gains += [query_gain[:, i * 512 : (i + 1) * 512].astype(F32) for i in range(4)]
+def pack_body(weight, states, final_gain, query_gain, columns, pack, gain_row, gain, query, sems):
+    copies = [
+        pltpu.make_async_copy(states, pack.at[pl.ds(0, 64)], sems.at[8]),
+        pltpu.make_async_copy(final_gain, gain, sems.at[9]),
+        pltpu.make_async_copy(query_gain, query, sems.at[10]),
+    ]
+    for k in range(8):
+        part = weight.at[0, :, pl.ds(k * 512, 512)]
+        copies.append(pltpu.make_async_copy(part, columns.at[k], sems.at[k]))
+    for copy in copies:
+        copy.start()
+    copies[1].wait()
+    copies[2].wait()
+    gain_row[...] = gain[...].astype(F32).reshape(1, 512)
+    gains = [gain_row[...]]
+    gains += [query[:, i * 512 : (i + 1) * 512].astype(F32) for i in range(4)]
     gains += [jnp.zeros((11, 512), F32)]
     pack[64:, :] = jnp.concatenate(gains, axis=0).astype(BF)
+    copies[0].wait()
+    for copy in copies[3:]:
+        copy.wait()
 
 
 def norm_body(p0, p1, p2, p3, ahead_in, behind_in, streams, upstreams,
@@ -96,7 +112,7 @@
         copy.wait()
 
 
-def near_body(half, p1, p2, p3, across_in, ahead_in, behind_in, near, others, across, ahead, behind):
+def near_body(across_in, half, p1, p2, p3, ahead_in, behind_in, near, others, across, ahead, behind):
     near[0] = half[...]
     for k, part in enumerate((p1, p2, p3)):
         near[k + 1] = part[...]
@@ -113,21 +129,43 @@
     lower[...] = behind_in[128:]
 
 
-def project_body(own, other, *refs):
-    blocks, (out, held, weight_out, weight, result, sems) = refs[:9], refs[9:]
-    c, z, xl, y = coordinates("core", "z", "xl", "y")
+def own_places(held, own_half):
+    c, xl, y = coordinates("core", "xl", "y")
+    m = (c + (0 if own_half else 1)) % 2
+    return [held.at[m, (xl + dxl) % 2 * 4 + (y + NY - dy) % NY] for dy in range(NY) for dxl in range(2)]
+
+
+def ring_places(weight):
+    (z,) = coordinates("z")
+    starts = [(z + 8 + far) % 8 * 256 + 128 * (k == 8) for k, far in enumerate(RING)]
+    return [weight.at[pl.ds(pl.multiple_of(at, 128), 256 if k < 7 else 128)] for k, at in enumerate(starts)]
+
+
+def save_body(own, *refs):
+    blocks, (held, weight, sems) = refs[:5], refs[5:]
     copies = []
-    for i, rows in enumerate((own, other)):
-        for dy in range(NY):
-            for dxl in range(2):
-                place = held.at[(c + i) % 2, (xl + dxl) % 2 * 4 + (y + NY - dy) % NY]
-                copies.append(pltpu.make_async_copy(rows.at[dy, dxl], place, sems.at[i * 8 + dy * 2 + dxl]))
-                copies[-1].start()
-    for k, block in enumerate(blocks):
-        place = (z + 8 + RING[k]) % 8 * 256 + 128 * (k == 8)
-        weight[pl.ds(pl.multiple_of(place, 128), block.shape[0]), :] = block[...]
-    copies.append(pltpu.make_async_copy(weight, weight_out, sems.at[16]))
-    copies[-1].start()
+    for k, place in enumerate(own_places(held, True)):
+        copies.append(pltpu.make_async_copy(own.at[k // 2, k % 2], place, sems.at[k]))
+    for k, place in enumerate(ring_places(weight)[:5]):
+        copies.append(pltpu.make_async_copy(blocks[k], place, sems.at[8 + k]))
+    for copy in copies:
+        copy.start()
+    for copy in copies:
+        copy.wait()
+
+
+def project_body(held_in, weight_in, own, other, *refs):
+    blocks, (held, weight_out, out, weight, result, sems) = refs[:9], refs[9:]
+    c, xl, y = coordinates("core", "xl", "y")
+    copies = []
+    for k, place in enumerate(ring_places(weight_out)[5:]):
+        copies.append(pltpu.make_async_copy(blocks[5 + k], place, sems.at[8 + k]))
+    for k, place in enumerate(own_places(held, False)):
+        copies.append(pltpu.make_async_copy(other.at[k // 2, k % 2], place, sems.at[k]))
+    for copy in copies:
+        copy.start()
+    for block, place in zip(blocks, ring_places(weight)):
+        place[...] = block[...]
     for i, rows in enumerate((own, other)):
         result[...] = jnp.dot(rows[...].reshape(256, D), weight[...], preferred_element_type=F32).astype(BF)
         for dy in range(NY):
@@ -147,7 +185,7 @@
         pairs[2 * i + 1 - c] = other[8 * i : 8 * i + 8]
     streams[0] = stream_in[...]
     incoming[...] = upstream[...].astype(F32)
-    length = lengths[xh, 0]
+    length = lengths[0, xh]
     block = (lax.broadcasted_iota(jnp.int32, (128, 256), 0) // 32) == (
         lax.broadcasted_iota(jnp.int32, (128, 256), 1) // HEAD)
     block = jnp.where(block, 1.0, 0.0).astype(BF)
@@ -305,30 +343,38 @@
     for k in range(1, 16):
         total += received[k].astype(F32)
     extras = total[64:72] + total[72:80]
-    sums[...] = extras
+    sums[...] = jnp.broadcast_to(extras[None], (8, 8, 512))
     rows[...] = jnp.transpose(jnp.broadcast_to(extras[5:6], (128, 512)))
     for m in range(2):
         span = slice(m * 32, (m + 1) * 32)
         row_sum = rows[lanes(m * 256 + (xl * 4 + y) * 32, 32), 0:1]
         scale = factor[span, 0:1]
-        scaled = total[span] * final_gain[...].astype(F32)
+        scaled = total[span] * final_gain[...]
         wide = states[span, :].astype(F32)
         gradient[span, :] = scale * scaled - wide * (scale * scale * (row_sum / D))
 
 
-def close_body(first, second, third, final_gain, final_gradient, layers_gradient):
-    total = first[...] + second[...] + third[...]
+def close_body(received, final_gain, final_gradient, layers_gradient):
+    total = received[0]
+    for k in range(1, 8):
+        total += received[k]
     for i in range(4):
         layers_gradient[:, i * 512 : (i + 1) * 512] = total[i : i + 1]
-    final_gradient[...] = total[4:5] / final_gain[...].astype(F32)
+    final_gradient[...] = total[4:5] / final_gain[...]
 
 
 def per_device(
     encoder_states, encoder_lengths, final_gain, decoder_states, query_gain, cross_weight, upstream
 ):
-    block = lax.all_to_all(cross_weight[0], ("xl", "y"), 1, 0, tiled=True)
     states = encoder_states.reshape(64, 512)
-    (pack,) = kernel_call(pack_body, (states, final_gain[None], query_gain), [((80, 512), BF)])
+    columns, pack, gain_row = kernel_call(
+        pack_body,
+        (cross_weight, states, final_gain, query_gain),
+        [((8, 32, 512), BF), ((80, 512), BF), ((1, 512), F32)],
+        [((512,), BF), ((1, D), BF), pltpu.SemaphoreType.DMA((11,))],
+        far=(0, 1, 2, 3),
+    )
+    block = lax.all_to_all(columns, ("xl", "y"), 0, 0, tiled=True).reshape(256, 512)
     packs = [pack, shift(pack, core=1), shift(pack, xh=1), shift(pack, xh=1, core=1)]
     tile = ((256, 512), BF)
     half, factor, query_gains, stream, incoming, ahead1, behind1 = kernel_call(
@@ -341,10 +387,11 @@
     )
     near, others, across, ahead2, behind2 = kernel_call(
         near_body,
-        [half] + [shift(half, y=dy) for dy in range(1, NY)]
-        + [shift(half, xl=1), shift(ahead1, z=1), shift(behind1, z=-1)],
+        [shift(half, xl=1), half]
+        + [shift(half, y=dy) for dy in range(1, NY)]
+        + [shift(ahead1, z=1), shift(behind1, z=-1)],
         [((NY, 32, D), BF), ((NY - 1, 32, D), BF), ((32, D), BF), tile, tile],
-        aliases={4: 2, 5: 3, 6: 4},
+        aliases={0: 2, 5: 3, 6: 4},
     )
     own_rows, upper, lower, ahead3, behind3 = kernel_call(
         group_body,
@@ -353,18 +400,28 @@
         aliases={3: 3, 4: 4},
     )
     ring = [block, ahead1, behind1, ahead2, behind2, ahead3, behind3, shift(upper, z=1), shift(lower, z=-1)]
-    projected, held, weight = kernel_call(
+    held, weight = kernel_call(
+        save_body,
+        [own_rows] + ring[:5],
+        [((2, 8, 32, D), BF), ((D, 512), BF)],
+        [pltpu.SemaphoreType.DMA((13,))],
+        far_outs=(0, 1),
+    )
+    held, weight, projected = kernel_call(
         project_body,
-        [own_rows, shift(own_rows, core=1)] + ring,
-        [((16, 32, 512), BF), ((2, 8, 32, D), BF), ((D, 512), BF)],
-        [((D, 512), BF), ((256, 512), BF), pltpu.SemaphoreType.DMA((17,))],
-        far_outs=(1, 2),
+        [held, weight, own_rows, shift(own_rows, core=1)] + ring,
+        [((2, 8, 32, D), BF), ((D, 512), BF), ((16, 32, 512), BF)],
+        [((D, 512), BF), ((256, 512), BF), pltpu.SemaphoreType.DMA((12,))],
+        far=(0, 1),
+        far_outs=(0, 1),
+        near_outs=(2,),
+        aliases={0: 0, 1: 1},
     )
     own_pairs = lax.all_to_all(projected, ("xh", "xl", "y"), 0, 0, tiled=True)
     other_pairs = shift(own_pairs, core=1)
     keep, send, gain_parts = kernel_call(
         decoder_body,
-        (encoder_lengths, own_pairs, other_pairs, stream, incoming, query_gains),
+        (encoder_lengths.T, own_pairs, other_pairs, stream, incoming, query_gains),
         [((2, 32, 4096), BF), ((2, 32, 4096), BF), ((4, 1, D), F32)],
         [
             ((4, 8, 32, 512), BF),
@@ -376,7 +433,7 @@
         ],
         scalars=1,
     )
-    (joined,) = kernel_call(join_body, (keep, shift(send, core=1)), [((16, 32, 512), BF)])
+    (joined,) = kernel_call(join_body, (keep, shift(send, core=1)), [((16, 32, 512), BF)], near_outs=(0,))
     joined = lax.all_to_all(joined, ("xh", "xl", "y"), 0, 0, tiled=True)
     term_keep, extra, term_send = kernel_call(
         back_body,
@@ -390,24 +447,22 @@
             pltpu.SemaphoreType.DMA,
         ],
         far=(1,),
+        near_outs=(0, 1, 2),
     )
     (merged,) = kernel_call(
-        merge_body, (term_keep, extra, shift(term_send, core=1)), [((16, 80, 512), BF)]
+        merge_body, (term_keep, extra, shift(term_send, core=1)), [((16, 80, 512), BF)], near_outs=(0,)
     )
     merged = lax.all_to_all(merged, ("xh", "xl", "y"), 0, 0, tiled=True)
     gradient, sums = kernel_call(
         finish_body,
-        (merged, states, factor, final_gain[None]),
-        [((64, 512), F32), ((8, 512), F32)],
+        (merged, pack, factor, gain_row),
+        [((64, 512), F32), ((8, 8, 512), F32)],
         [((512, 128), F32)],
-    )
-    ahead = shift(sums, z=1)
-    pair = sums + ahead
-    triple = pair + shift(sums, z=-1)
+        near_outs=(1,),
+    )
+    sums = lax.all_to_all(sums, "z", 0, 0, tiled=True)
     final_gradient, layers_gradient = kernel_call(
-        close_body,
-        (triple, shift(triple, z=-3), shift(pair, z=2), final_gain[None]),
-        [((1, 512), F32), ((1, D), F32)],
+        close_body, (sums, gain_row), [((1, 512), F32), ((1, D), F32)]
     )
     return (gradient.reshape(2, 32, 512), final_gradient[0], layers_gradient)
 

time: 148 us -> 145 us (0.980)
  blocking collectives: 66.3 us -> 79.4 us
  waiting for transfers between devices: 33 us -> 23 us
  starting transfers between devices: 32.1 us -> 25.6 us
  Pallas kernels: 14.4 us -> 16.2 us
    all_to_all x1 -> x2, blocking collectives: 11.1 us -> 24.8 us  [the longest x1 13.8 us: per_device(): sums = lax.all_to_all(sums, 'z', 0, 0, tiled=True)]
    ppermute x24 -> x20, waiting for transfers between devices: 33 us -> 23 us  [shift(): return lax.ppermute(block, AXES, pairs)]
    ppermute x24 -> x20, starting transfers between devices: 32.1 us -> 25.6 us  [shift(): return lax.ppermute(block, AXES, pairs)]
    pallas_call x11 -> x12, Pallas kernels: 14.4 us -> 16.2 us  [kernel_call(): pl.pallas_call(body, out_shape=[pltpu.HBM(s, d) if i in far_outs else plt...]
  transfers between devices with their start and end apart: 24 -> 20, of which waited for: 14 -> 11; matrix products, arithmetic and copies ran while one was open for 0% -> 0% of each run, Pallas kernels for 0% -> 1%
where the time goes in v3:
time: 145 us
  blocking collectives  79.4 us (55%)
  starting transfers between devices  25.6 us (18%)
  waiting for transfers between devices  23 us (16%)
  Pallas kernels  16.2 us (11%)
    ppermute x20, starting transfers between devices, shift(): return lax.ppermute(block, AXES, pairs)  25.6 us
    all_to_all x1, blocking collectives, per_device(): merged = lax.all_to_all(merged, ('xh', 'xl', 'y'), 0, 0, tiled=True)  23.1 us
    ppermute x20, waiting for transfers between devices, shift(): return lax.ppermute(block, AXES, pairs)  23 us
    all_to_all x1, blocking collectives, per_device(): own_pairs = lax.all_to_all(projected, ('xh', 'xl', 'y'), 0, 0, tiled=True)  16.4 us
    pallas_call x12, Pallas kernels, kernel_call(): pl.pallas_call(body, out_shape=[pltpu.HBM(s, d) if i in far_outs else plt...  16.2 us
    all_to_all x1, blocking collectives, per_device(): joined = lax.all_to_all(joined, ('xh', 'xl', 'y'), 0, 0, tiled=True)  15.1 us
    all_to_all x1, blocking collectives, per_device(): sums = lax.all_to_all(sums, 'z', 0, 0, tiled=True)  13.8 us
    all_to_all x1, blocking collectives, per_device(): lax.all_to_all(columns, ('xl', 'y'), 0, 0, tiled=True).reshape(256, 512)  11.1 us
  transfers between devices with their start and end apart: 20, of which 11 were waited for; matrix products, arithmetic and copies ran while one was open for 0% of the time, Pallas kernels for 1%

profile of v3, /device:TPU:8, one launch (start us, length us, event | category | flops | bytes accessed | tf_op | source)
XLA Modules:
  0.0 145.0 jit_solution(14503853831171385324)
XLA Ops:
  0.6 1.0 shard_map.94
  1.7 11.1 %all_to_all.25 = bf16[8,32,512]{2,1,0:T(8,128)(2,1)S(1)} all-to-all(bf16[8,32,512]{2,1,0:T(8,128)(2,1)S(1)} %get-tuple-element.39), channel_id=1, replica_groups=mesh['xh'=2,'core'=2,'z'=8,'xl'=2,'y'=4] {'xl','y'}, dimensions={0} | all-to-all | bytes 524288 | tf_op jit(solution)/shard_map/all_to_all | solution.py:377
  12.7 5.9 %collective-permute-start.4 = (bf16[256,512]{1,0:T(8,128)(2,1)S(1)}, bf16[256,512]{1,0:T(8,128)(2,1)S(1)}, u32[]{:S(2)}, u32[]{:S(2)}) collective-permute-start(bf16[256,512]{1,0:T(8,128)(2,1)S(1)} %bitcast.5), channel_id=1, source_target_pairs={{0,56},{1,57},{2,58},{3,59},{4,60},{5,61},{6,62},{7,63},{8,0},{9,1... | collective-permute-start | bytes 786440 | tf_op jit(solution)/shard_map/ppermute | solution.py:32
  18.6 0.0 collective-permute-start.3
  18.6 0.5 collective-permute-start.2
  19.1 2.3 %collective-permute-start.1 = (bf16[80,512]{1,0:T(8,128)(2,1)S(1)}, bf16[80,512]{1,0:T(8,128)(2,1)S(1)}, u32[]{:S(2)}, u32[]{:S(2)}) collective-permute-start(bf16[80,512]{1,0:T(8,128)(2,1)S(1)} %get-tuple-element.38.p0.states), channel_id=1, source_target_pairs={{0,128},{1,129},{2,130},{3,131},{4,132},{5,133},{6,134},{7,135},{8... | collective-permute-start | bytes 245768 | tf_op jit(solution)/shard_map/ppermute | solution.py:32
  21.4 0.6 collective-permute-start
  22.0 2.9 %collective-permute-done.2.p3 = bf16[80,512]{1,0:T(8,128)(2,1)S(1)} collective-permute-done((bf16[80,512]{1,0:T(8,128)(2,1)S(1)}, bf16[80,512]{1,0:T(8,128)(2,1)S(1)}, u32[]{:S(2)}, u32[]{:S(2)}) %collective-permute-start.2) | collective-permute-done | bytes 81952 | tf_op jit(solution)/shard_map/ppermute | solution.py:32
  24.8 0.7 collective-permute-done.1.p2
  25.5 0.0 collective-permute-done.p1
  25.5 0.0 collective-permute-done.4.behind_in
  25.5 0.7 collective-permute-done.3.ahead_in
  26.2 1.1 shard_map.95
  27.3 1.9 %collective-permute-start.8 = (bf16[32,2048]{1,0:T(8,128)(2,1)S(1)}, bf16[32,2048]{1,0:T(8,128)(2,1)S(1)}, u32[]{:S(2)}, u32[]{:S(2)}) collective-permute-start(bf16[32,2048]{1,0:T(8,128)(2,1)S(1)} %get-tuple-element.40.half), channel_id=1, source_target_pairs={{0,3},{1,0},{2,1},{3,2},{4,7},{5,4},{6,5},{7,6},{8,11},{9,8},{10,9... | collective-permute-start | bytes 393224 | tf_op jit(solution)/shard_map/ppermute | solution.py:32
  29.1 3.2 %collective-permute-start.10 = (bf16[256,512]{1,0:T(8,128)(2,1)S(1)}, bf16[256,512]{1,0:T(8,128)(2,1)S(1)}, u32[]{:S(2)}, u32[]{:S(2)}) collective-permute-start(bf16[256,512]{1,0:T(8,128)(2,1)S(1)} %get-tuple-element.42.refs_2_), channel_id=1, source_target_pairs={{0,56},{1,57},{2,58},{3,59},{4,60},{5,61},{6,62},{7,63},{8,0},{9,1... | collective-permute-start | bytes 786440 | tf_op jit(solution)/shard_map/ppermute | solution.py:32
  32.4 0.6 collective-permute-start.7
  32.9 1.9 %collective-permute-start.6 = (bf16[32,2048]{1,0:T(8,128)(2,1)S(1)}, bf16[32,2048]{1,0:T(8,128)(2,1)S(1)}, u32[]{:S(2)}, u32[]{:S(2)}) collective-permute-start(bf16[32,2048]{1,0:T(8,128)(2,1)S(1)} %get-tuple-element.40.half), channel_id=1, source_target_pairs={{0,1},{1,2},{2,3},{3,0},{4,5},{5,6},{6,7},{7,4},{8,9},{9,10},{10,1... | collective-permute-start | bytes 393224 | tf_op jit(solution)/shard_map/ppermute | solution.py:32
  34.8 0.0 collective-permute-done.8.p3
  34.8 1.1 collective-permute-start.5
  35.9 2.9 %collective-permute-done.7.p2 = bf16[32,2048]{1,0:T(8,128)(2,1)S(1)} collective-permute-done((bf16[32,2048]{1,0:T(8,128)(2,1)S(1)}, bf16[32,2048]{1,0:T(8,128)(2,1)S(1)}, u32[]{:S(2)}, u32[]{:S(2)}) %collective-permute-start.7) | collective-permute-done | bytes 131104 | tf_op jit(solution)/shard_map/ppermute | solution.py:32
  38.8 1.5 %collective-permute-done.6.p1 = bf16[32,2048]{1,0:T(8,128)(2,1)S(1)} collective-permute-done((bf16[32,2048]{1,0:T(8,128)(2,1)S(1)}, bf16[32,2048]{1,0:T(8,128)(2,1)S(1)}, u32[]{:S(2)}, u32[]{:S(2)}) %collective-permute-start.6) | collective-permute-done | bytes 131104 | tf_op jit(solution)/shard_map/ppermute | solution.py:32
  40.4 0.1 shard_map.96
  40.4 0.8 collective-permute-start.11
  41.2 3.2 %collective-permute-start.13 = (bf16[256,512]{1,0:T(8,128)(2,1)S(1)}, bf16[256,512]{1,0:T(8,128)(2,1)S(1)}, u32[]{:S(2)}, u32[]{:S(2)}) collective-permute-start(bf16[256,512]{1,0:T(8,128)(2,1)S(1)} %get-tuple-element.47.refs_4_), channel_id=1, source_target_pairs={{0,56},{1,57},{2,58},{3,59},{4,60},{5,61},{6,62},{7,63},{8,0},{9,1... | collective-permute-start | bytes 786440 | tf_op jit(solution)/shard_map/ppermute | solution.py:32
  44.4 4.3 %collective-permute-done.12.ahead_in = bf16[256,512]{1,0:T(8,128)(2,1)S(1)} collective-permute-done((bf16[256,512]{1,0:T(8,128)(2,1)S(1)}, bf16[256,512]{1,0:T(8,128)(2,1)S(1)}, u32[]{:S(2)}, u32[]{:S(2)}) %collective-permute-start.12) | collective-permute-done | bytes 262176 | tf_op jit(solution)/shard_map/ppermute | solution.py:32
  48.8 1.4 collective-permute-done.11.beyond
  50.1 0.1 shard_map.97
  50.2 0.1 collective-permute-start.14
  50.3 0.1 collective-permute-start.15
  50.4 3.2 %collective-permute-start.16 = (bf16[128,512]{1,0:T(8,128)(2,1)S(1)}, bf16[128,512]{1,0:T(8,128)(2,1)S(1)}, u32[]{:S(2)}, u32[]{:S(2)}) collective-permute-start(bf16[128,512]{1,0:T(8,128)(2,1)S(1)} %get-tuple-element.54), channel_id=1, source_target_pairs={{0,56},{1,57},{2,58},{3,59},{4,60},{5,61},{6,62},{7,63},{8,0},{9,1... | collective-permute-start | bytes 393224 | tf_op jit(solution)/shard_map/ppermute | solution.py:32
  53.7 1.6 %shard_map.98 = (bf16[2,8,32,2048]{3,2,1,0:T(8,128)(2,1)}, bf16[2048,512]{1,0:T(8,128)(2,1)}) custom-call(bf16[4,2,32,2048]{3,2,1,0:T(8,128)(2,1)S(1)} %get-tuple-element.48.own, bf16[256,512]{1,0:T(8,128)(2,1)S(1)} %bitcast.7, bf16[256,512]{1,0:T(8,128)(2,1)S(1)} %get-tuple-element.41.refs_1_, bf16[256,512]{1,0:T(8,128)(2,1)S(1)} %get-tuple-element.42.refs_2_, ...), custom_call_target="tpu_custom_call" | custom-call | tf_op jit(solution)/shard_map/pallas_call | solution.py:40
  55.2 2.2 %collective-permute-done.15.refs_7_ = bf16[128,512]{1,0:T(8,128)(2,1)S(1)} collective-permute-done((bf16[128,512]{1,0:T(8,128)(2,1)S(1)}, bf16[128,512]{1,0:T(8,128)(2,1)S(1)}, u32[]{:S(2)}, u32[]{:S(2)}) %collective-permute-start.15) | collective-permute-done | bytes 131104 | tf_op jit(solution)/shard_map/ppermute | solution.py:32
  57.5 2.3 %shard_map.99 = (bf16[2,8,32,2048]{3,2,1,0:T(8,128)(2,1)}, bf16[2048,512]{1,0:T(8,128)(2,1)}, bf16[16,32,512]{2,1,0:T(8,128)(2,1)S(1)}) custom-call(bf16[2,8,32,2048]{3,2,1,0:T(8,128)(2,1)} %get-tuple-element.49.held_in, bf16[2048,512]{1,0:T(8,128)(2,1)} %get-tuple-element.50.weight_in, ...), custom_call_target="tpu_custom_call", output_to_operand_aliasing={{0}: (0, {}), {1}: (1, {})} | custom-call | tf_op jit(solution)/shard_map/pallas_call | solution.py:40
  59.8 16.4 %all_to_all.26.own = bf16[16,32,512]{2,1,0:T(8,128)(2,1)S(1)} all-to-all(bf16[16,32,512]{2,1,0:T(8,128)(2,1)S(1)} %get-tuple-element.55), channel_id=1, replica_groups=mesh['xh'=2,'core'=2,'z'=8,'xl'=2,'y'=4] {'xh','xl','y'}, dimensions={0} | all-to-all | bytes 1048576 | tf_op jit(solution)/shard_map/all_to_all | solution.py:420
  76.2 1.9 %collective-permute-done.17.other = bf16[16,32,512]{2,1,0:T(8,128)(2,1)S(1)} collective-permute-done((bf16[16,32,512]{2,1,0:T(8,128)(2,1)S(1)}, bf16[16,32,512]{2,1,0:T(8,128)(2,1)S(1)}, u32[]{:S(2)}, u32[]{:S(2)}) %collective-permute-start.17) | collective-permute-done | bytes 524320 | tf_op jit(solution)/shard_map/ppermute | solution.py:32
  78.1 5.6 %shard_map.100 = (bf16[2,32,4096]{2,1,0:T(8,128)(2,1)S(1)}, bf16[2,32,4096]{2,1,0:T(8,128)(2,1)S(1)}, f32[4,1,2048]{2,1,0:T(1,128)S(1)}) custom-call(s32[1,2]{1,0:T(1,128)S(1)} %bitcast.9, bf16[16,32,512]{2,1,0:T(8,128)(2,1)S(1)} %all_to_all.26.own, bf16[16,32,512]{2,1,0:T(8,128)(2,1)S(1)} %collective-permute-done.17.other, ...), custom_call_target="tpu_custom_call" | custom-call | tf_op jit(solution)/shard_map/pallas_call | solution.py:40
  83.6 0.2 collective-permute-start.18
  83.9 1.7 %collective-permute-done.18.received = bf16[2,32,4096]{2,1,0:T(8,128)(2,1)S(1)} collective-permute-done((bf16[2,32,4096]{2,1,0:T(8,128)(2,1)S(1)}, bf16[2,32,4096]{2,1,0:T(8,128)(2,1)S(1)}, u32[]{:S(2)}, u32[]{:S(2)}) %collective-permute-start.18) | collective-permute-done | bytes 524320 | tf_op jit(solution)/shard_map/ppermute | solution.py:32
  85.6 0.1 shard_map.101
  85.8 15.1 %all_to_all.27.gradient = bf16[16,32,512]{2,1,0:T(8,128)(2,1)S(1)} all-to-all(bf16[16,32,512]{2,1,0:T(8,128)(2,1)S(1)} %shard_map.101), channel_id=1, replica_groups=mesh['xh'=2,'core'=2,'z'=8,'xl'=2,'y'=4] {'xh','xl','y'}, dimensions={0} | all-to-all | bytes 1048576 | tf_op jit(solution)/shard_map/all_to_all | solution.py:437
  100.9 2.7 %shard_map.102 = (f32[512,1024]{1,0:T(8,128)S(1)}, f32[8,1024]{1,0:T(8,128)S(1)}, bf16[528,1024]{1,0:T(8,128)(2,1)S(1)}) custom-call(bf16[16,32,512]{2,1,0:T(8,128)(2,1)S(1)} %all_to_all.27.gradient, bf16[2,8,32,2048]{3,2,1,0:T(8,128)(2,1)} %get-tuple-element.61.held_far, bf16[2048,512]{1,0:T(8,128)(2,1)S(1)} %copy-done, ...), custom_call_target="tpu_custom_call" | custom-call | tf_op jit(solution)/shard_map/pallas_call | solution.py:40
  103.6 0.1 collective-permute-start.19
  103.7 2.7 %collective-permute-done.19.received = bf16[528,1024]{1,0:T(8,128)(2,1)S(1)} collective-permute-done((bf16[528,1024]{1,0:T(8,128)(2,1)S(1)}, bf16[528,1024]{1,0:T(8,128)(2,1)S(1)}, u32[]{:S(2)}, u32[]{:S(2)}) %collective-permute-start.19) | collective-permute-done | bytes 1081376 | tf_op jit(solution)/shard_map/ppermute | solution.py:32
  106.4 0.2 shard_map.103
  106.6 23.1 %all_to_all.28.received = bf16[16,80,512]{2,1,0:T(8,128)(2,1)S(1)} all-to-all(bf16[16,80,512]{2,1,0:T(8,128)(2,1)S(1)} %shard_map.103), channel_id=1, replica_groups=mesh['xh'=2,'core'=2,'z'=8,'xl'=2,'y'=4] {'xh','xl','y'}, dimensions={0} | all-to-all | bytes 2621440 | tf_op jit(solution)/shard_map/all_to_all | solution.py:455
  129.7 0.9 shard_map.104
  130.6 13.8 %all_to_all.29.received = f32[8,8,512]{2,1,0:T(8,128)S(1)} all-to-all(f32[8,8,512]{2,1,0:T(8,128)S(1)} %get-tuple-element.70), channel_id=1, replica_groups=mesh['xh'=2,'core'=2,'z'=8,'xl'=2,'y'=4] {'z'}, dimensions={0} | all-to-all | bytes 262144 | tf_op jit(solution)/shard_map/all_to_all | solution.py:463
  144.4 0.6 shard_map.105
  (13 shorter events, 0.0 us)
Async XLA Ops:
  12.7 12.8 %collective-permute-start.4 = (bf16[256,512]{1,0:T(8,128)(2,1)S(1)}, bf16[256,512]{1,0:T(8,128)(2,1)S(1)}, u32[]{:S(2)}, u32[]{:S(2)}) collective-permute-start(bf16[256,512]{1,0:T(8,128)(2,1)S(1)} %bitcast.5), channel_id=1, source_target_pairs={{0,56},{1,57},{2,58},{3,59},{4,60},{5,61},{6,62},{7,63},{8,0},{9,1... | collective-permute-start | bytes 786440 | tf_op jit(solution)/shard_map/ppermute | solution.py:32
  18.6 7.6 %collective-permute-start.3 = (bf16[256,512]{1,0:T(8,128)(2,1)S(1)}, bf16[256,512]{1,0:T(8,128)(2,1)S(1)}, u32[]{:S(2)}, u32[]{:S(2)}) collective-permute-start(bf16[256,512]{1,0:T(8,128)(2,1)S(1)} %bitcast.6), channel_id=1, source_target_pairs={{0,8},{1,9},{2,10},{3,11},{4,12},{5,13},{6,14},{7,15},{8,16},{9,17... | collective-permute-start | bytes 786440 | tf_op jit(solution)/shard_map/ppermute | solution.py:32
  18.6 6.2 %collective-permute-start.2 = (bf16[80,512]{1,0:T(8,128)(2,1)S(1)}, bf16[80,512]{1,0:T(8,128)(2,1)S(1)}, u32[]{:S(2)}, u32[]{:S(2)}) collective-permute-start(bf16[80,512]{1,0:T(8,128)(2,1)S(1)} %get-tuple-element.38.p0.states), channel_id=1, source_target_pairs={{0,192},{1,193},{2,194},{3,195},{4,196},{5,197},{6,198},{7,199},{8... | collective-permute-start | bytes 245768 | tf_op jit(solution)/shard_map/ppermute | solution.py:32
  19.1 6.4 %collective-permute-start.1 = (bf16[80,512]{1,0:T(8,128)(2,1)S(1)}, bf16[80,512]{1,0:T(8,128)(2,1)S(1)}, u32[]{:S(2)}, u32[]{:S(2)}) collective-permute-start(bf16[80,512]{1,0:T(8,128)(2,1)S(1)} %get-tuple-element.38.p0.states), channel_id=1, source_target_pairs={{0,128},{1,129},{2,130},{3,131},{4,132},{5,133},{6,134},{7,135},{8... | collective-permute-start | bytes 245768 | tf_op jit(solution)/shard_map/ppermute | solution.py:32
  21.4 4.1 %collective-permute-start = (bf16[80,512]{1,0:T(8,128)(2,1)S(1)}, bf16[80,512]{1,0:T(8,128)(2,1)S(1)}, u32[]{:S(2)}, u32[]{:S(2)}) collective-permute-start(bf16[80,512]{1,0:T(8,128)(2,1)S(1)} %get-tuple-element.38.p0.states), channel_id=1, source_target_pairs={{0,64},{1,65},{2,66},{3,67},{4,68},{5,69},{6,70},{7,71},{8,72},{9,... | collective-permute-start | bytes 245768 | tf_op jit(solution)/shard_map/ppermute | solution.py:32
  27.3 7.6 %collective-permute-start.8 = (bf16[32,2048]{1,0:T(8,128)(2,1)S(1)}, bf16[32,2048]{1,0:T(8,128)(2,1)S(1)}, u32[]{:S(2)}, u32[]{:S(2)}) collective-permute-start(bf16[32,2048]{1,0:T(8,128)(2,1)S(1)} %get-tuple-element.40.half), channel_id=1, source_target_pairs={{0,3},{1,0},{2,1},{3,2},{4,7},{5,4},{6,5},{7,6},{8,11},{9,8},{10,9... | collective-permute-start | bytes 393224 | tf_op jit(solution)/shard_map/ppermute | solution.py:32
  29.1 11.2 %collective-permute-start.9 = (bf16[256,512]{1,0:T(8,128)(2,1)S(1)}, bf16[256,512]{1,0:T(8,128)(2,1)S(1)}, u32[]{:S(2)}, u32[]{:S(2)}) collective-permute-start(bf16[256,512]{1,0:T(8,128)(2,1)S(1)} %get-tuple-element.41.refs_1_), channel_id=1, source_target_pairs={{0,8},{1,9},{2,10},{3,11},{4,12},{5,13},{6,14},{7,15},{8,16},{9,17... | collective-permute-start | bytes 786440 | tf_op jit(solution)/shard_map/ppermute | solution.py:32
  29.1 11.2 %collective-permute-start.10 = (bf16[256,512]{1,0:T(8,128)(2,1)S(1)}, bf16[256,512]{1,0:T(8,128)(2,1)S(1)}, u32[]{:S(2)}, u32[]{:S(2)}) collective-permute-start(bf16[256,512]{1,0:T(8,128)(2,1)S(1)} %get-tuple-element.42.refs_2_), channel_id=1, source_target_pairs={{0,56},{1,57},{2,58},{3,59},{4,60},{5,61},{6,62},{7,63},{8,0},{9,1... | collective-permute-start | bytes 786440 | tf_op jit(solution)/shard_map/ppermute | solution.py:32
  32.4 6.5 %collective-permute-start.7 = (bf16[32,2048]{1,0:T(8,128)(2,1)S(1)}, bf16[32,2048]{1,0:T(8,128)(2,1)S(1)}, u32[]{:S(2)}, u32[]{:S(2)}) collective-permute-start(bf16[32,2048]{1,0:T(8,128)(2,1)S(1)} %get-tuple-element.40.half), channel_id=1, source_target_pairs={{0,2},{1,3},{2,0},{3,1},{4,6},{5,7},{6,4},{7,5},{8,10},{9,11},{10,... | collective-permute-start | bytes 393224 | tf_op jit(solution)/shard_map/ppermute | solution.py:32
  32.9 7.4 %collective-permute-start.6 = (bf16[32,2048]{1,0:T(8,128)(2,1)S(1)}, bf16[32,2048]{1,0:T(8,128)(2,1)S(1)}, u32[]{:S(2)}, u32[]{:S(2)}) collective-permute-start(bf16[32,2048]{1,0:T(8,128)(2,1)S(1)} %get-tuple-element.40.half), channel_id=1, source_target_pairs={{0,1},{1,2},{2,3},{3,0},{4,5},{5,6},{6,7},{7,4},{8,9},{9,10},{10,1... | collective-permute-start | bytes 393224 | tf_op jit(solution)/shard_map/ppermute | solution.py:32
  34.8 5.5 %collective-permute-start.5 = (bf16[32,2048]{1,0:T(8,128)(2,1)S(1)}, bf16[32,2048]{1,0:T(8,128)(2,1)S(1)}, u32[]{:S(2)}, u32[]{:S(2)}) collective-permute-start(bf16[32,2048]{1,0:T(8,128)(2,1)S(1)} %get-tuple-element.40.half), channel_id=1, source_target_pairs={{0,4},{1,5},{2,6},{3,7},{4,0},{5,1},{6,2},{7,3},{8,12},{9,13},{10,... | collective-permute-start | bytes 393224 | tf_op jit(solution)/shard_map/ppermute | solution.py:32
  40.4 9.7 %collective-permute-start.11 = (bf16[3,32,2048]{2,1,0:T(8,128)(2,1)S(1)}, bf16[3,32,2048]{2,1,0:T(8,128)(2,1)S(1)}, u32[]{:S(2)}, u32[]{:S(2)}) collective-permute-start(bf16[3,32,2048]{2,1,0:T(8,128)(2,1)S(1)} %get-tuple-element.45), channel_id=1, source_target_pairs={{0,4},{1,5},{2,6},{3,7},{4,0},{5,1},{6,2},{7,3},{8,12},{9,13},{10,... | collective-permute-start | bytes 1179656 | tf_op jit(solution)/shard_map/ppermute | solution.py:32
  41.2 7.6 %collective-permute-start.12 = (bf16[256,512]{1,0:T(8,128)(2,1)S(1)}, bf16[256,512]{1,0:T(8,128)(2,1)S(1)}, u32[]{:S(2)}, u32[]{:S(2)}) collective-permute-start(bf16[256,512]{1,0:T(8,128)(2,1)S(1)} %get-tuple-element.46.refs_3_), channel_id=1, source_target_pairs={{0,8},{1,9},{2,10},{3,11},{4,12},{5,13},{6,14},{7,15},{8,16},{9,17... | collective-permute-start | bytes 786440 | tf_op jit(solution)/shard_map/ppermute | solution.py:32
  41.2 7.6 %collective-permute-start.13 = (bf16[256,512]{1,0:T(8,128)(2,1)S(1)}, bf16[256,512]{1,0:T(8,128)(2,1)S(1)}, u32[]{:S(2)}, u32[]{:S(2)}) collective-permute-start(bf16[256,512]{1,0:T(8,128)(2,1)S(1)} %get-tuple-element.47.refs_4_), channel_id=1, source_target_pairs={{0,56},{1,57},{2,58},{3,59},{4,60},{5,61},{6,62},{7,63},{8,0},{9,1... | collective-permute-start | bytes 786440 | tf_op jit(solution)/shard_map/ppermute | solution.py:32
  50.2 7.2 %collective-permute-start.14 = (bf16[4,2,32,2048]{3,2,1,0:T(8,128)(2,1)S(1)}, bf16[4,2,32,2048]{3,2,1,0:T(8,128)(2,1)S(1)}, u32[]{:S(2)}, u32[]{:S(2)}) collective-permute-start(bf16[4,2,32,2048]{3,2,1,0:T(8,128)(2,1)S(1)} %get-tuple-element.48.own), channel_id=1, source_target_pairs={{0,64},{1,65},{2,66},{3,67},{4,68},{5,69},{6,70},{7,71},{8,72},{9,... | collective-permute-start | bytes 3145736 | tf_op jit(solution)/shard_map/ppermute | solution.py:32
  50.3 7.1 %collective-permute-start.15 = (bf16[128,512]{1,0:T(8,128)(2,1)S(1)}, bf16[128,512]{1,0:T(8,128)(2,1)S(1)}, u32[]{:S(2)}, u32[]{:S(2)}) collective-permute-start(bf16[128,512]{1,0:T(8,128)(2,1)S(1)} %get-tuple-element.53), channel_id=1, source_target_pairs={{0,8},{1,9},{2,10},{3,11},{4,12},{5,13},{6,14},{7,15},{8,16},{9,17... | collective-permute-start | bytes 393224 | tf_op jit(solution)/shard_map/ppermute | solution.py:32
  50.4 7.0 %collective-permute-start.16 = (bf16[128,512]{1,0:T(8,128)(2,1)S(1)}, bf16[128,512]{1,0:T(8,128)(2,1)S(1)}, u32[]{:S(2)}, u32[]{:S(2)}) collective-permute-start(bf16[128,512]{1,0:T(8,128)(2,1)S(1)} %get-tuple-element.54), channel_id=1, source_target_pairs={{0,56},{1,57},{2,58},{3,59},{4,60},{5,61},{6,62},{7,63},{8,0},{9,1... | collective-permute-start | bytes 393224 | tf_op jit(solution)/shard_map/ppermute | solution.py:32
  57.5 20.6 %copy-start.1 = (s32[2,1]{0,1:T(1,128)S(1)}, s32[2,1]{0,1:T(1,128)}, u32[]{:S(2)}) copy-start(s32[2,1]{0,1:T(1,128)} %param.8) | copy-start | bytes 28
  76.2 24.7 %copy-start = (bf16[2048,512]{1,0:T(8,128)(2,1)S(1)}, bf16[2048,512]{1,0:T(8,128)(2,1)}, u32[]{:S(2)}) copy-start(bf16[2048,512]{1,0:T(8,128)(2,1)} %get-tuple-element.62.weight) | copy-start | bytes 6291460
  76.2 1.9 %collective-permute-start.17 = (bf16[16,32,512]{2,1,0:T(8,128)(2,1)S(1)}, bf16[16,32,512]{2,1,0:T(8,128)(2,1)S(1)}, u32[]{:S(2)}, u32[]{:S(2)}) collective-permute-start(bf16[16,32,512]{2,1,0:T(8,128)(2,1)S(1)} %all_to_all.26.own), channel_id=1, source_target_pairs={{0,64},{1,65},{2,66},{3,67},{4,68},{5,69},{6,70},{7,71},{8,72},{9,... | collective-permute-start | bytes 1572872 | tf_op jit(solution)/shard_map/ppermute | solution.py:32
  83.6 2.0 %collective-permute-start.18 = (bf16[2,32,4096]{2,1,0:T(8,128)(2,1)S(1)}, bf16[2,32,4096]{2,1,0:T(8,128)(2,1)S(1)}, u32[]{:S(2)}, u32[]{:S(2)}) collective-permute-start(bf16[2,32,4096]{2,1,0:T(8,128)(2,1)S(1)} %get-tuple-element.60), channel_id=1, source_target_pairs={{0,64},{1,65},{2,66},{3,67},{4,68},{5,69},{6,70},{7,71},{8,72},{9,... | collective-permute-start | bytes 1572872 | tf_op jit(solution)/shard_map/ppermute | solution.py:32
  103.6 2.8 %collective-permute-start.19 = (bf16[528,1024]{1,0:T(8,128)(2,1)S(1)}, bf16[528,1024]{1,0:T(8,128)(2,1)S(1)}, u32[]{:S(2)}, u32[]{:S(2)}) collective-permute-start(bf16[528,1024]{1,0:T(8,128)(2,1)S(1)} %get-tuple-element.66), channel_id=1, source_target_pairs={{0,64},{1,65},{2,66},{3,67},{4,68},{5,69},{6,70},{7,71},{8,72},{9,... | collective-permute-start | bytes 3244040 | tf_op jit(solution)/shard_map/ppermute | solution.py:32

commit v4 on v3

--- a/solution.py
+++ b/solution.py
@@ -311,40 +311,52 @@
             extra[...] = block
 
 
-def merge_body(keep, extra, received, out):
+def gains_body(extra, received, out):
     carried = received[512:, :].astype(F32)
     extras = extra[...] + carried[0:8] + carried[8:16]
     for xh in range(2):
-        span = slice(xh * 512, (xh + 1) * 512)
         block = jnp.concatenate(
             [
                 extras[2 * xh : 2 * xh + 1, :512],
                 extras[2 * xh : 2 * xh + 1, 512:],
                 extras[2 * xh + 1 : 2 * xh + 2, :512],
                 extras[2 * xh + 1 : 2 * xh + 2, 512:],
-                extras[4:5, span],
+                extras[4:5, xh * 512 : (xh + 1) * 512],
                 extras[5:6, :512],
                 jnp.zeros((2, 512), F32),
             ],
             axis=0,
         )
-        block = jnp.concatenate(high_low(block), axis=0)
+        for k in range(8):
+            out[xh * 8 + k] = block
+
+
+def merge_body(keep, received, gains, out, sums, row_sums):
+    total = gains[0]
+    for k in range(1, 16):
+        total += gains[k]
+    sums[...] = total
+    row_sums[...] = total[5:6]
+    for xh in range(2):
+        span = slice(xh * 512, (xh + 1) * 512)
         for k in range(8):
             for m in range(2):
                 place = (m * 8 + k) * 32
                 part = keep[place : place + 32, span] + received[place : place + 32, span].astype(F32)
                 out[xh * 8 + k, m * 32 : (m + 1) * 32, :] = part.astype(BF)
-            out[xh * 8 + k, 64:, :] = block
-
-
-def finish_body(received, states, factor, final_gain, gradient, sums, rows):
+
+
+def finish_body(received, states, factor, final_gain, row_totals, first, second, third,
+                gradient, final_gradient, layers_gradient, rows):
     xl, y = coordinates("xl", "y")
+    sums = first[...] + second[...] + third[...]
+    for i in range(4):
+        layers_gradient[:, i * 512 : (i + 1) * 512] = sums[i : i + 1]
+    final_gradient[...] = sums[4:5] / final_gain[...]
     total = received[0].astype(F32)
     for k in range(1, 16):
         total += received[k].astype(F32)
-    extras = total[64:72] + total[72:80]
-    sums[...] = jnp.broadcast_to(extras[None], (8, 8, 512))
-    rows[...] = jnp.transpose(jnp.broadcast_to(extras[5:6], (128, 512)))
+    rows[...] = jnp.transpose(jnp.broadcast_to(row_totals[...], (128, 512)))
     for m in range(2):
         span = slice(m * 32, (m + 1) * 32)
         row_sum = rows[lanes(m * 256 + (xl * 4 + y) * 32, 32), 0:1]
@@ -352,15 +364,6 @@
         scaled = total[span] * final_gain[...]
         wide = states[span, :].astype(F32)
         gradient[span, :] = scale * scaled - wide * (scale * scale * (row_sum / D))
-
-
-def close_body(received, final_gain, final_gradient, layers_gradient):
-    total = received[0]
-    for k in range(1, 8):
-        total += received[k]
-    for i in range(4):
-        layers_gradient[:, i * 512 : (i + 1) * 512] = total[i : i + 1]
-    final_gradient[...] = total[4:5] / final_gain[...]
 
 
 def per_device(
@@ -449,20 +452,23 @@
         far=(1,),
         near_outs=(0, 1, 2),
     )
-    (merged,) = kernel_call(
-        merge_body, (term_keep, extra, shift(term_send, core=1)), [((16, 80, 512), BF)], near_outs=(0,)
+    received = shift(term_send, core=1)
+    (gains,) = kernel_call(gains_body, (extra, received), [((16, 8, 512), F32)], near_outs=(0,))
+    gains = lax.all_to_all(gains, ("xh", "xl", "y"), 0, 0, tiled=True)
+    merged, sums, row_sums = kernel_call(
+        merge_body,
+        (term_keep, received, gains),
+        [((16, 64, 512), BF), ((8, 512), F32), ((1, 512), F32)],
+        near_outs=(0,),
     )
     merged = lax.all_to_all(merged, ("xh", "xl", "y"), 0, 0, tiled=True)
-    gradient, sums = kernel_call(
+    pair = sums + shift(sums, z=1)
+    triple = pair + shift(sums, z=-1)
+    gradient, final_gradient, layers_gradient = kernel_call(
         finish_body,
-        (merged, pack, factor, gain_row),
-        [((64, 512), F32), ((8, 8, 512), F32)],
+        (merged, pack, factor, gain_row, row_sums, triple, shift(triple, z=-3), shift(pair, z=2)),
+        [((64, 512), F32), ((1, 512), F32), ((1, D), F32)],
         [((512, 128), F32)],
-        near_outs=(1,),
-    )
-    sums = lax.all_to_all(sums, "z", 0, 0, tiled=True)
-    final_gradient, layers_gradient = kernel_call(
-        close_body, (sums, gain_row), [((1, 512), F32), ((1, D), F32)]
     )
     return (gradient.reshape(2, 32, 512), final_gradient[0], layers_gradient)
 

time: 145 us -> 141 us (0.972)
  blocking collectives: 79.4 us -> 54.4 us
  starting transfers between devices: 25.6 us -> 35.8 us
  waiting for transfers between devices: 23 us -> 32.8 us
    all_to_all x2 -> x1, blocking collectives: 36.9 us -> 11.9 us  [per_device(): gains = lax.all_to_all(gains, ('xh', 'xl', 'y'), 0, 0, tiled=True)]
    ppermute x20 -> x24, waiting for transfers between devices: 23 us -> 31.3 us  [shift(): return lax.ppermute(block, AXES, pairs)]
    all_to_all x0 -> x1, starting transfers between devices: none -> 5.11 us  [per_device(): merged = lax.all_to_all(merged, ('xh', 'xl', 'y'), 0, 0, tiled=True)]
    ppermute x20 -> x24, starting transfers between devices: 25.6 us -> 30.7 us  [shift(): return lax.ppermute(block, AXES, pairs)]
    all_to_all x0 -> x1, waiting for transfers between devices: none -> 1.57 us  [per_device(): merged = lax.all_to_all(merged, ('xh', 'xl', 'y'), 0, 0, tiled=True)]
  transfers between devices with their start and end apart: 20 -> 25, of which waited for: 11 -> 15; matrix products, arithmetic and copies ran while one was open for 0% -> 0% of each run, Pallas kernels for 1% -> 1%
where the time goes in v4:
time: 141 us
  blocking collectives  54.4 us (39%)
  starting transfers between devices  35.8 us (25%)
  waiting for transfers between devices  32.8 us (23%)
  Pallas kernels  16.7 us (12%)
    ppermute x24, waiting for transfers between devices, shift(): return lax.ppermute(block, AXES, pairs)  31.3 us
    ppermute x24, starting transfers between devices, shift(): return lax.ppermute(block, AXES, pairs)  30.7 us
    pallas_call x12, Pallas kernels, kernel_call(): pl.pallas_call(body, out_shape=[pltpu.HBM(s, d) if i in far_outs else plt...  16.7 us
    all_to_all x1, blocking collectives, per_device(): own_pairs = lax.all_to_all(projected, ('xh', 'xl', 'y'), 0, 0, tiled=True)  16.3 us
    all_to_all x1, blocking collectives, per_device(): joined = lax.all_to_all(joined, ('xh', 'xl', 'y'), 0, 0, tiled=True)  15.1 us
    all_to_all x1, blocking collectives, per_device(): gains = lax.all_to_all(gains, ('xh', 'xl', 'y'), 0, 0, tiled=True)  11.9 us
    all_to_all x1, blocking collectives, per_device(): lax.all_to_all(columns, ('xl', 'y'), 0, 0, tiled=True).reshape(256, 512)  11.1 us
    all_to_all x1, starting transfers between devices, per_device(): merged = lax.all_to_all(merged, ('xh', 'xl', 'y'), 0, 0, tiled=True)  5.11 us
  transfers between devices with their start and end apart: 25, of which 15 were waited for; matrix products, arithmetic and copies ran while one was open for 0% of the time, Pallas kernels for 1%

profile of v4, /device:TPU:8, one launch (start us, length us, event | category | flops | bytes accessed | tf_op | source)
XLA Modules:
  0.0 140.5 jit_solution(13729752616283375208)
XLA Ops:
  0.6 1.0 shard_map.94
  1.7 11.1 %all_to_all.25 = bf16[8,32,512]{2,1,0:T(8,128)(2,1)S(1)} all-to-all(bf16[8,32,512]{2,1,0:T(8,128)(2,1)S(1)} %get-tuple-element.41), channel_id=1, replica_groups=mesh['xh'=2,'core'=2,'z'=8,'xl'=2,'y'=4] {'xl','y'}, dimensions={0} | all-to-all | bytes 524288 | tf_op jit(solution)/shard_map/all_to_all | solution.py:380
  12.7 5.9 %collective-permute-start.4 = (bf16[256,512]{1,0:T(8,128)(2,1)S(1)}, bf16[256,512]{1,0:T(8,128)(2,1)S(1)}, u32[]{:S(2)}, u32[]{:S(2)}) collective-permute-start(bf16[256,512]{1,0:T(8,128)(2,1)S(1)} %bitcast.5), channel_id=1, source_target_pairs={{0,56},{1,57},{2,58},{3,59},{4,60},{5,61},{6,62},{7,63},{8,0},{9,1... | collective-permute-start | bytes 786440 | tf_op jit(solution)/shard_map/ppermute | solution.py:32
  18.6 0.5 collective-permute-start.2
  19.1 2.3 %collective-permute-start.1 = (bf16[80,512]{1,0:T(8,128)(2,1)S(1)}, bf16[80,512]{1,0:T(8,128)(2,1)S(1)}, u32[]{:S(2)}, u32[]{:S(2)}) collective-permute-start(bf16[80,512]{1,0:T(8,128)(2,1)S(1)} %get-tuple-element.40.p0.states), channel_id=1, source_target_pairs={{0,128},{1,129},{2,130},{3,131},{4,132},{5,133},{6,134},{7,135},{8... | collective-permute-start | bytes 245768 | tf_op jit(solution)/shard_map/ppermute | solution.py:32
  21.4 0.6 collective-permute-start
  22.0 2.9 %collective-permute-done.2.p3 = bf16[80,512]{1,0:T(8,128)(2,1)S(1)} collective-permute-done((bf16[80,512]{1,0:T(8,128)(2,1)S(1)}, bf16[80,512]{1,0:T(8,128)(2,1)S(1)}, u32[]{:S(2)}, u32[]{:S(2)}) %collective-permute-start.2) | collective-permute-done | bytes 81952 | tf_op jit(solution)/shard_map/ppermute | solution.py:32
  24.8 0.7 collective-permute-done.1.p2
  25.5 0.7 collective-permute-done.3.ahead_in
  26.2 1.1 shard_map.95
  27.3 1.9 %collective-permute-start.8 = (bf16[32,2048]{1,0:T(8,128)(2,1)S(1)}, bf16[32,2048]{1,0:T(8,128)(2,1)S(1)}, u32[]{:S(2)}, u32[]{:S(2)}) collective-permute-start(bf16[32,2048]{1,0:T(8,128)(2,1)S(1)} %get-tuple-element.42.half), channel_id=1, source_target_pairs={{0,3},{1,0},{2,1},{3,2},{4,7},{5,4},{6,5},{7,6},{8,11},{9,8},{10,9... | collective-permute-start | bytes 393224 | tf_op jit(solution)/shard_map/ppermute | solution.py:32
  29.1 3.2 %collective-permute-start.10 = (bf16[256,512]{1,0:T(8,128)(2,1)S(1)}, bf16[256,512]{1,0:T(8,128)(2,1)S(1)}, u32[]{:S(2)}, u32[]{:S(2)}) collective-permute-start(bf16[256,512]{1,0:T(8,128)(2,1)S(1)} %get-tuple-element.44.refs_2_), channel_id=1, source_target_pairs={{0,56},{1,57},{2,58},{3,59},{4,60},{5,61},{6,62},{7,63},{8,0},{9,1... | collective-permute-start | bytes 786440 | tf_op jit(solution)/shard_map/ppermute | solution.py:32
  32.4 0.6 collective-permute-start.7
  32.9 1.9 %collective-permute-start.6 = (bf16[32,2048]{1,0:T(8,128)(2,1)S(1)}, bf16[32,2048]{1,0:T(8,128)(2,1)S(1)}, u32[]{:S(2)}, u32[]{:S(2)}) collective-permute-start(bf16[32,2048]{1,0:T(8,128)(2,1)S(1)} %get-tuple-element.42.half), channel_id=1, source_target_pairs={{0,1},{1,2},{2,3},{3,0},{4,5},{5,6},{6,7},{7,4},{8,9},{9,10},{10,1... | collective-permute-start | bytes 393224 | tf_op jit(solution)/shard_map/ppermute | solution.py:32
  34.8 1.1 collective-permute-start.5
  35.9 2.9 %collective-permute-done.7.p2 = bf16[32,2048]{1,0:T(8,128)(2,1)S(1)} collective-permute-done((bf16[32,2048]{1,0:T(8,128)(2,1)S(1)}, bf16[32,2048]{1,0:T(8,128)(2,1)S(1)}, u32[]{:S(2)}, u32[]{:S(2)}) %collective-permute-start.7) | collective-permute-done | bytes 131104 | tf_op jit(solution)/shard_map/ppermute | solution.py:32
  38.8 1.5 %collective-permute-done.6.p1 = bf16[32,2048]{1,0:T(8,128)(2,1)S(1)} collective-permute-done((bf16[32,2048]{1,0:T(8,128)(2,1)S(1)}, bf16[32,2048]{1,0:T(8,128)(2,1)S(1)}, u32[]{:S(2)}, u32[]{:S(2)}) %collective-permute-start.6) | collective-permute-done | bytes 131104 | tf_op jit(solution)/shard_map/ppermute | solution.py:32
  40.4 0.8 collective-permute-start.11
  41.2 3.2 %collective-permute-start.13 = (bf16[256,512]{1,0:T(8,128)(2,1)S(1)}, bf16[256,512]{1,0:T(8,128)(2,1)S(1)}, u32[]{:S(2)}, u32[]{:S(2)}) collective-permute-start(bf16[256,512]{1,0:T(8,128)(2,1)S(1)} %get-tuple-element.49.refs_4_), channel_id=1, source_target_pairs={{0,56},{1,57},{2,58},{3,59},{4,60},{5,61},{6,62},{7,63},{8,0},{9,1... | collective-permute-start | bytes 786440 | tf_op jit(solution)/shard_map/ppermute | solution.py:32
  44.4 4.3 %collective-permute-done.12.ahead_in = bf16[256,512]{1,0:T(8,128)(2,1)S(1)} collective-permute-done((bf16[256,512]{1,0:T(8,128)(2,1)S(1)}, bf16[256,512]{1,0:T(8,128)(2,1)S(1)}, u32[]{:S(2)}, u32[]{:S(2)}) %collective-permute-start.12) | collective-permute-done | bytes 262176 | tf_op jit(solution)/shard_map/ppermute | solution.py:32
  48.8 1.4 collective-permute-done.11.beyond
  50.1 0.1 shard_map.97
  50.2 0.1 collective-permute-start.14
  50.3 0.1 collective-permute-start.15
  50.4 3.2 %collective-permute-start.16 = (bf16[128,512]{1,0:T(8,128)(2,1)S(1)}, bf16[128,512]{1,0:T(8,128)(2,1)S(1)}, u32[]{:S(2)}, u32[]{:S(2)}) collective-permute-start(bf16[128,512]{1,0:T(8,128)(2,1)S(1)} %get-tuple-element.56), channel_id=1, source_target_pairs={{0,56},{1,57},{2,58},{3,59},{4,60},{5,61},{6,62},{7,63},{8,0},{9,1... | collective-permute-start | bytes 393224 | tf_op jit(solution)/shard_map/ppermute | solution.py:32
  53.7 1.6 %shard_map.98 = (bf16[2,8,32,2048]{3,2,1,0:T(8,128)(2,1)}, bf16[2048,512]{1,0:T(8,128)(2,1)}) custom-call(bf16[4,2,32,2048]{3,2,1,0:T(8,128)(2,1)S(1)} %get-tuple-element.50.own, bf16[256,512]{1,0:T(8,128)(2,1)S(1)} %bitcast.7, bf16[256,512]{1,0:T(8,128)(2,1)S(1)} %get-tuple-element.43.refs_1_, bf16[256,512]{1,0:T(8,128)(2,1)S(1)} %get-tuple-element.44.refs_2_, ...), custom_call_target="tpu_custom_call" | custom-call | tf_op jit(solution)/shard_map/pallas_call | solution.py:40
  55.3 2.2 %collective-permute-done.15.refs_7_ = bf16[128,512]{1,0:T(8,128)(2,1)S(1)} collective-permute-done((bf16[128,512]{1,0:T(8,128)(2,1)S(1)}, bf16[128,512]{1,0:T(8,128)(2,1)S(1)}, u32[]{:S(2)}, u32[]{:S(2)}) %collective-permute-start.15) | collective-permute-done | bytes 131104 | tf_op jit(solution)/shard_map/ppermute | solution.py:32
  57.5 2.4 %shard_map.99 = (bf16[2,8,32,2048]{3,2,1,0:T(8,128)(2,1)}, bf16[2048,512]{1,0:T(8,128)(2,1)}, bf16[16,32,512]{2,1,0:T(8,128)(2,1)S(1)}) custom-call(bf16[2,8,32,2048]{3,2,1,0:T(8,128)(2,1)} %get-tuple-element.51.held_in, bf16[2048,512]{1,0:T(8,128)(2,1)} %get-tuple-element.52.weight_in, ...), custom_call_target="tpu_custom_call", output_to_operand_aliasing={{0}: (0, {}), {1}: (1, {})} | custom-call | tf_op jit(solution)/shard_map/pallas_call | solution.py:40
  59.8 16.3 %all_to_all.26.own = bf16[16,32,512]{2,1,0:T(8,128)(2,1)S(1)} all-to-all(bf16[16,32,512]{2,1,0:T(8,128)(2,1)S(1)} %get-tuple-element.57), channel_id=1, replica_groups=mesh['xh'=2,'core'=2,'z'=8,'xl'=2,'y'=4] {'xh','xl','y'}, dimensions={0} | all-to-all | bytes 1048576 | tf_op jit(solution)/shard_map/all_to_all | solution.py:423
  76.2 1.9 %collective-permute-done.17.other = bf16[16,32,512]{2,1,0:T(8,128)(2,1)S(1)} collective-permute-done((bf16[16,32,512]{2,1,0:T(8,128)(2,1)S(1)}, bf16[16,32,512]{2,1,0:T(8,128)(2,1)S(1)}, u32[]{:S(2)}, u32[]{:S(2)}) %collective-permute-start.17) | collective-permute-done | bytes 524320 | tf_op jit(solution)/shard_map/ppermute | solution.py:32
  78.1 5.6 %shard_map.100 = (bf16[2,32,4096]{2,1,0:T(8,128)(2,1)S(1)}, bf16[2,32,4096]{2,1,0:T(8,128)(2,1)S(1)}, f32[4,1,2048]{2,1,0:T(1,128)S(1)}) custom-call(s32[1,2]{1,0:T(1,128)S(1)} %bitcast.9, bf16[16,32,512]{2,1,0:T(8,128)(2,1)S(1)} %all_to_all.26.own, bf16[16,32,512]{2,1,0:T(8,128)(2,1)S(1)} %collective-permute-done.17.other, ...), custom_call_target="tpu_custom_call" | custom-call | tf_op jit(solution)/shard_map/pallas_call | solution.py:40
  83.7 0.3 collective-permute-start.18
  83.9 1.7 %collective-permute-done.18.received = bf16[2,32,4096]{2,1,0:T(8,128)(2,1)S(1)} collective-permute-done((bf16[2,32,4096]{2,1,0:T(8,128)(2,1)S(1)}, bf16[2,32,4096]{2,1,0:T(8,128)(2,1)S(1)}, u32[]{:S(2)}, u32[]{:S(2)}) %collective-permute-start.18) | collective-permute-done | bytes 524320 | tf_op jit(solution)/shard_map/ppermute | solution.py:32
  85.6 0.1 shard_map.101
  85.8 15.1 %all_to_all.27.gradient = bf16[16,32,512]{2,1,0:T(8,128)(2,1)S(1)} all-to-all(bf16[16,32,512]{2,1,0:T(8,128)(2,1)S(1)} %shard_map.101), channel_id=1, replica_groups=mesh['xh'=2,'core'=2,'z'=8,'xl'=2,'y'=4] {'xh','xl','y'}, dimensions={0} | all-to-all | bytes 1048576 | tf_op jit(solution)/shard_map/all_to_all | solution.py:440
  100.9 2.7 %shard_map.102 = (f32[512,1024]{1,0:T(8,128)S(1)}, f32[8,1024]{1,0:T(8,128)S(1)}, bf16[528,1024]{1,0:T(8,128)(2,1)S(1)}) custom-call(bf16[16,32,512]{2,1,0:T(8,128)(2,1)S(1)} %all_to_all.27.gradient, bf16[2,8,32,2048]{3,2,1,0:T(8,128)(2,1)} %get-tuple-element.63.held_far, bf16[2048,512]{1,0:T(8,128)(2,1)S(1)} %copy-done, ...), custom_call_target="tpu_custom_call" | custom-call | tf_op jit(solution)/shard_map/pallas_call | solution.py:40
  103.6 0.1 collective-permute-start.19
  103.7 2.7 %collective-permute-done.19.received = bf16[528,1024]{1,0:T(8,128)(2,1)S(1)} collective-permute-done((bf16[528,1024]{1,0:T(8,128)(2,1)S(1)}, bf16[528,1024]{1,0:T(8,128)(2,1)S(1)}, u32[]{:S(2)}, u32[]{:S(2)}) %collective-permute-start.19) | collective-permute-done | bytes 1081376 | tf_op jit(solution)/shard_map/ppermute | solution.py:32
  106.4 11.9 %all_to_all.28.gains = f32[16,8,512]{2,1,0:T(8,128)S(1)} all-to-all(f32[16,8,512]{2,1,0:T(8,128)S(1)} %shard_map.103), channel_id=1, replica_groups=mesh['xh'=2,'core'=2,'z'=8,'xl'=2,'y'=4] {'xh','xl','y'}, dimensions={0} | all-to-all | bytes 524288 | tf_op jit(solution)/shard_map/all_to_all | solution.py:457
  118.3 1.2 shard_map.104
  119.5 5.1 %all-to-all-start.4 = ((bf16[16,64,512]{2,1,0:T(8,128)(2,1)}), bf16[16,64,512]{2,1,0:T(8,128)(2,1)S(1)}, u32[]{:S(2)}, u32[]{:S(2)}) async-start(bf16[16,64,512]{2,1,0:T(8,128)(2,1)} %get-tuple-element.69), calls=%async_computation.4 | async-start | bytes 2097152 | tf_op jit(solution)/shard_map/all_to_all | solution.py:464
  124.7 2.6 %collective-permute-start.21 = (f32[8,512]{1,0:T(8,128)S(1)}, f32[8,512]{1,0:T(8,128)S(1)}, u32[]{:S(2)}, u32[]{:S(2)}) collective-permute-start(f32[8,512]{1,0:T(8,128)S(1)} %get-tuple-element.73), channel_id=1, source_target_pairs={{0,56},{1,57},{2,58},{3,59},{4,60},{5,61},{6,62},{7,63},{8,0},{9,1... | collective-permute-start | bytes 49160 | tf_op jit(solution)/shard_map/ppermute | solution.py:32
  127.2 1.4 %collective-permute-done.21 = f32[8,512]{1,0:T(8,128)S(1)} collective-permute-done((f32[8,512]{1,0:T(8,128)S(1)}, f32[8,512]{1,0:T(8,128)S(1)}, u32[]{:S(2)}, u32[]{:S(2)}) %collective-permute-start.21) | collective-permute-done | bytes 16416 | tf_op jit(solution)/shard_map/ppermute | solution.py:32
  128.7 3.5 %collective-permute-done.20 = f32[8,512]{1,0:T(8,128)S(1)} collective-permute-done((f32[8,512]{1,0:T(8,128)S(1)}, f32[8,512]{1,0:T(8,128)S(1)}, u32[]{:S(2)}, u32[]{:S(2)}) %collective-permute-start.20) | collective-permute-done | bytes 16416 | tf_op jit(solution)/shard_map/ppermute | solution.py:32
  132.2 2.4 %collective-permute-start.22 = (f32[8,512]{1,0:T(8,128)S(1)}, f32[8,512]{1,0:T(8,128)S(1)}, u32[]{:S(2)}, u32[]{:S(2)}) collective-permute-start(f32[8,512]{1,0:T(8,128)S(1)} %get-tuple-element.77.first), channel_id=1, source_target_pairs={{0,40},{1,41},{2,42},{3,43},{4,44},{5,45},{6,46},{7,47},{8,48},{9,... | collective-permute-start | bytes 49160 | tf_op jit(solution)/shard_map/ppermute | solution.py:32
  134.6 3.4 %collective-permute-done.23.third = f32[8,512]{1,0:T(8,128)S(1)} collective-permute-done((f32[8,512]{1,0:T(8,128)S(1)}, f32[8,512]{1,0:T(8,128)S(1)}, u32[]{:S(2)}, u32[]{:S(2)}) %collective-permute-start.23) | collective-permute-done | bytes 16416 | tf_op jit(solution)/shard_map/ppermute | solution.py:32
  138.0 1.6 %all-to-all-done.4.received = bf16[16,64,512]{2,1,0:T(8,128)(2,1)S(1)} async-done(((bf16[16,64,512]{2,1,0:T(8,128)(2,1)}), bf16[16,64,512]{2,1,0:T(8,128)(2,1)S(1)}, u32[]{:S(2)}, u32[]{:S(2)}) %all-to-all-start.4) | async-done | bytes 1048608 | tf_op jit(solution)/shard_map/all_to_all | solution.py:464
  139.6 0.9 shard_map.105
  (23 shorter events, 0.1 us)
Async XLA Ops:
  12.7 12.8 %collective-permute-start.4 = (bf16[256,512]{1,0:T(8,128)(2,1)S(1)}, bf16[256,512]{1,0:T(8,128)(2,1)S(1)}, u32[]{:S(2)}, u32[]{:S(2)}) collective-permute-start(bf16[256,512]{1,0:T(8,128)(2,1)S(1)} %bitcast.5), channel_id=1, source_target_pairs={{0,56},{1,57},{2,58},{3,59},{4,60},{5,61},{6,62},{7,63},{8,0},{9,1... | collective-permute-start | bytes 786440 | tf_op jit(solution)/shard_map/ppermute | solution.py:32
  18.6 7.6 %collective-permute-start.3 = (bf16[256,512]{1,0:T(8,128)(2,1)S(1)}, bf16[256,512]{1,0:T(8,128)(2,1)S(1)}, u32[]{:S(2)}, u32[]{:S(2)}) collective-permute-start(bf16[256,512]{1,0:T(8,128)(2,1)S(1)} %bitcast.6), channel_id=1, source_target_pairs={{0,8},{1,9},{2,10},{3,11},{4,12},{5,13},{6,14},{7,15},{8,16},{9,17... | collective-permute-start | bytes 786440 | tf_op jit(solution)/shard_map/ppermute | solution.py:32
  18.6 6.2 %collective-permute-start.2 = (bf16[80,512]{1,0:T(8,128)(2,1)S(1)}, bf16[80,512]{1,0:T(8,128)(2,1)S(1)}, u32[]{:S(2)}, u32[]{:S(2)}) collective-permute-start(bf16[80,512]{1,0:T(8,128)(2,1)S(1)} %get-tuple-element.40.p0.states), channel_id=1, source_target_pairs={{0,192},{1,193},{2,194},{3,195},{4,196},{5,197},{6,198},{7,199},{8... | collective-permute-start | bytes 245768 | tf_op jit(solution)/shard_map/ppermute | solution.py:32
  19.1 6.4 %collective-permute-start.1 = (bf16[80,512]{1,0:T(8,128)(2,1)S(1)}, bf16[80,512]{1,0:T(8,128)(2,1)S(1)}, u32[]{:S(2)}, u32[]{:S(2)}) collective-permute-start(bf16[80,512]{1,0:T(8,128)(2,1)S(1)} %get-tuple-element.40.p0.states), channel_id=1, source_target_pairs={{0,128},{1,129},{2,130},{3,131},{4,132},{5,133},{6,134},{7,135},{8... | collective-permute-start | bytes 245768 | tf_op jit(solution)/shard_map/ppermute | solution.py:32
  21.4 4.1 %collective-permute-start = (bf16[80,512]{1,0:T(8,128)(2,1)S(1)}, bf16[80,512]{1,0:T(8,128)(2,1)S(1)}, u32[]{:S(2)}, u32[]{:S(2)}) collective-permute-start(bf16[80,512]{1,0:T(8,128)(2,1)S(1)} %get-tuple-element.40.p0.states), channel_id=1, source_target_pairs={{0,64},{1,65},{2,66},{3,67},{4,68},{5,69},{6,70},{7,71},{8,72},{9,... | collective-permute-start | bytes 245768 | tf_op jit(solution)/shard_map/ppermute | solution.py:32
  27.3 7.6 %collective-permute-start.8 = (bf16[32,2048]{1,0:T(8,128)(2,1)S(1)}, bf16[32,2048]{1,0:T(8,128)(2,1)S(1)}, u32[]{:S(2)}, u32[]{:S(2)}) collective-permute-start(bf16[32,2048]{1,0:T(8,128)(2,1)S(1)} %get-tuple-element.42.half), channel_id=1, source_target_pairs={{0,3},{1,0},{2,1},{3,2},{4,7},{5,4},{6,5},{7,6},{8,11},{9,8},{10,9... | collective-permute-start | bytes 393224 | tf_op jit(solution)/shard_map/ppermute | solution.py:32
  29.1 11.2 %collective-permute-start.9 = (bf16[256,512]{1,0:T(8,128)(2,1)S(1)}, bf16[256,512]{1,0:T(8,128)(2,1)S(1)}, u32[]{:S(2)}, u32[]{:S(2)}) collective-permute-start(bf16[256,512]{1,0:T(8,128)(2,1)S(1)} %get-tuple-element.43.refs_1_), channel_id=1, source_target_pairs={{0,8},{1,9},{2,10},{3,11},{4,12},{5,13},{6,14},{7,15},{8,16},{9,17... | collective-permute-start | bytes 786440 | tf_op jit(solution)/shard_map/ppermute | solution.py:32
  29.1 11.2 %collective-permute-start.10 = (bf16[256,512]{1,0:T(8,128)(2,1)S(1)}, bf16[256,512]{1,0:T(8,128)(2,1)S(1)}, u32[]{:S(2)}, u32[]{:S(2)}) collective-permute-start(bf16[256,512]{1,0:T(8,128)(2,1)S(1)} %get-tuple-element.44.refs_2_), channel_id=1, source_target_pairs={{0,56},{1,57},{2,58},{3,59},{4,60},{5,61},{6,62},{7,63},{8,0},{9,1... | collective-permute-start | bytes 786440 | tf_op jit(solution)/shard_map/ppermute | solution.py:32
  32.4 6.5 %collective-permute-start.7 = (bf16[32,2048]{1,0:T(8,128)(2,1)S(1)}, bf16[32,2048]{1,0:T(8,128)(2,1)S(1)}, u32[]{:S(2)}, u32[]{:S(2)}) collective-permute-start(bf16[32,2048]{1,0:T(8,128)(2,1)S(1)} %get-tuple-element.42.half), channel_id=1, source_target_pairs={{0,2},{1,3},{2,0},{3,1},{4,6},{5,7},{6,4},{7,5},{8,10},{9,11},{10,... | collective-permute-start | bytes 393224 | tf_op jit(solution)/shard_map/ppermute | solution.py:32
  32.9 7.4 %collective-permute-start.6 = (bf16[32,2048]{1,0:T(8,128)(2,1)S(1)}, bf16[32,2048]{1,0:T(8,128)(2,1)S(1)}, u32[]{:S(2)}, u32[]{:S(2)}) collective-permute-start(bf16[32,2048]{1,0:T(8,128)(2,1)S(1)} %get-tuple-element.42.half), channel_id=1, source_target_pairs={{0,1},{1,2},{2,3},{3,0},{4,5},{5,6},{6,7},{7,4},{8,9},{9,10},{10,1... | collective-permute-start | bytes 393224 | tf_op jit(solution)/shard_map/ppermute | solution.py:32
  34.8 5.5 %collective-permute-start.5 = (bf16[32,2048]{1,0:T(8,128)(2,1)S(1)}, bf16[32,2048]{1,0:T(8,128)(2,1)S(1)}, u32[]{:S(2)}, u32[]{:S(2)}) collective-permute-start(bf16[32,2048]{1,0:T(8,128)(2,1)S(1)} %get-tuple-element.42.half), channel_id=1, source_target_pairs={{0,4},{1,5},{2,6},{3,7},{4,0},{5,1},{6,2},{7,3},{8,12},{9,13},{10,... | collective-permute-start | bytes 393224 | tf_op jit(solution)/shard_map/ppermute | solution.py:32
  40.4 9.7 %collective-permute-start.11 = (bf16[3,32,2048]{2,1,0:T(8,128)(2,1)S(1)}, bf16[3,32,2048]{2,1,0:T(8,128)(2,1)S(1)}, u32[]{:S(2)}, u32[]{:S(2)}) collective-permute-start(bf16[3,32,2048]{2,1,0:T(8,128)(2,1)S(1)} %get-tuple-element.47), channel_id=1, source_target_pairs={{0,4},{1,5},{2,6},{3,7},{4,0},{5,1},{6,2},{7,3},{8,12},{9,13},{10,... | collective-permute-start | bytes 1179656 | tf_op jit(solution)/shard_map/ppermute | solution.py:32
  41.2 7.6 %collective-permute-start.12 = (bf16[256,512]{1,0:T(8,128)(2,1)S(1)}, bf16[256,512]{1,0:T(8,128)(2,1)S(1)}, u32[]{:S(2)}, u32[]{:S(2)}) collective-permute-start(bf16[256,512]{1,0:T(8,128)(2,1)S(1)} %get-tuple-element.48.refs_3_), channel_id=1, source_target_pairs={{0,8},{1,9},{2,10},{3,11},{4,12},{5,13},{6,14},{7,15},{8,16},{9,17... | collective-permute-start | bytes 786440 | tf_op jit(solution)/shard_map/ppermute | solution.py:32
  41.2 7.6 %collective-permute-start.13 = (bf16[256,512]{1,0:T(8,128)(2,1)S(1)}, bf16[256,512]{1,0:T(8,128)(2,1)S(1)}, u32[]{:S(2)}, u32[]{:S(2)}) collective-permute-start(bf16[256,512]{1,0:T(8,128)(2,1)S(1)} %get-tuple-element.49.refs_4_), channel_id=1, source_target_pairs={{0,56},{1,57},{2,58},{3,59},{4,60},{5,61},{6,62},{7,63},{8,0},{9,1... | collective-permute-start | bytes 786440 | tf_op jit(solution)/shard_map/ppermute | solution.py:32
  50.2 7.2 %collective-permute-start.14 = (bf16[4,2,32,2048]{3,2,1,0:T(8,128)(2,1)S(1)}, bf16[4,2,32,2048]{3,2,1,0:T(8,128)(2,1)S(1)}, u32[]{:S(2)}, u32[]{:S(2)}) collective-permute-start(bf16[4,2,32,2048]{3,2,1,0:T(8,128)(2,1)S(1)} %get-tuple-element.50.own), channel_id=1, source_target_pairs={{0,64},{1,65},{2,66},{3,67},{4,68},{5,69},{6,70},{7,71},{8,72},{9,... | collective-permute-start | bytes 3145736 | tf_op jit(solution)/shard_map/ppermute | solution.py:32
  50.3 7.1 %collective-permute-start.15 = (bf16[128,512]{1,0:T(8,128)(2,1)S(1)}, bf16[128,512]{1,0:T(8,128)(2,1)S(1)}, u32[]{:S(2)}, u32[]{:S(2)}) collective-permute-start(bf16[128,512]{1,0:T(8,128)(2,1)S(1)} %get-tuple-element.55), channel_id=1, source_target_pairs={{0,8},{1,9},{2,10},{3,11},{4,12},{5,13},{6,14},{7,15},{8,16},{9,17... | collective-permute-start | bytes 393224 | tf_op jit(solution)/shard_map/ppermute | solution.py:32
  50.4 7.0 %collective-permute-start.16 = (bf16[128,512]{1,0:T(8,128)(2,1)S(1)}, bf16[128,512]{1,0:T(8,128)(2,1)S(1)}, u32[]{:S(2)}, u32[]{:S(2)}) collective-permute-start(bf16[128,512]{1,0:T(8,128)(2,1)S(1)} %get-tuple-element.56), channel_id=1, source_target_pairs={{0,56},{1,57},{2,58},{3,59},{4,60},{5,61},{6,62},{7,63},{8,0},{9,1... | collective-permute-start | bytes 393224 | tf_op jit(solution)/shard_map/ppermute | solution.py:32
  57.5 20.6 %copy-start.1 = (s32[2,1]{0,1:T(1,128)S(1)}, s32[2,1]{0,1:T(1,128)}, u32[]{:S(2)}) copy-start(s32[2,1]{0,1:T(1,128)} %param.8) | copy-start | bytes 28
  76.2 24.7 %copy-start = (bf16[2048,512]{1,0:T(8,128)(2,1)S(1)}, bf16[2048,512]{1,0:T(8,128)(2,1)}, u32[]{:S(2)}) copy-start(bf16[2048,512]{1,0:T(8,128)(2,1)} %get-tuple-element.64.weight) | copy-start | bytes 6291460
  76.2 1.9 %collective-permute-start.17 = (bf16[16,32,512]{2,1,0:T(8,128)(2,1)S(1)}, bf16[16,32,512]{2,1,0:T(8,128)(2,1)S(1)}, u32[]{:S(2)}, u32[]{:S(2)}) collective-permute-start(bf16[16,32,512]{2,1,0:T(8,128)(2,1)S(1)} %all_to_all.26.own), channel_id=1, source_target_pairs={{0,64},{1,65},{2,66},{3,67},{4,68},{5,69},{6,70},{7,71},{8,72},{9,... | collective-permute-start | bytes 1572872 | tf_op jit(solution)/shard_map/ppermute | solution.py:32
  83.7 2.0 %collective-permute-start.18 = (bf16[2,32,4096]{2,1,0:T(8,128)(2,1)S(1)}, bf16[2,32,4096]{2,1,0:T(8,128)(2,1)S(1)}, u32[]{:S(2)}, u32[]{:S(2)}) collective-permute-start(bf16[2,32,4096]{2,1,0:T(8,128)(2,1)S(1)} %get-tuple-element.62), channel_id=1, source_target_pairs={{0,64},{1,65},{2,66},{3,67},{4,68},{5,69},{6,70},{7,71},{8,72},{9,... | collective-permute-start | bytes 1572872 | tf_op jit(solution)/shard_map/ppermute | solution.py:32
  103.6 2.8 %collective-permute-start.19 = (bf16[528,1024]{1,0:T(8,128)(2,1)S(1)}, bf16[528,1024]{1,0:T(8,128)(2,1)S(1)}, u32[]{:S(2)}, u32[]{:S(2)}) collective-permute-start(bf16[528,1024]{1,0:T(8,128)(2,1)S(1)} %get-tuple-element.67), channel_id=1, source_target_pairs={{0,64},{1,65},{2,66},{3,67},{4,68},{5,69},{6,70},{7,71},{8,72},{9,... | collective-permute-start | bytes 3244040 | tf_op jit(solution)/shard_map/ppermute | solution.py:32
  119.5 20.1 %all-to-all-start.4 = ((bf16[16,64,512]{2,1,0:T(8,128)(2,1)}), bf16[16,64,512]{2,1,0:T(8,128)(2,1)S(1)}, u32[]{:S(2)}, u32[]{:S(2)}) async-start(bf16[16,64,512]{2,1,0:T(8,128)(2,1)} %get-tuple-element.69), calls=%async_computation.4 | async-start | bytes 2097152 | tf_op jit(solution)/shard_map/all_to_all | solution.py:464
  124.7 4.0 %collective-permute-start.21 = (f32[8,512]{1,0:T(8,128)S(1)}, f32[8,512]{1,0:T(8,128)S(1)}, u32[]{:S(2)}, u32[]{:S(2)}) collective-permute-start(f32[8,512]{1,0:T(8,128)S(1)} %get-tuple-element.73), channel_id=1, source_target_pairs={{0,56},{1,57},{2,58},{3,59},{4,60},{5,61},{6,62},{7,63},{8,0},{9,1... | collective-permute-start | bytes 49160 | tf_op jit(solution)/shard_map/ppermute | solution.py:32
  127.2 4.9 %collective-permute-start.20 = (f32[8,512]{1,0:T(8,128)S(1)}, f32[8,512]{1,0:T(8,128)S(1)}, u32[]{:S(2)}, u32[]{:S(2)}) collective-permute-start(f32[8,512]{1,0:T(8,128)S(1)} %get-tuple-element.73), channel_id=1, source_target_pairs={{0,8},{1,9},{2,10},{3,11},{4,12},{5,13},{6,14},{7,15},{8,16},{9,17... | collective-permute-start | bytes 49160 | tf_op jit(solution)/shard_map/ppermute | solution.py:32
  132.2 5.8 %collective-permute-start.23 = (f32[8,512]{1,0:T(8,128)S(1)}, f32[8,512]{1,0:T(8,128)S(1)}, u32[]{:S(2)}, u32[]{:S(2)}) collective-permute-start(f32[8,512]{1,0:T(8,128)S(1)} %get-tuple-element.78), channel_id=1, source_target_pairs={{0,16},{1,17},{2,18},{3,19},{4,20},{5,21},{6,22},{7,23},{8,24},{9,... | collective-permute-start | bytes 49160 | tf_op jit(solution)/shard_map/ppermute | solution.py:32
  132.2 5.8 %collective-permute-start.22 = (f32[8,512]{1,0:T(8,128)S(1)}, f32[8,512]{1,0:T(8,128)S(1)}, u32[]{:S(2)}, u32[]{:S(2)}) collective-permute-start(f32[8,512]{1,0:T(8,128)S(1)} %get-tuple-element.77.first), channel_id=1, source_target_pairs={{0,40},{1,41},{2,42},{3,43},{4,44},{5,45},{6,46},{7,47},{8,48},{9,... | collective-permute-start | bytes 49160 | tf_op jit(solution)/shard_map/ppermute | solution.py:32

commit v5 on v4

--- a/solution.py
+++ b/solution.py
@@ -264,12 +264,7 @@
             out[xh * 8 + k] = total.astype(BF)
 
 
-def high_low(part):
-    high = part.astype(BF)
-    return high, (part - high.astype(F32)).astype(BF)
-
-
-def back_body(gradient, held_far, weight, gain_parts, keep, extra, send, terms, parts, rows, held, sem):
+def back_body(gradient, held_far, weight, gain_parts, keep, extra, extra_send, send, terms, parts, rows, held, sem):
     (c,) = coordinates("core")
     copy = pltpu.make_async_copy(held_far, held, sem)
     copy.start()
@@ -302,31 +297,32 @@
         for i in range(2):
             part = terms[:, lanes((2 * i + parity) * 512, 512)]
             if is_send:
-                send[:512, i * 512 : (i + 1) * 512] = part.astype(BF)
+                send[:, i * 512 : (i + 1) * 512] = part.astype(BF)
             else:
                 keep[:, i * 512 : (i + 1) * 512] = part
         if is_send:
-            send[512:, :] = jnp.concatenate(high_low(block), axis=0)
+            extra_send[...] = block
         else:
             extra[...] = block
 
 
+def flatten(block):
+    return jnp.concatenate([block[i : i + 1] for i in range(8)], axis=1)
+
+
 def gains_body(extra, received, out):
-    carried = received[512:, :].astype(F32)
-    extras = extra[...] + carried[0:8] + carried[8:16]
+    extras = extra[...] + received[...]
     for xh in range(2):
-        block = jnp.concatenate(
+        flat = jnp.concatenate(
             [
-                extras[2 * xh : 2 * xh + 1, :512],
-                extras[2 * xh : 2 * xh + 1, 512:],
-                extras[2 * xh + 1 : 2 * xh + 2, :512],
-                extras[2 * xh + 1 : 2 * xh + 2, 512:],
+                extras[2 * xh : 2 * xh + 1],
+                extras[2 * xh + 1 : 2 * xh + 2],
                 extras[4:5, xh * 512 : (xh + 1) * 512],
                 extras[5:6, :512],
-                jnp.zeros((2, 512), F32),
             ],
-            axis=0,
+            axis=1,
         )
+        block = jnp.concatenate([flat[:, i * 384 : (i + 1) * 384] for i in range(8)], axis=0)
         for k in range(8):
             out[xh * 8 + k] = block
 
@@ -336,7 +332,7 @@
     for k in range(1, 16):
         total += gains[k]
     sums[...] = total
-    row_sums[...] = total[5:6]
+    row_sums[...] = flatten(total)[:, 2560:]
     for xh in range(2):
         span = slice(xh * 512, (xh + 1) * 512)
         for k in range(8):
@@ -350,9 +346,9 @@
                 gradient, final_gradient, layers_gradient, rows):
     xl, y = coordinates("xl", "y")
     sums = first[...] + second[...] + third[...]
-    for i in range(4):
-        layers_gradient[:, i * 512 : (i + 1) * 512] = sums[i : i + 1]
-    final_gradient[...] = sums[4:5] / final_gain[...]
+    flat = flatten(sums)
+    layers_gradient[...] = flat[:, :D]
+    final_gradient[...] = flat[:, D:2560] / final_gain[...]
     total = received[0].astype(F32)
     for k in range(1, 16):
         total += received[k].astype(F32)
@@ -438,10 +434,10 @@
     )
     (joined,) = kernel_call(join_body, (keep, shift(send, core=1)), [((16, 32, 512), BF)], near_outs=(0,))
     joined = lax.all_to_all(joined, ("xh", "xl", "y"), 0, 0, tiled=True)
-    term_keep, extra, term_send = kernel_call(
+    term_keep, extra, extra_send, term_send = kernel_call(
         back_body,
         (joined, held, weight, gain_parts),
-        [((512, 1024), F32), ((8, 1024), F32), ((528, 1024), BF)],
+        [((512, 1024), F32), ((8, 1024), F32), ((8, 1024), F32), ((512, 1024), BF)],
         [
             ((512, D), F32),
             ((1, D), F32),
@@ -450,15 +446,15 @@
             pltpu.SemaphoreType.DMA,
         ],
         far=(1,),
-        near_outs=(0, 1, 2),
+        near_outs=(0, 1, 2, 3),
     )
     received = shift(term_send, core=1)
-    (gains,) = kernel_call(gains_body, (extra, received), [((16, 8, 512), F32)], near_outs=(0,))
+    (gains,) = kernel_call(gains_body, (extra, shift(extra_send, core=1)), [((16, 8, 384), F32)], near_outs=(0,))
     gains = lax.all_to_all(gains, ("xh", "xl", "y"), 0, 0, tiled=True)
     merged, sums, row_sums = kernel_call(
         merge_body,
         (term_keep, received, gains),
-        [((16, 64, 512), BF), ((8, 512), F32), ((1, 512), F32)],
+        [((16, 64, 512), BF), ((8, 384), F32), ((1, 512), F32)],
         near_outs=(0,),
     )
     merged = lax.all_to_all(merged, ("xh", "xl", "y"), 0, 0, tiled=True)

time: 141 us -> 141 us (level)
    ppermute x24 -> x25, waiting for transfers between devices: 31.3 us -> 30.7 us  [shift(): return lax.ppermute(block, AXES, pairs)]
    ppermute x24 -> x25, starting transfers between devices: 30.7 us -> 31.1 us  [shift(): return lax.ppermute(block, AXES, pairs)]
  transfers between devices with their start and end apart: 25 -> 26, of which waited for: 15 -> 15; matrix products, arithmetic and copies ran while one was open for 0% -> 0% of each run, Pallas kernels for 1% -> 1%
where the time goes in v5:
time: 141 us; the launch traced here: 140 us
  blocking collectives  54 us (38%)
  starting transfers between devices  36.1 us (26%)
  waiting for transfers between devices  32.4 us (23%)
  Pallas kernels  16.6 us (12%)
    ppermute x25, starting transfers between devices, shift(): return lax.ppermute(block, AXES, pairs)  31.1 us
    ppermute x25, waiting for transfers between devices, shift(): return lax.ppermute(block, AXES, pairs)  30.7 us
    pallas_call x12, Pallas kernels, kernel_call(): pl.pallas_call(body, out_shape=[pltpu.HBM(s, d) if i in far_outs else plt...  16.6 us
    all_to_all x1, blocking collectives, per_device(): own_pairs = lax.all_to_all(projected, ('xh', 'xl', 'y'), 0, 0, tiled=True)  16.4 us
    all_to_all x1, blocking collectives, per_device(): joined = lax.all_to_all(joined, ('xh', 'xl', 'y'), 0, 0, tiled=True)  15.1 us
    all_to_all x1, blocking collectives, per_device(): gains = lax.all_to_all(gains, ('xh', 'xl', 'y'), 0, 0, tiled=True)  11.4 us
    all_to_all x1, blocking collectives, per_device(): lax.all_to_all(columns, ('xl', 'y'), 0, 0, tiled=True).reshape(256, 512)  11.1 us
    all_to_all x1, starting transfers between devices, per_device(): merged = lax.all_to_all(merged, ('xh', 'xl', 'y'), 0, 0, tiled=True)  4.98 us
  transfers between devices with their start and end apart: 26, of which 15 were waited for; matrix products, arithmetic and copies ran while one was open for 0% of the time, Pallas kernels for 1%

profile of v5, /device:TPU:8, one launch (start us, length us, event | category | flops | bytes accessed | tf_op | source)
XLA Modules:
  0.0 139.9 jit_solution(3360394498551191080)
XLA Ops:
  0.6 1.0 shard_map.94
  1.7 11.1 %all_to_all.25 = bf16[8,32,512]{2,1,0:T(8,128)(2,1)S(1)} all-to-all(bf16[8,32,512]{2,1,0:T(8,128)(2,1)S(1)} %get-tuple-element.42), channel_id=1, replica_groups=mesh['xh'=2,'core'=2,'z'=8,'xl'=2,'y'=4] {'xl','y'}, dimensions={0} | all-to-all | bytes 524288 | tf_op jit(solution)/shard_map/all_to_all | solution.py:376
  12.7 5.9 %collective-permute-start.4 = (bf16[256,512]{1,0:T(8,128)(2,1)S(1)}, bf16[256,512]{1,0:T(8,128)(2,1)S(1)}, u32[]{:S(2)}, u32[]{:S(2)}) collective-permute-start(bf16[256,512]{1,0:T(8,128)(2,1)S(1)} %bitcast.5), channel_id=1, source_target_pairs={{0,56},{1,57},{2,58},{3,59},{4,60},{5,61},{6,62},{7,63},{8,0},{9,1... | collective-permute-start | bytes 786440 | tf_op jit(solution)/shard_map/ppermute | solution.py:32
  18.6 0.5 collective-permute-start.2
  19.1 2.3 %collective-permute-start.1 = (bf16[80,512]{1,0:T(8,128)(2,1)S(1)}, bf16[80,512]{1,0:T(8,128)(2,1)S(1)}, u32[]{:S(2)}, u32[]{:S(2)}) collective-permute-start(bf16[80,512]{1,0:T(8,128)(2,1)S(1)} %get-tuple-element.41.p0.states), channel_id=1, source_target_pairs={{0,128},{1,129},{2,130},{3,131},{4,132},{5,133},{6,134},{7,135},{8... | collective-permute-start | bytes 245768 | tf_op jit(solution)/shard_map/ppermute | solution.py:32
  21.4 0.6 collective-permute-start
  22.0 2.9 %collective-permute-done.2.p3 = bf16[80,512]{1,0:T(8,128)(2,1)S(1)} collective-permute-done((bf16[80,512]{1,0:T(8,128)(2,1)S(1)}, bf16[80,512]{1,0:T(8,128)(2,1)S(1)}, u32[]{:S(2)}, u32[]{:S(2)}) %collective-permute-start.2) | collective-permute-done | bytes 81952 | tf_op jit(solution)/shard_map/ppermute | solution.py:32
  24.8 0.7 collective-permute-done.1.p2
  25.5 0.7 collective-permute-done.3.ahead_in
  26.2 1.1 shard_map.95
  27.3 1.9 %collective-permute-start.8 = (bf16[32,2048]{1,0:T(8,128)(2,1)S(1)}, bf16[32,2048]{1,0:T(8,128)(2,1)S(1)}, u32[]{:S(2)}, u32[]{:S(2)}) collective-permute-start(bf16[32,2048]{1,0:T(8,128)(2,1)S(1)} %get-tuple-element.43.half), channel_id=1, source_target_pairs={{0,3},{1,0},{2,1},{3,2},{4,7},{5,4},{6,5},{7,6},{8,11},{9,8},{10,9... | collective-permute-start | bytes 393224 | tf_op jit(solution)/shard_map/ppermute | solution.py:32
  29.1 3.2 %collective-permute-start.10 = (bf16[256,512]{1,0:T(8,128)(2,1)S(1)}, bf16[256,512]{1,0:T(8,128)(2,1)S(1)}, u32[]{:S(2)}, u32[]{:S(2)}) collective-permute-start(bf16[256,512]{1,0:T(8,128)(2,1)S(1)} %get-tuple-element.45.refs_2_), channel_id=1, source_target_pairs={{0,56},{1,57},{2,58},{3,59},{4,60},{5,61},{6,62},{7,63},{8,0},{9,1... | collective-permute-start | bytes 786440 | tf_op jit(solution)/shard_map/ppermute | solution.py:32
  32.4 0.6 collective-permute-start.7
  32.9 1.9 %collective-permute-start.6 = (bf16[32,2048]{1,0:T(8,128)(2,1)S(1)}, bf16[32,2048]{1,0:T(8,128)(2,1)S(1)}, u32[]{:S(2)}, u32[]{:S(2)}) collective-permute-start(bf16[32,2048]{1,0:T(8,128)(2,1)S(1)} %get-tuple-element.43.half), channel_id=1, source_target_pairs={{0,1},{1,2},{2,3},{3,0},{4,5},{5,6},{6,7},{7,4},{8,9},{9,10},{10,1... | collective-permute-start | bytes 393224 | tf_op jit(solution)/shard_map/ppermute | solution.py:32
  34.8 1.1 collective-permute-start.5
  35.9 2.9 %collective-permute-done.7.p2 = bf16[32,2048]{1,0:T(8,128)(2,1)S(1)} collective-permute-done((bf16[32,2048]{1,0:T(8,128)(2,1)S(1)}, bf16[32,2048]{1,0:T(8,128)(2,1)S(1)}, u32[]{:S(2)}, u32[]{:S(2)}) %collective-permute-start.7) | collective-permute-done | bytes 131104 | tf_op jit(solution)/shard_map/ppermute | solution.py:32
  38.8 1.5 %collective-permute-done.6.p1 = bf16[32,2048]{1,0:T(8,128)(2,1)S(1)} collective-permute-done((bf16[32,2048]{1,0:T(8,128)(2,1)S(1)}, bf16[32,2048]{1,0:T(8,128)(2,1)S(1)}, u32[]{:S(2)}, u32[]{:S(2)}) %collective-permute-start.6) | collective-permute-done | bytes 131104 | tf_op jit(solution)/shard_map/ppermute | solution.py:32
  40.4 0.8 collective-permute-start.11
  41.2 3.2 %collective-permute-start.13 = (bf16[256,512]{1,0:T(8,128)(2,1)S(1)}, bf16[256,512]{1,0:T(8,128)(2,1)S(1)}, u32[]{:S(2)}, u32[]{:S(2)}) collective-permute-start(bf16[256,512]{1,0:T(8,128)(2,1)S(1)} %get-tuple-element.50.refs_4_), channel_id=1, source_target_pairs={{0,56},{1,57},{2,58},{3,59},{4,60},{5,61},{6,62},{7,63},{8,0},{9,1... | collective-permute-start | bytes 786440 | tf_op jit(solution)/shard_map/ppermute | solution.py:32
  44.4 4.3 %collective-permute-done.12.ahead_in = bf16[256,512]{1,0:T(8,128)(2,1)S(1)} collective-permute-done((bf16[256,512]{1,0:T(8,128)(2,1)S(1)}, bf16[256,512]{1,0:T(8,128)(2,1)S(1)}, u32[]{:S(2)}, u32[]{:S(2)}) %collective-permute-start.12) | collective-permute-done | bytes 262176 | tf_op jit(solution)/shard_map/ppermute | solution.py:32
  48.8 1.4 collective-permute-done.11.beyond
  50.1 0.1 shard_map.97
  50.2 0.1 collective-permute-start.14
  50.4 3.2 %collective-permute-start.16 = (bf16[128,512]{1,0:T(8,128)(2,1)S(1)}, bf16[128,512]{1,0:T(8,128)(2,1)S(1)}, u32[]{:S(2)}, u32[]{:S(2)}) collective-permute-start(bf16[128,512]{1,0:T(8,128)(2,1)S(1)} %get-tuple-element.57), channel_id=1, source_target_pairs={{0,56},{1,57},{2,58},{3,59},{4,60},{5,61},{6,62},{7,63},{8,0},{9,1... | collective-permute-start | bytes 393224 | tf_op jit(solution)/shard_map/ppermute | solution.py:32
  53.7 1.6 %shard_map.98 = (bf16[2,8,32,2048]{3,2,1,0:T(8,128)(2,1)}, bf16[2048,512]{1,0:T(8,128)(2,1)}) custom-call(bf16[4,2,32,2048]{3,2,1,0:T(8,128)(2,1)S(1)} %get-tuple-element.51.own, bf16[256,512]{1,0:T(8,128)(2,1)S(1)} %bitcast.7, bf16[256,512]{1,0:T(8,128)(2,1)S(1)} %get-tuple-element.44.refs_1_, bf16[256,512]{1,0:T(8,128)(2,1)S(1)} %get-tuple-element.45.refs_2_, ...), custom_call_target="tpu_custom_call" | custom-call | tf_op jit(solution)/shard_map/pallas_call | solution.py:40
  55.2 2.2 %collective-permute-done.15.refs_7_ = bf16[128,512]{1,0:T(8,128)(2,1)S(1)} collective-permute-done((bf16[128,512]{1,0:T(8,128)(2,1)S(1)}, bf16[128,512]{1,0:T(8,128)(2,1)S(1)}, u32[]{:S(2)}, u32[]{:S(2)}) %collective-permute-start.15) | collective-permute-done | bytes 131104 | tf_op jit(solution)/shard_map/ppermute | solution.py:32
  57.5 2.3 %shard_map.99 = (bf16[2,8,32,2048]{3,2,1,0:T(8,128)(2,1)}, bf16[2048,512]{1,0:T(8,128)(2,1)}, bf16[16,32,512]{2,1,0:T(8,128)(2,1)S(1)}) custom-call(bf16[2,8,32,2048]{3,2,1,0:T(8,128)(2,1)} %get-tuple-element.52.held_in, bf16[2048,512]{1,0:T(8,128)(2,1)} %get-tuple-element.53.weight_in, ...), custom_call_target="tpu_custom_call", output_to_operand_aliasing={{0}: (0, {}), {1}: (1, {})} | custom-call | tf_op jit(solution)/shard_map/pallas_call | solution.py:40
  59.8 16.4 %all_to_all.26.own = bf16[16,32,512]{2,1,0:T(8,128)(2,1)S(1)} all-to-all(bf16[16,32,512]{2,1,0:T(8,128)(2,1)S(1)} %get-tuple-element.58), channel_id=1, replica_groups=mesh['xh'=2,'core'=2,'z'=8,'xl'=2,'y'=4] {'xh','xl','y'}, dimensions={0} | all-to-all | bytes 1048576 | tf_op jit(solution)/shard_map/all_to_all | solution.py:419
  76.2 1.9 %collective-permute-done.17.other = bf16[16,32,512]{2,1,0:T(8,128)(2,1)S(1)} collective-permute-done((bf16[16,32,512]{2,1,0:T(8,128)(2,1)S(1)}, bf16[16,32,512]{2,1,0:T(8,128)(2,1)S(1)}, u32[]{:S(2)}, u32[]{:S(2)}) %collective-permute-start.17) | collective-permute-done | bytes 524320 | tf_op jit(solution)/shard_map/ppermute | solution.py:32
  78.1 5.6 %shard_map.100 = (bf16[2,32,4096]{2,1,0:T(8,128)(2,1)S(1)}, bf16[2,32,4096]{2,1,0:T(8,128)(2,1)S(1)}, f32[4,1,2048]{2,1,0:T(1,128)S(1)}) custom-call(s32[1,2]{1,0:T(1,128)S(1)} %bitcast.9, bf16[16,32,512]{2,1,0:T(8,128)(2,1)S(1)} %all_to_all.26.own, bf16[16,32,512]{2,1,0:T(8,128)(2,1)S(1)} %collective-permute-done.17.other, ...), custom_call_target="tpu_custom_call" | custom-call | tf_op jit(solution)/shard_map/pallas_call | solution.py:40
  83.7 0.2 collective-permute-start.18
  83.9 1.8 %collective-permute-done.18.received = bf16[2,32,4096]{2,1,0:T(8,128)(2,1)S(1)} collective-permute-done((bf16[2,32,4096]{2,1,0:T(8,128)(2,1)S(1)}, bf16[2,32,4096]{2,1,0:T(8,128)(2,1)S(1)}, u32[]{:S(2)}, u32[]{:S(2)}) %collective-permute-start.18) | collective-permute-done | bytes 524320 | tf_op jit(solution)/shard_map/ppermute | solution.py:32
  85.6 0.1 shard_map.101
  85.8 15.1 %all_to_all.27.gradient = bf16[16,32,512]{2,1,0:T(8,128)(2,1)S(1)} all-to-all(bf16[16,32,512]{2,1,0:T(8,128)(2,1)S(1)} %shard_map.101), channel_id=1, replica_groups=mesh['xh'=2,'core'=2,'z'=8,'xl'=2,'y'=4] {'xh','xl','y'}, dimensions={0} | all-to-all | bytes 1048576 | tf_op jit(solution)/shard_map/all_to_all | solution.py:436
  100.9 2.6 %shard_map.102 = (f32[512,1024]{1,0:T(8,128)S(1)}, f32[8,1024]{1,0:T(8,128)S(1)}, f32[8,1024]{1,0:T(8,128)S(1)}, bf16[512,1024]{1,0:T(8,128)(2,1)S(1)}) custom-call(bf16[16,32,512]{2,1,0:T(8,128)(2,1)S(1)} %all_to_all.27.gradient, bf16[2,8,32,2048]{3,2,1,0:T(8,128)(2,1)} %get-tuple-element.64.held_far, bf16[2048,512]{1,0:T(8,128)(2,1)S(1)} %copy-done, ...), custom_call_target="tpu_custom_call" | custom-call | tf_op jit(solution)/shard_map/pallas_call | solution.py:40
  103.6 0.1 collective-permute-start.19
  103.7 0.5 collective-permute-start.20
  104.2 2.2 %collective-permute-done.20.received = f32[8,1024]{1,0:T(8,128)S(1)} collective-permute-done((f32[8,1024]{1,0:T(8,128)S(1)}, f32[8,1024]{1,0:T(8,128)S(1)}, u32[]{:S(2)}, u32[]{:S(2)}) %collective-permute-start.20) | collective-permute-done | bytes 32800 | tf_op jit(solution)/shard_map/ppermute | solution.py:32
  106.4 11.4 %all_to_all.28.gains = f32[16,8,384]{2,1,0:T(8,128)S(1)} all-to-all(f32[16,8,384]{2,1,0:T(8,128)S(1)} %shard_map.103), channel_id=1, replica_groups=mesh['xh'=2,'core'=2,'z'=8,'xl'=2,'y'=4] {'xh','xl','y'}, dimensions={0} | all-to-all | bytes 393216 | tf_op jit(solution)/shard_map/all_to_all | solution.py:453
  117.8 1.2 shard_map.104
  119.0 5.0 %all-to-all-start.4 = ((bf16[16,64,512]{2,1,0:T(8,128)(2,1)}), bf16[16,64,512]{2,1,0:T(8,128)(2,1)S(1)}, u32[]{:S(2)}, u32[]{:S(2)}) async-start(bf16[16,64,512]{2,1,0:T(8,128)(2,1)} %get-tuple-element.71), calls=%async_computation.4 | async-start | bytes 2097152 | tf_op jit(solution)/shard_map/all_to_all | solution.py:460
  123.9 2.6 %collective-permute-start.22 = (f32[8,384]{1,0:T(8,128)S(1)}, f32[8,384]{1,0:T(8,128)S(1)}, u32[]{:S(2)}, u32[]{:S(2)}) collective-permute-start(f32[8,384]{1,0:T(8,128)S(1)} %get-tuple-element.75), channel_id=1, source_target_pairs={{0,56},{1,57},{2,58},{3,59},{4,60},{5,61},{6,62},{7,63},{8,0},{9,1... | collective-permute-start | bytes 36872 | tf_op jit(solution)/shard_map/ppermute | solution.py:32
  126.5 1.4 %collective-permute-done.22 = f32[8,384]{1,0:T(8,128)S(1)} collective-permute-done((f32[8,384]{1,0:T(8,128)S(1)}, f32[8,384]{1,0:T(8,128)S(1)}, u32[]{:S(2)}, u32[]{:S(2)}) %collective-permute-start.22) | collective-permute-done | bytes 12320 | tf_op jit(solution)/shard_map/ppermute | solution.py:32
  127.9 3.5 %collective-permute-done.21 = f32[8,384]{1,0:T(8,128)S(1)} collective-permute-done((f32[8,384]{1,0:T(8,128)S(1)}, f32[8,384]{1,0:T(8,128)S(1)}, u32[]{:S(2)}, u32[]{:S(2)}) %collective-permute-start.21) | collective-permute-done | bytes 12320 | tf_op jit(solution)/shard_map/ppermute | solution.py:32
  131.4 2.4 %collective-permute-start.23 = (f32[8,384]{1,0:T(8,128)S(1)}, f32[8,384]{1,0:T(8,128)S(1)}, u32[]{:S(2)}, u32[]{:S(2)}) collective-permute-start(f32[8,384]{1,0:T(8,128)S(1)} %get-tuple-element.79.first), channel_id=1, source_target_pairs={{0,40},{1,41},{2,42},{3,43},{4,44},{5,45},{6,46},{7,47},{8,48},{9,... | collective-permute-start | bytes 36872 | tf_op jit(solution)/shard_map/ppermute | solution.py:32
  133.9 3.4 %collective-permute-done.24.third = f32[8,384]{1,0:T(8,128)S(1)} collective-permute-done((f32[8,384]{1,0:T(8,128)S(1)}, f32[8,384]{1,0:T(8,128)S(1)}, u32[]{:S(2)}, u32[]{:S(2)}) %collective-permute-start.24) | collective-permute-done | bytes 12320 | tf_op jit(solution)/shard_map/ppermute | solution.py:32
  137.2 1.7 %all-to-all-done.4.received = bf16[16,64,512]{2,1,0:T(8,128)(2,1)S(1)} async-done(((bf16[16,64,512]{2,1,0:T(8,128)(2,1)}), bf16[16,64,512]{2,1,0:T(8,128)(2,1)S(1)}, u32[]{:S(2)}, u32[]{:S(2)}) %all-to-all-start.4) | async-done | bytes 1048608 | tf_op jit(solution)/shard_map/all_to_all | solution.py:460
  139.0 0.9 shard_map.105
  (25 shorter events, 0.2 us)
Async XLA Ops:
  12.7 12.8 %collective-permute-start.4 = (bf16[256,512]{1,0:T(8,128)(2,1)S(1)}, bf16[256,512]{1,0:T(8,128)(2,1)S(1)}, u32[]{:S(2)}, u32[]{:S(2)}) collective-permute-start(bf16[256,512]{1,0:T(8,128)(2,1)S(1)} %bitcast.5), channel_id=1, source_target_pairs={{0,56},{1,57},{2,58},{3,59},{4,60},{5,61},{6,62},{7,63},{8,0},{9,1... | collective-permute-start | bytes 786440 | tf_op jit(solution)/shard_map/ppermute | solution.py:32
  18.6 7.6 %collective-permute-start.3 = (bf16[256,512]{1,0:T(8,128)(2,1)S(1)}, bf16[256,512]{1,0:T(8,128)(2,1)S(1)}, u32[]{:S(2)}, u32[]{:S(2)}) collective-permute-start(bf16[256,512]{1,0:T(8,128)(2,1)S(1)} %bitcast.6), channel_id=1, source_target_pairs={{0,8},{1,9},{2,10},{3,11},{4,12},{5,13},{6,14},{7,15},{8,16},{9,17... | collective-permute-start | bytes 786440 | tf_op jit(solution)/shard_map/ppermute | solution.py:32
  18.6 6.2 %collective-permute-start.2 = (bf16[80,512]{1,0:T(8,128)(2,1)S(1)}, bf16[80,512]{1,0:T(8,128)(2,1)S(1)}, u32[]{:S(2)}, u32[]{:S(2)}) collective-permute-start(bf16[80,512]{1,0:T(8,128)(2,1)S(1)} %get-tuple-element.41.p0.states), channel_id=1, source_target_pairs={{0,192},{1,193},{2,194},{3,195},{4,196},{5,197},{6,198},{7,199},{8... | collective-permute-start | bytes 245768 | tf_op jit(solution)/shard_map/ppermute | solution.py:32
  19.1 6.4 %collective-permute-start.1 = (bf16[80,512]{1,0:T(8,128)(2,1)S(1)}, bf16[80,512]{1,0:T(8,128)(2,1)S(1)}, u32[]{:S(2)}, u32[]{:S(2)}) collective-permute-start(bf16[80,512]{1,0:T(8,128)(2,1)S(1)} %get-tuple-element.41.p0.states), channel_id=1, source_target_pairs={{0,128},{1,129},{2,130},{3,131},{4,132},{5,133},{6,134},{7,135},{8... | collective-permute-start | bytes 245768 | tf_op jit(solution)/shard_map/ppermute | solution.py:32
  21.4 4.1 %collective-permute-start = (bf16[80,512]{1,0:T(8,128)(2,1)S(1)}, bf16[80,512]{1,0:T(8,128)(2,1)S(1)}, u32[]{:S(2)}, u32[]{:S(2)}) collective-permute-start(bf16[80,512]{1,0:T(8,128)(2,1)S(1)} %get-tuple-element.41.p0.states), channel_id=1, source_target_pairs={{0,64},{1,65},{2,66},{3,67},{4,68},{5,69},{6,70},{7,71},{8,72},{9,... | collective-permute-start | bytes 245768 | tf_op jit(solution)/shard_map/ppermute | solution.py:32
  27.3 7.6 %collective-permute-start.8 = (bf16[32,2048]{1,0:T(8,128)(2,1)S(1)}, bf16[32,2048]{1,0:T(8,128)(2,1)S(1)}, u32[]{:S(2)}, u32[]{:S(2)}) collective-permute-start(bf16[32,2048]{1,0:T(8,128)(2,1)S(1)} %get-tuple-element.43.half), channel_id=1, source_target_pairs={{0,3},{1,0},{2,1},{3,2},{4,7},{5,4},{6,5},{7,6},{8,11},{9,8},{10,9... | collective-permute-start | bytes 393224 | tf_op jit(solution)/shard_map/ppermute | solution.py:32
  29.1 11.2 %collective-permute-start.9 = (bf16[256,512]{1,0:T(8,128)(2,1)S(1)}, bf16[256,512]{1,0:T(8,128)(2,1)S(1)}, u32[]{:S(2)}, u32[]{:S(2)}) collective-permute-start(bf16[256,512]{1,0:T(8,128)(2,1)S(1)} %get-tuple-element.44.refs_1_), channel_id=1, source_target_pairs={{0,8},{1,9},{2,10},{3,11},{4,12},{5,13},{6,14},{7,15},{8,16},{9,17... | collective-permute-start | bytes 786440 | tf_op jit(solution)/shard_map/ppermute | solution.py:32
  29.1 11.2 %collective-permute-start.10 = (bf16[256,512]{1,0:T(8,128)(2,1)S(1)}, bf16[256,512]{1,0:T(8,128)(2,1)S(1)}, u32[]{:S(2)}, u32[]{:S(2)}) collective-permute-start(bf16[256,512]{1,0:T(8,128)(2,1)S(1)} %get-tuple-element.45.refs_2_), channel_id=1, source_target_pairs={{0,56},{1,57},{2,58},{3,59},{4,60},{5,61},{6,62},{7,63},{8,0},{9,1... | collective-permute-start | bytes 786440 | tf_op jit(solution)/shard_map/ppermute | solution.py:32
  32.4 6.5 %collective-permute-start.7 = (bf16[32,2048]{1,0:T(8,128)(2,1)S(1)}, bf16[32,2048]{1,0:T(8,128)(2,1)S(1)}, u32[]{:S(2)}, u32[]{:S(2)}) collective-permute-start(bf16[32,2048]{1,0:T(8,128)(2,1)S(1)} %get-tuple-element.43.half), channel_id=1, source_target_pairs={{0,2},{1,3},{2,0},{3,1},{4,6},{5,7},{6,4},{7,5},{8,10},{9,11},{10,... | collective-permute-start | bytes 393224 | tf_op jit(solution)/shard_map/ppermute | solution.py:32
  32.9 7.4 %collective-permute-start.6 = (bf16[32,2048]{1,0:T(8,128)(2,1)S(1)}, bf16[32,2048]{1,0:T(8,128)(2,1)S(1)}, u32[]{:S(2)}, u32[]{:S(2)}) collective-permute-start(bf16[32,2048]{1,0:T(8,128)(2,1)S(1)} %get-tuple-element.43.half), channel_id=1, source_target_pairs={{0,1},{1,2},{2,3},{3,0},{4,5},{5,6},{6,7},{7,4},{8,9},{9,10},{10,1... | collective-permute-start | bytes 393224 | tf_op jit(solution)/shard_map/ppermute | solution.py:32
  34.8 5.5 %collective-permute-start.5 = (bf16[32,2048]{1,0:T(8,128)(2,1)S(1)}, bf16[32,2048]{1,0:T(8,128)(2,1)S(1)}, u32[]{:S(2)}, u32[]{:S(2)}) collective-permute-start(bf16[32,2048]{1,0:T(8,128)(2,1)S(1)} %get-tuple-element.43.half), channel_id=1, source_target_pairs={{0,4},{1,5},{2,6},{3,7},{4,0},{5,1},{6,2},{7,3},{8,12},{9,13},{10,... | collective-permute-start | bytes 393224 | tf_op jit(solution)/shard_map/ppermute | solution.py:32
  40.4 9.7 %collective-permute-start.11 = (bf16[3,32,2048]{2,1,0:T(8,128)(2,1)S(1)}, bf16[3,32,2048]{2,1,0:T(8,128)(2,1)S(1)}, u32[]{:S(2)}, u32[]{:S(2)}) collective-permute-start(bf16[3,32,2048]{2,1,0:T(8,128)(2,1)S(1)} %get-tuple-element.48), channel_id=1, source_target_pairs={{0,4},{1,5},{2,6},{3,7},{4,0},{5,1},{6,2},{7,3},{8,12},{9,13},{10,... | collective-permute-start | bytes 1179656 | tf_op jit(solution)/shard_map/ppermute | solution.py:32
  41.2 7.6 %collective-permute-start.12 = (bf16[256,512]{1,0:T(8,128)(2,1)S(1)}, bf16[256,512]{1,0:T(8,128)(2,1)S(1)}, u32[]{:S(2)}, u32[]{:S(2)}) collective-permute-start(bf16[256,512]{1,0:T(8,128)(2,1)S(1)} %get-tuple-element.49.refs_3_), channel_id=1, source_target_pairs={{0,8},{1,9},{2,10},{3,11},{4,12},{5,13},{6,14},{7,15},{8,16},{9,17... | collective-permute-start | bytes 786440 | tf_op jit(solution)/shard_map/ppermute | solution.py:32
  41.2 7.6 %collective-permute-start.13 = (bf16[256,512]{1,0:T(8,128)(2,1)S(1)}, bf16[256,512]{1,0:T(8,128)(2,1)S(1)}, u32[]{:S(2)}, u32[]{:S(2)}) collective-permute-start(bf16[256,512]{1,0:T(8,128)(2,1)S(1)} %get-tuple-element.50.refs_4_), channel_id=1, source_target_pairs={{0,56},{1,57},{2,58},{3,59},{4,60},{5,61},{6,62},{7,63},{8,0},{9,1... | collective-permute-start | bytes 786440 | tf_op jit(solution)/shard_map/ppermute | solution.py:32
  50.2 7.2 %collective-permute-start.14 = (bf16[4,2,32,2048]{3,2,1,0:T(8,128)(2,1)S(1)}, bf16[4,2,32,2048]{3,2,1,0:T(8,128)(2,1)S(1)}, u32[]{:S(2)}, u32[]{:S(2)}) collective-permute-start(bf16[4,2,32,2048]{3,2,1,0:T(8,128)(2,1)S(1)} %get-tuple-element.51.own), channel_id=1, source_target_pairs={{0,64},{1,65},{2,66},{3,67},{4,68},{5,69},{6,70},{7,71},{8,72},{9,... | collective-permute-start | bytes 3145736 | tf_op jit(solution)/shard_map/ppermute | solution.py:32
  50.3 7.1 %collective-permute-start.15 = (bf16[128,512]{1,0:T(8,128)(2,1)S(1)}, bf16[128,512]{1,0:T(8,128)(2,1)S(1)}, u32[]{:S(2)}, u32[]{:S(2)}) collective-permute-start(bf16[128,512]{1,0:T(8,128)(2,1)S(1)} %get-tuple-element.56), channel_id=1, source_target_pairs={{0,8},{1,9},{2,10},{3,11},{4,12},{5,13},{6,14},{7,15},{8,16},{9,17... | collective-permute-start | bytes 393224 | tf_op jit(solution)/shard_map/ppermute | solution.py:32
  50.4 7.0 %collective-permute-start.16 = (bf16[128,512]{1,0:T(8,128)(2,1)S(1)}, bf16[128,512]{1,0:T(8,128)(2,1)S(1)}, u32[]{:S(2)}, u32[]{:S(2)}) collective-permute-start(bf16[128,512]{1,0:T(8,128)(2,1)S(1)} %get-tuple-element.57), channel_id=1, source_target_pairs={{0,56},{1,57},{2,58},{3,59},{4,60},{5,61},{6,62},{7,63},{8,0},{9,1... | collective-permute-start | bytes 393224 | tf_op jit(solution)/shard_map/ppermute | solution.py:32
  57.5 20.6 %copy-start.1 = (s32[2,1]{0,1:T(1,128)S(1)}, s32[2,1]{0,1:T(1,128)}, u32[]{:S(2)}) copy-start(s32[2,1]{0,1:T(1,128)} %param.8) | copy-start | bytes 28
  76.2 24.7 %copy-start = (bf16[2048,512]{1,0:T(8,128)(2,1)S(1)}, bf16[2048,512]{1,0:T(8,128)(2,1)}, u32[]{:S(2)}) copy-start(bf16[2048,512]{1,0:T(8,128)(2,1)} %get-tuple-element.65.weight) | copy-start | bytes 6291460
  76.2 1.9 %collective-permute-start.17 = (bf16[16,32,512]{2,1,0:T(8,128)(2,1)S(1)}, bf16[16,32,512]{2,1,0:T(8,128)(2,1)S(1)}, u32[]{:S(2)}, u32[]{:S(2)}) collective-permute-start(bf16[16,32,512]{2,1,0:T(8,128)(2,1)S(1)} %all_to_all.26.own), channel_id=1, source_target_pairs={{0,64},{1,65},{2,66},{3,67},{4,68},{5,69},{6,70},{7,71},{8,72},{9,... | collective-permute-start | bytes 1572872 | tf_op jit(solution)/shard_map/ppermute | solution.py:32
  83.7 2.0 %collective-permute-start.18 = (bf16[2,32,4096]{2,1,0:T(8,128)(2,1)S(1)}, bf16[2,32,4096]{2,1,0:T(8,128)(2,1)S(1)}, u32[]{:S(2)}, u32[]{:S(2)}) collective-permute-start(bf16[2,32,4096]{2,1,0:T(8,128)(2,1)S(1)} %get-tuple-element.63), channel_id=1, source_target_pairs={{0,64},{1,65},{2,66},{3,67},{4,68},{5,69},{6,70},{7,71},{8,72},{9,... | collective-permute-start | bytes 1572872 | tf_op jit(solution)/shard_map/ppermute | solution.py:32
  103.6 14.2 %collective-permute-start.19 = (bf16[512,1024]{1,0:T(8,128)(2,1)S(1)}, bf16[512,1024]{1,0:T(8,128)(2,1)S(1)}, u32[]{:S(2)}, u32[]{:S(2)}) collective-permute-start(bf16[512,1024]{1,0:T(8,128)(2,1)S(1)} %get-tuple-element.68), channel_id=1, source_target_pairs={{0,64},{1,65},{2,66},{3,67},{4,68},{5,69},{6,70},{7,71},{8,72},{9,... | collective-permute-start | bytes 3145736 | tf_op jit(solution)/shard_map/ppermute | solution.py:32
  103.7 2.7 %collective-permute-start.20 = (f32[8,1024]{1,0:T(8,128)S(1)}, f32[8,1024]{1,0:T(8,128)S(1)}, u32[]{:S(2)}, u32[]{:S(2)}) collective-permute-start(f32[8,1024]{1,0:T(8,128)S(1)} %get-tuple-element.70), channel_id=1, source_target_pairs={{0,64},{1,65},{2,66},{3,67},{4,68},{5,69},{6,70},{7,71},{8,72},{9,... | collective-permute-start | bytes 98312 | tf_op jit(solution)/shard_map/ppermute | solution.py:32
  119.0 20.0 %all-to-all-start.4 = ((bf16[16,64,512]{2,1,0:T(8,128)(2,1)}), bf16[16,64,512]{2,1,0:T(8,128)(2,1)S(1)}, u32[]{:S(2)}, u32[]{:S(2)}) async-start(bf16[16,64,512]{2,1,0:T(8,128)(2,1)} %get-tuple-element.71), calls=%async_computation.4 | async-start | bytes 2097152 | tf_op jit(solution)/shard_map/all_to_all | solution.py:460
  123.9 4.0 %collective-permute-start.22 = (f32[8,384]{1,0:T(8,128)S(1)}, f32[8,384]{1,0:T(8,128)S(1)}, u32[]{:S(2)}, u32[]{:S(2)}) collective-permute-start(f32[8,384]{1,0:T(8,128)S(1)} %get-tuple-element.75), channel_id=1, source_target_pairs={{0,56},{1,57},{2,58},{3,59},{4,60},{5,61},{6,62},{7,63},{8,0},{9,1... | collective-permute-start | bytes 36872 | tf_op jit(solution)/shard_map/ppermute | solution.py:32
  126.5 4.9 %collective-permute-start.21 = (f32[8,384]{1,0:T(8,128)S(1)}, f32[8,384]{1,0:T(8,128)S(1)}, u32[]{:S(2)}, u32[]{:S(2)}) collective-permute-start(f32[8,384]{1,0:T(8,128)S(1)} %get-tuple-element.75), channel_id=1, source_target_pairs={{0,8},{1,9},{2,10},{3,11},{4,12},{5,13},{6,14},{7,15},{8,16},{9,17... | collective-permute-start | bytes 36872 | tf_op jit(solution)/shard_map/ppermute | solution.py:32
  131.4 5.8 %collective-permute-start.24 = (f32[8,384]{1,0:T(8,128)S(1)}, f32[8,384]{1,0:T(8,128)S(1)}, u32[]{:S(2)}, u32[]{:S(2)}) collective-permute-start(f32[8,384]{1,0:T(8,128)S(1)} %get-tuple-element.80), channel_id=1, source_target_pairs={{0,16},{1,17},{2,18},{3,19},{4,20},{5,21},{6,22},{7,23},{8,24},{9,... | collective-permute-start | bytes 36872 | tf_op jit(solution)/shard_map/ppermute | solution.py:32
  131.4 5.8 %collective-permute-start.23 = (f32[8,384]{1,0:T(8,128)S(1)}, f32[8,384]{1,0:T(8,128)S(1)}, u32[]{:S(2)}, u32[]{:S(2)}) collective-permute-start(f32[8,384]{1,0:T(8,128)S(1)} %get-tuple-element.79.first), channel_id=1, source_target_pairs={{0,40},{1,41},{2,42},{3,43},{4,44},{5,45},{6,46},{7,47},{8,48},{9,... | collective-permute-start | bytes 36872 | tf_op jit(solution)/shard_map/ppermute | solution.py:32
